TPU v7x, 128 devices: a whole 4x4x4 slice. The times are simulated.
128 devices in a mesh: dp: 4 (over x), row: 16 (over z, y), col: 2 (over core).
Axes of the slice: x: 4, y: 4, z: 4, core: 2. Of those that a mesh axis runs over, the one named last changes fastest.
Arguments:
- tokens: bfloat16 [2048, 14336], P('dp', 'row'), may hold values from -6 to 6
- frozen: bfloat16 [14336, 12288], P('row', 'col')
- adapter_down: bfloat16 [14336, 128], P('row')
- adapter_up: bfloat16 [128, 12288], P(None, 'col'), may hold values from -1.21 to 1.21
- magnitude: float32 [8, 12288], P(None, 'col'), may hold values from 0.5 to 4
- grad_out: bfloat16 [2048, 12288], P('dp', 'col'), may hold values from -6 to 6
- tenant_lengths: int32 [32], replicated, may hold values from 1 to 256, 2048 in all
- tenant_adapter: int32 [32], replicated, may hold values from 0 to 7
Outputs:
- adapted: bfloat16 [2048, 12288], P('dp', 'col')
- input_grad: bfloat16 [2048, 14336], P('dp', 'row')
- grad_down: float32 [14336, 128], P('row')
- grad_up: float32 [128, 12288], P(None, 'col')
- grad_magnitude: float32 [8, 12288], P(None, 'col')
Inputs may be any that keep to these rules, and one draw needn't show every extreme that they name: `tenant_lengths`: the lengths sum to 2048.
All inputs are finite; a program needn't handle non-finite values.
Results may differ from a plain program's by a relative error of at most 0.0075.
Values may be sent and summed in bfloat16 or wider, within the bound.
No kernel may reach another device: no remote copies, remote signals or barrier semaphores. Data moves between devices by JAX's collectives and lax.ppermute only.
A program may use at most 192 MiB of HBM per device.

v0:
```python
import jax
import jax.numpy as jnp
from jax import lax
from jax.sharding import PartitionSpec as P


def token_adapters(tenant_lengths, tenant_adapter, tok_count, first_token):
    starts_at = jnp.cumsum(tenant_lengths) - tenant_lengths
    position = first_token + jnp.arange(tok_count, dtype=jnp.int32)
    tenant = jnp.sum((starts_at[None, :] <= position[:, None]).astype(jnp.int32), axis=1) - 1
    picked = (
        tenant[:, None] == jnp.arange(tenant_lengths.shape[0], dtype=jnp.int32)[None, :]
    ).astype(jnp.int32)
    return jnp.sum(picked * tenant_adapter[None, :], axis=1)


def split_parts(values):
    upper = values.astype(jnp.bfloat16)
    lower = (values - upper.astype(jnp.float32)).astype(jnp.bfloat16)
    return (upper, lower)


def wide_left(values, narrow, dims):
    upper, lower = split_parts(values)
    first = lax.dot_general(upper, narrow, dims, preferred_element_type=jnp.float32)
    return first + lax.dot_general(lower, narrow, dims, preferred_element_type=jnp.float32)


def wide_right(narrow, values, dims):
    upper, lower = split_parts(values)
    first = lax.dot_general(narrow, upper, dims, preferred_element_type=jnp.float32)
    return first + lax.dot_general(narrow, lower, dims, preferred_element_type=jnp.float32)


def column_squares(squares, cross, gram, adapter_up, rank_size, adapters):
    plain = (((1,), (0,)), ((), ()))
    flat_cols = adapter_up.shape[0]
    block_ids = jnp.arange(flat_cols, dtype=jnp.int32) // rank_size
    blocks = (block_ids[:, None] == block_ids[None, :]).astype(jnp.float32)
    gram_up = wide_left(gram * blocks, adapter_up, plain)
    up_wide = adapter_up.astype(jnp.float32)
    terms = (up_wide * (2.0 * cross + gram_up)).reshape(adapters, rank_size, -1)
    return squares[None, :] + jnp.sum(terms, axis=1)


def on_device(
    tokens, frozen, adapter_down, adapter_up, magnitude, grad_out, tenant_lengths, tenant_adapter
):
    highest = lax.Precision.HIGHEST
    plain = (((1,), (0,)), ((), ()))
    contract_first = (((0,), (0,)), ((), ()))
    contract_last = (((1,), (1,)), ((), ()))
    tok_rows = tokens.shape[0]
    adapters = magnitude.shape[0]
    flat_cols = adapter_down.shape[1]
    rank_size = flat_cols // adapters
    first_token = lax.axis_index("dp") * tok_rows
    adapter = token_adapters(tenant_lengths, tenant_adapter, tok_rows, first_token)
    one_hot = (adapter[:, None] == jnp.arange(adapters, dtype=jnp.int32)[None, :]).astype(
        jnp.float32
    )
    slot_mask = (
        adapter[:, None] == (jnp.arange(flat_cols, dtype=jnp.int32) // rank_size)[None, :]
    ).astype(jnp.float32)
    squares_part = jnp.sum(jnp.square(frozen.astype(jnp.float32)), axis=0)
    cross_part = lax.dot_general(
        adapter_down, frozen, contract_first, preferred_element_type=jnp.float32
    )
    gram_part = lax.dot_general(
        adapter_down, adapter_down, contract_first, preferred_element_type=jnp.float32
    )
    squares_sum, cross_sum, gram_sum = lax.psum((squares_part, cross_part, gram_part), "row")
    col_sq = column_squares(squares_sum, cross_sum, gram_sum, adapter_up, rank_size, adapters)
    col_norm = jnp.sqrt(col_sq + 1e-06)
    scale_table = magnitude / col_norm
    tok_scale = jnp.dot(one_hot, scale_table, precision=highest)
    down_part = jnp.dot(tokens, adapter_down, preferred_element_type=jnp.float32) * slot_mask
    down_full = lax.psum(down_part, "row")
    row_share = tok_rows // lax.axis_size("row")
    row_first = lax.axis_index("row") * row_share
    picked_rows = tokens
    picked_down = down_full
    mixed_all = lax.psum(
        jnp.dot(picked_rows, frozen, preferred_element_type=jnp.float32), "row"
    ) + wide_left(picked_down, adapter_up, plain)
    adapted = (tok_scale * mixed_all).astype(jnp.bfloat16)
    mixed_rows = lax.dynamic_slice_in_dim(mixed_all, row_first, row_share, 0)
    scaled_grad = (grad_out.astype(jnp.float32) * tok_scale).astype(jnp.bfloat16)
    back_part = (
        lax.dot_general(scaled_grad, adapter_up, contract_last, preferred_element_type=jnp.float32)
        * slot_mask
    )
    back_full = lax.psum(back_part, "col")
    col_share = tok_rows // lax.axis_size("col")
    col_first = lax.axis_index("col") * col_share
    picked_grad = scaled_grad
    picked_back = back_full
    input_sum = lax.psum(
        lax.dot_general(picked_grad, frozen, contract_last, preferred_element_type=jnp.float32),
        "col",
    ) + wide_left(picked_back, adapter_down, contract_last)
    input_grad = input_sum.astype(jnp.bfloat16)
    hot_rows = lax.dynamic_slice_in_dim(one_hot, row_first, row_share, 0)
    out_grad_rows = lax.dynamic_slice_in_dim(grad_out, row_first, row_share, 0).astype(jnp.float32)
    mag_part = lax.dot_general(
        hot_rows, out_grad_rows * mixed_rows, contract_first, precision=highest
    )
    picked_rows = lax.dynamic_slice_in_dim(tokens, col_first, col_share, 0)
    picked_back = lax.dynamic_slice_in_dim(back_full, col_first, col_share, 0)
    grad_down = lax.psum(wide_right(picked_rows, picked_back, contract_first), ("dp", "col"))
    picked_down = lax.dynamic_slice_in_dim(down_full, row_first, row_share, 0)
    picked_grad = lax.dynamic_slice_in_dim(scaled_grad, row_first, row_share, 0)
    grad_up, mag_sum = lax.psum(
        (wide_left(picked_down, picked_grad, contract_first), mag_part), ("dp", "row")
    )
    return (adapted, input_grad, grad_down, grad_up, mag_sum / col_norm)


def solution(mesh):
    placed = (
        P("dp", "row"),
        P("row", "col"),
        P("row", None),
        P(None, "col"),
        P(None, "col"),
        P("dp", "col"),
        P(),
        P(),
    )
    return jax.shard_map(
        on_device,
        mesh=mesh,
        in_specs=placed,
        out_specs=(P("dp", "col"), P("dp", "row"), P("row", None), P(None, "col"), P(None, "col")),
        check_vma=False,
    )
```

profile of v0, /device:TPU:0, one launch (start us, length us, event | category | flops | bytes accessed | tf_op | source)
XLA Modules:
  0.0 540.5 jit_solution(2378664842289102648)
XLA Ops:
  9.0 1.9 fusion.43
  10.9 7.9 %fusion.42 = f32[128,6144]{1,0:T(8,128)} fusion(bf16[896,128]{1,0:T(8,128)(2,1)} %param.10, bf16[896,6144]{1,0:T(8,128)(2,1)} %param.9), kind=kOutput, calls=%fused_computation.71 | convolution fusion | flops 1409286144 | bytes 14385152 | tf_op jit(solution)/shard_map/dot_general | solution.py:66
  18.8 9.2 %fusion.44 = f32[512,6144]{1,0:T(8,128)} fusion(bf16[512,896]{1,0:T(8,128)(2,1)S(1)} %copy-done, bf16[896,6144]{1,0:T(8,128)(2,1)S(1)} %copy-done.2), kind=kOutput, calls=%fused_computation.73 | convolution fusion | flops 5637144576 | bytes 24510464 | tf_op jit(solution)/shard_map/dot_general | solution.py:84
  29.4 6.4 %multiply_reduce_fusion = f32[6144]{0:T(1024)S(1)} fusion(bf16[896,6144]{1,0:T(8,128)(2,1)} %param.9), kind=kLoop, calls=%fused_computation | loop fusion | flops 16508928 | bytes 11034624 | tf_op jit(solution)/shard_map/reduce_sum | solution.py:65
  35.8 78.6 %psum.70 = f32[6144]{0:T(1024)S(1)} all-reduce(f32[6144]{0:T(1024)S(1)} %multiply_reduce_fusion), channel_id=1, replica_groups=mesh['dp'=4,'row'=16,'col'=2] {'row'}, use_global_device_ids=true, to_apply=%region_4.5 | all-reduce | flops 6144 | bytes 49152 | tf_op jit(solution)/shard_map/psum | solution.py:72
  114.5 133.4 %all-reduce.12.cloned.1.call-done = (f32[128,128]{1,0:T(8,128)}, f32[128,6144]{1,0:T(8,128)}, f32[512,6144]{1,0:T(8,128)}, f32[512,128]{1,0:T(8,128)}) async-done(((f32[128,128]{1,0:T(8,128)}, f32[128,6144]{1,0:T(8,128)}, f32[512,6144]{1,0:T(8,128)}, f32[512,128]{1,0:T(8,128)}), (f32[128,128]{1,0:T(8,128)}, f32[128,6144]{1,0:T(8,128)}, f32[512,6144]{1,0:T(8,128)}, ...) | async-done | bytes 16056336 | tf_op jit(solution)/shard_map/psum | solution.py:72
  249.3 7.4 %fusion.22 = f32[512,6144]{1,0:T(8,128)} fusion(bf16[128,6144]{1,0:T(8,128)(2,1)S(1)} %copy-done.3, f32[512,128]{1,0:T(8,128)} %get-tuple-element.10), kind=kOutput, calls=%fused_computation.39 | convolution fusion | flops 805371904 | bytes 14417920 | tf_op jit(solution)/shard_map/dot_general | solution.py:25
  256.7 1.5 bitcast_reduce_fusion
  258.2 10.0 %add_add_fusion = f32[512,6144]{1,0:T(8,128)S(1)} fusion(f32[512,6144]{1,0:T(8,128)} %get-tuple-element.9, f32[512,6144]{1,0:T(8,128)} %fusion.22, bf16[128,6144]{1,0:T(8,128)(2,1)S(1)} %copy-done.3, f32[512,128]{1,0:T(8,128)S(1)} %copy-done.7), kind=kOutput, calls=%fused_computation.3 | convolution fusion | flops 811859968 | bytes 39583744 | tf_op jit(solution)/shard_map/dot_general | solution.py:26
  268.2 14.0 %multiply_convert_fusion = (bf16[512,6144]{1,0:T(8,128)(2,1)}, bf16[512,6144]{1,0:T(8,128)(2,1)}) fusion(bf16[512,6144]{1,0:T(8,128)(2,1)} %param.13, f32[512,6144]{1,0:T(8,128)S(1)} %add_add_fusion, f32[8,6144]{1,0:T(8,128)S(1)} %copy-done.9, f32[8,6144]{1,0:T(8,128)S(1)} %bitcast_reduce_fusion, f32[6144]{0:T(1024)S(1)} %psum.70, s32[512]{0:T(512)S(1)} %select_reduce_fusion), kind=kOutput, calls=%fused_computation.1 | convolution fusion | flops 317870080 | bytes 31877120 | tf_op jit(solution)/shard_map/dot_general | solution.py:76
  282.2 13.1 %fusion.45 = f32[512,896]{1,0:T(8,128)} fusion(bf16[512,6144]{1,0:T(8,128)(2,1)} %get-tuple-element.13, bf16[896,6144]{1,0:T(8,128)(2,1)} %param.9), kind=kOutput, calls=%fused_computation.74 | convolution fusion | flops 5637144576 | bytes 19136512 | tf_op jit(solution)/shard_map/dot_general | solution.py:99
  295.3 2.5 convolution_select_fusion.1
  298.1 2.3 fusion.2
  300.4 1.6 fusion.11
  302.0 3.3 convolution_add_fusion
  305.3 19.1 %all-reduce.14.cloned.1.call-done = (f32[512,896]{1,0:T(8,128)}, f32[512,128]{1,0:T(8,128)}) async-done(((f32[512,896]{1,0:T(8,128)}, f32[512,128]{1,0:T(8,128)}), (f32[512,896]{1,0:T(8,128)}, f32[512,128]{1,0:T(8,128)})) %all-reduce.14.cloned.1.call-update) | async-done | bytes 2097168 | tf_op jit(solution)/shard_map/psum | solution.py:98
  325.7 2.0 convolution_add_fusion.2
  327.7 2.6 fusion.19
  330.3 3.6 add_convert_fusion
  333.9 133.9 %all-reduce.10.cloned.1.call-done = (f32[128,6144]{1,0:T(8,128)}, f32[8,6144]{1,0:T(8,128)}) async-done(((f32[128,6144]{1,0:T(8,128)}, f32[8,6144]{1,0:T(8,128)}), (f32[128,6144]{1,0:T(8,128)}, f32[8,6144]{1,0:T(8,128)})) %all-reduce.10.cloned.1.call-update) | async-done | bytes 3342352 | tf_op jit(solution)/shard_map/psum | solution.py:113
  467.8 1.7 fusion.15
  469.5 58.8 %all-reduce.8.cloned.1.call-done = f32[896,128]{1,0:T(8,128)} async-done(((f32[896,128]{1,0:T(8,128)}), f32[896,128]{1,0:T(8,128)}) %all-reduce.8.cloned.1.call-update) | async-done | bytes 458768 | tf_op jit(solution)/shard_map/psum | solution.py:110
  528.3 1.8 copy.27
  530.1 3.9 copy.28
  (43 shorter events, 6.0 us)
Async XLA Ops:
  7.2 11.7 %copy-start = (bf16[512,896]{1,0:T(8,128)(2,1)S(1)}, bf16[512,896]{1,0:T(8,128)(2,1)}, u32[]{:S(2)}) copy-start(bf16[512,896]{1,0:T(8,128)(2,1)} %param.8) | copy-start | bytes 2752516
  7.2 240.6 %all-reduce.12.cloned.1.call-start = ((), (), s32[]{:S(2)}) async-start(), calls=%async_computation.2 | async-start | bytes 32112640 | tf_op jit(solution)/shard_map/psum | solution.py:72
  10.9 7.9 %copy-start.2 = (bf16[896,6144]{1,0:T(8,128)(2,1)S(1)}, bf16[896,6144]{1,0:T(8,128)(2,1)}, u32[]{:S(2)}) copy-start(bf16[896,6144]{1,0:T(8,128)(2,1)} %param.9) | copy-start | bytes 33030148
  18.8 9.3 %copy-start.10 = (s32[32]{0:T(128)S(1)}, s32[32]{0:T(128)}, u32[]{:S(2)}) copy-start(s32[32]{0:T(128)} %param.15) | copy-start | bytes 388
  18.8 9.3 %copy-start.4 = (bf16[896,128]{1,0:T(8,128)(2,1)S(1)}, bf16[896,128]{1,0:T(8,128)(2,1)}, u32[]{:S(2)}) copy-start(bf16[896,128]{1,0:T(8,128)(2,1)} %param.10) | copy-start | bytes 688132
  29.3 218.5 %copy-start.3 = (bf16[128,6144]{1,0:T(8,128)(2,1)S(1)}, bf16[128,6144]{1,0:T(8,128)(2,1)}, u32[]{:S(2)}) copy-start(bf16[128,6144]{1,0:T(8,128)(2,1)} %param.11) | copy-start | bytes 4718596
  29.3 295.1 %all-reduce.14.cloned.1.call-start = ((), (), s32[]{:S(2)}) async-start(), calls=%async_computation.3 | async-start | bytes 4194304 | tf_op jit(solution)/shard_map/psum | solution.py:98
  249.3 7.4 %copy-start.6 = (f32[128,6144]{1,0:T(8,128)S(1)}, f32[128,6144]{1,0:T(8,128)}, u32[]{:S(2)}) copy-start(f32[128,6144]{1,0:T(8,128)} %get-tuple-element.8) | copy-start | bytes 9437188
  249.3 7.4 %copy-start.8 = (f32[128,128]{1,0:T(8,128)S(1)}, f32[128,128]{1,0:T(8,128)}, u32[]{:S(2)}) copy-start(f32[128,128]{1,0:T(8,128)} %get-tuple-element.7) | copy-start | bytes 196612
  256.7 1.5 copy-start.7
  258.2 10.0 %copy-start.9 = (f32[8,6144]{1,0:T(8,128)S(1)}, f32[8,6144]{1,0:T(8,128)}, u32[]{:S(2)}) copy-start(f32[8,6144]{1,0:T(8,128)} %param.12) | copy-start | bytes 589828
  268.2 14.0 %copy-start.1 = (f32[512,6144]{1,0:T(8,128)}, f32[512,6144]{1,0:T(8,128)S(1)}, u32[]{:S(2)}) copy-start(f32[512,6144]{1,0:T(8,128)S(1)} %add_add_fusion) | copy-start | bytes 37748740
  282.2 13.1 %copy-start.5 = (bf16[512,6144]{1,0:T(8,128)(2,1)S(1)}, bf16[512,6144]{1,0:T(8,128)(2,1)}, u32[]{:S(2)}) copy-start(bf16[512,6144]{1,0:T(8,128)(2,1)} %get-tuple-element.13) | copy-start | bytes 18874372
  297.9 169.9 %all-reduce.10.cloned.1.call-start = ((), (), s32[]{:S(2)}) async-start(), calls=%async_computation.1 | async-start | bytes 6684672 | tf_op jit(solution)/shard_map/psum | solution.py:113
  305.3 223.0 %all-reduce.8.cloned.1.call-start = ((), (), s32[]{:S(2)}) async-start(), calls=%async_computation | async-start | bytes 917504 | tf_op jit(solution)/shard_map/psum | solution.py:110
Sparse Core Ops, SparseCore 0:
  29.4 218.3 all-reduce.11
  298.0 26.4 all-reduce.13
  330.1 137.6 all-reduce.9
  470.5 57.7 all-reduce.7
where the time goes:
time: 541 us
  waiting for transfers between devices  345 us (64%)
  matrix products  86.7 us (16%)
  blocking collectives  78.6 us (15%)
  between operations  13.9 us (3%)
  other arithmetic  9.28 us (2%)
  local copies, waits for them, and re-layouts  6.53 us (1%)
    psum x1, waiting for transfers between devices, on_device(): lax.psum((wide_left(picked_down, picked_grad, contract_first), mag_part),...  134 us
    psum x1, waiting for transfers between devices, on_device(): lax.psum((squares_part, cross_part, gram_part), 'row')  133 us
    psum x1, blocking collectives, on_device(): lax.psum((squares_part, cross_part, gram_part), 'row')  78.6 us
    psum x1, waiting for transfers between devices, on_device(): lax.psum(wide_right(picked_rows, picked_back, contract_first), ('dp', 'co...  58.8 us
    psum x1, waiting for transfers between devices, on_device(): lax.psum(lax.dot_general(picked_grad, frozen, contract_last, preferred_el...  19.1 us
    dot_general x4, matrix products, wide_left(): lax.dot_general(lower, narrow, dims, preferred_element_type=jnp.float32)  18.3 us
    dot_general x1, matrix products, on_device(): tok_scale = jnp.dot(one_hot, scale_table, precision=highest)  14 us
    dot_general x1, matrix products, on_device(): lax.dot_general(picked_grad, frozen, contract_last, preferred_element_typ...  13.1 us
  transfers between devices with their start and end apart: 4, of which 4 were waited for; matrix products, arithmetic and copies ran while one was open for 5% of the time, Pallas kernels for 0%

commit v1 on v0

v1 whole, which is shorter than its diff:
```python
import functools

import jax
import jax.numpy as jnp
from jax import lax
from jax.experimental import pallas as pl
from jax.experimental.pallas import tpu as pltpu
from jax.sharding import Mesh
from jax.sharding import PartitionSpec as P

BF = jnp.bfloat16
F32 = jnp.float32
SIDE = 4
PLAIN = (((1,), (0,)), ((), ()))
FIRST = (((0,), (0,)), ((), ()))
LAST = (((1,), (1,)), ((), ()))

STREAMS = (
    (("y", 1), ("y", 3), ("z", 1), ("z", 3)),
    (("y", 3), ("y", 1), ("z", 3), ("z", 1)),
    (("z", 1), ("z", 3), ("y", 1), ("y", 3)),
    (("z", 3), ("z", 1), ("y", 3), ("y", 1)),
)
SPAN = 512


def swap(values, pairing):
    axis, flip = pairing
    return lax.ppermute(values, axis, [(i, i ^ flip) for i in range(SIDE)])


def wide(values):
    return values.astype(F32)


def dot(a, b, dims=PLAIN):
    return lax.dot_general(a, b, dims, preferred_element_type=F32)


def split_parts(values):
    upper = values.astype(BF)
    return upper, (values - wide(upper)).astype(BF)


def token_adapters(tenant_lengths, tenant_adapter, tok_count, first_token):
    starts_at = jnp.cumsum(tenant_lengths) - tenant_lengths
    position = first_token + jnp.arange(tok_count, dtype=jnp.int32)
    tenant = jnp.sum((starts_at[None, :] <= position[:, None]).astype(jnp.int32), axis=1) - 1
    picked = (
        tenant[:, None] == jnp.arange(tenant_lengths.shape[0], dtype=jnp.int32)[None, :]
    ).astype(jnp.int32)
    return jnp.sum(picked * tenant_adapter[None, :], axis=1)


def squares_kernel(adapters, where, frozen, down, up, out):
    weights = frozen[...]
    maps = down[...]
    flat = maps.shape[1]
    rank = flat // adapters
    cross = dot(maps, weights, FIRST)
    gram = dot(maps, maps, FIRST)
    rows = lax.broadcasted_iota(jnp.int32, (flat, flat), 0) // rank
    cols = lax.broadcasted_iota(jnp.int32, (flat, flat), 1) // rank
    upper, lower = split_parts(jnp.where(rows == cols, gram, 0.0))
    outer = up[...]
    gram_up = dot(upper, outer) + dot(lower, outer)
    terms = wide(outer) * (2.0 * cross + gram_up)
    squares = jnp.sum(jnp.square(wide(weights)), axis=0, keepdims=True)
    out[...] = squares + jnp.sum(terms.reshape(adapters, rank, -1), axis=1)


def column_squares(frozen, down, up, adapters, quarter):
    depth, flat = down.shape
    steps = frozen.shape[1] // SIDE // SPAN
    return pl.pallas_call(
        functools.partial(squares_kernel, adapters),
        grid_spec=pltpu.PrefetchScalarGridSpec(
            num_scalar_prefetch=1,
            grid=(steps,),
            in_specs=[
                pl.BlockSpec((depth, SPAN), lambda j, at: (0, at[0] * steps + j)),
                pl.BlockSpec((depth, flat), lambda j, at: (0, 0)),
                pl.BlockSpec((flat, SPAN), lambda j, at: (0, at[0] * steps + j)),
            ],
            out_specs=pl.BlockSpec((adapters, SPAN), lambda j, at: (0, j)),
        ),
        out_shape=jax.ShapeDtypeStruct((adapters, steps * SPAN), F32),
        compiler_params=pltpu.CompilerParams(vmem_limit_bytes=32 << 20),
        name="squares",
    )(quarter[None], frozen, down, up)


def mixed_kernel(where, tok0, tok1, low0, low1, hot0, hot1, grad0, grad1, frozen, up, out, mag, left, hot):
    rows = tok0.shape[1]
    depth = tok0.shape[2]

    @pl.when(pl.program_id(0) == 0)
    def _():
        left[:rows, :depth] = tok0[0]
        left[rows:, :depth] = tok1[0]
        left[:rows, depth:] = low0[0]
        left[rows:, depth:] = low1[0]
        hot[:, :rows] = hot0[0]
        hot[:, rows:] = hot1[0]

    total = dot(left[:, :depth], frozen[...]) + dot(left[:, depth:], up[...])
    out[...] = total.astype(BF)
    grads = jnp.concatenate([grad0[0], grad1[0]], axis=0)
    mag[...] = dot(hot[...], (total * wide(grads)).astype(BF))[: mag.shape[0]]


def mixed_part(stream, blocks, tokens, low, hot, grads, frozen, up, adapters):
    _, rows, depth = tokens.shape
    flat = up.shape[0]
    width = frozen.shape[1] // len(STREAMS)
    steps = width // SPAN

    def pair(shape, moving):
        def at(which):
            return lambda j, at: (at[which], 0, stream * steps + j if moving else 0)

        return [pl.BlockSpec(shape, at(0)), pl.BlockSpec(shape, at(1))]

    return pl.pallas_call(
        mixed_kernel,
        grid_spec=pltpu.PrefetchScalarGridSpec(
            num_scalar_prefetch=1,
            grid=(steps,),
            in_specs=[
                *pair((1, rows, depth), False),
                *pair((1, rows, flat), False),
                *pair((1, hot.shape[1], rows), False),
                *pair((1, rows, SPAN), True),
                pl.BlockSpec((depth, SPAN), lambda j, at: (0, stream * steps + j)),
                pl.BlockSpec((flat, SPAN), lambda j, at: (0, stream * steps + j)),
            ],
            out_specs=[
                pl.BlockSpec((2 * rows, SPAN), lambda j, at: (0, j)),
                pl.BlockSpec((adapters, SPAN), lambda j, at: (0, j)),
            ],
            scratch_shapes=[
                pltpu.VMEM((2 * rows, depth + flat), BF),
                pltpu.VMEM((hot.shape[1], 2 * rows), BF),
            ],
        ),
        out_shape=[
            jax.ShapeDtypeStruct((2 * rows, width), BF),
            jax.ShapeDtypeStruct((adapters, width), F32),
        ],
        compiler_params=pltpu.CompilerParams(vmem_limit_bytes=32 << 20),
        cost_estimate=pl.CostEstimate(
            flops=4 * rows * (depth + flat) * width,
            bytes_accessed=2 * (depth + 5 * rows) * width,
            transcendentals=0,
        ),
        name="mixed",
    )(blocks, tokens, tokens, low, low, hot, hot, grads, grads, frozen, up)


def on_device(
    tokens, frozen, adapter_down, adapter_up, magnitude, grad_out, tenant_lengths, tenant_adapter
):
    tok_rows, depth = tokens.shape
    adapters, cols = magnitude.shape
    flat = adapter_down.shape[1]
    rank = flat // adapters
    block = tok_rows // SIDE
    width = cols // len(STREAMS)
    quarter = cols // SIDE
    place = {axis: lax.axis_index(axis) for axis in ("dp", "z", "y", "col")}

    adapter = token_adapters(tenant_lengths, tenant_adapter, tok_rows, place["dp"] * tok_rows)
    own = adapter[:, None] == jnp.arange(adapters, dtype=jnp.int32)[None, :]
    slots = adapter[:, None] == (jnp.arange(flat, dtype=jnp.int32) // rank)[None, :]

    sq_part = column_squares(frozen, adapter_down, adapter_up, adapters, place["dp"])
    down_part = jnp.where(slots, dot(tokens, adapter_down), 0.0)
    low = down_part.astype(BF)
    pieces = quarter // flat
    small = sq_part
    down_sum = down_part
    for step, pairing in enumerate((("y", 1), ("z", 1), ("y", 3), ("z", 3))):
        upper, lower = split_parts(small)
        parts = [down_sum.astype(BF)]
        for half in (upper, lower):
            parts += [half[:, i * flat : (i + 1) * flat] for i in range(pieces)]
        sent = jnp.concatenate(parts, axis=0)
        total = wide(sent) + wide(swap(sent, pairing))
        down_sum = total[:tok_rows]
        both = total[tok_rows:].reshape(2, pieces, adapters, flat)
        both = both[0] + both[1]
        small = jnp.concatenate([both[i] for i in range(pieces)], axis=1)
    col_sq = jnp.zeros((adapters, cols), F32)
    spots = (place["dp"], place["dp"] ^ 1, place["dp"] ^ 3, place["dp"] ^ 2)
    found = (
        small,
        swap(small, ("dp", 1)),
        swap(small, ("dp", 3)),
        swap(small, ("dp", 2)),
    )
    for spot, values in zip(spots, found, strict=True):
        col_sq = lax.dynamic_update_slice(col_sq, values, (0, spot * quarter))
    col_norm = jnp.sqrt(col_sq + 1e-06)
    scale_table = magnitude / col_norm
    upper, rest = split_parts(scale_table)
    middle, last = split_parts(scale_table - wide(upper))
    table = jnp.concatenate([upper, middle, last], axis=0)
    hot3 = jnp.concatenate([own.astype(BF)] * 3, axis=1)

    tok_blocks = tokens.reshape(SIDE, block, depth)
    low_blocks = low.reshape(SIDE, block, flat)
    grad_blocks = grad_out.reshape(SIDE, block, cols)
    hot_rows = jnp.pad(own.astype(BF), ((0, 0), (0, 16 - adapters))).T
    hot_blocks = hot_rows.reshape(16, SIDE, block).transpose(1, 0, 2)

    def part(stream, blocks):
        return mixed_part(
            stream,
            jnp.stack(blocks).astype(jnp.int32),
            tok_blocks,
            low_blocks,
            hot_blocks,
            grad_blocks,
            frozen,
            adapter_up,
            adapters,
        )

    away, kept = [], []
    for stream, (one, two, _, _) in enumerate(STREAMS):
        me = place[one[0]]
        there = me ^ one[1]
        away.append(part(stream, (there, there ^ two[1])))
    arrived = [swap(sent, order[0]) for (sent, _), order in zip(away, STREAMS, strict=True)]
    for stream, (one, two, _, _) in enumerate(STREAMS):
        me = place[one[0]]
        kept.append(part(stream, (me, me ^ two[1])))
    mag = jnp.concatenate([a[1] + k[1] for a, k in zip(away, kept, strict=True)], axis=1)
    for pairing in (("dp", 1), ("dp", 3), ("y", 1), ("z", 1), ("y", 3), ("z", 3)):
        mag = mag + swap(mag, pairing)

    adapted = jnp.zeros((tok_rows, cols), BF)
    for stream, (one, two, three, four) in enumerate(STREAMS):
        first = stream * width
        me = place[one[0]]
        got = wide(kept[stream][0]) + wide(arrived[stream])
        total = got[:block] + wide(swap(got[block:].astype(BF), two))
        for pairing in (three, four):
            sent = total.astype(BF)
            total = wide(sent) + wide(swap(sent, pairing))
        rows = lax.dynamic_slice_in_dim(hot3, me * block, block, 0)
        done = (dot(rows, table[:, first : first + width]) * total).astype(BF)
        near = swap(done, one)
        far = swap(jnp.concatenate([done, near], axis=0), two)
        there = me ^ two[1]
        for spot, values in (
            (me, done),
            (me ^ one[1], near),
            (there, far[:block]),
            (there ^ one[1], far[block:]),
        ):
            adapted = lax.dynamic_update_slice(adapted, values, (spot * block, first))

    scaled_grad = (wide(grad_out) * dot(hot3, table)).astype(BF)
    down_upper, down_lower = split_parts(down_sum)
    grad_up = dot(down_upper, scaled_grad, FIRST) + dot(down_lower, scaled_grad, FIRST)
    back = jnp.where(slots, dot(scaled_grad, adapter_up, LAST), 0.0)
    back_upper, back_lower = split_parts(back)
    back_down = dot(back_upper, tokens, FIRST) + dot(back_lower, tokens, FIRST)
    input_part = dot(scaled_grad, frozen, LAST) + (
        dot(back_upper, adapter_down, LAST) + dot(back_lower, adapter_down, LAST)
    )
    sent = jnp.concatenate([input_part, back_down], axis=0).astype(BF)
    total = wide(sent) + wide(lax.ppermute(sent, "col", [(0, 1), (1, 0)]))
    input_grad = total[:tok_rows].astype(BF)
    cut = (cols + depth) // 2 // 256 * 256
    one = grad_up[:, :cut]
    two = jnp.concatenate([grad_up[:, cut:], total[tok_rows:]], axis=1)
    for flip in (1, 3):
        sent = one.astype(BF)
        one = wide(sent) + wide(swap(sent, ("dp", flip)))
        sent = two.astype(BF)
        two = wide(sent) + wide(swap(sent, ("dp", 4 - flip)))
    grad_up = jnp.concatenate([one, two[:, : cols - cut]], axis=1)
    grad_down = two[:, cols - cut :].T
    return (adapted, input_grad, grad_down, grad_up, mag / col_norm)


def solution(mesh):
    assert mesh.axis_names == ("dp", "row", "col")
    grid = Mesh(mesh.devices.reshape(SIDE, SIDE, SIDE, 2), ("dp", "z", "y", "col"))
    row = ("z", "y")
    placed = (
        P("dp", row),
        P(row, "col"),
        P(row, None),
        P(None, "col"),
        P(None, "col"),
        P("dp", "col"),
        P(),
        P(),
    )
    return jax.shard_map(
        on_device,
        mesh=grid,
        in_specs=placed,
        out_specs=(P("dp", "col"), P("dp", row), P(row, None), P(None, "col"), P(None, "col")),
        check_vma=False,
    )
```

time: 541 us -> 289 us (0.53)
  waiting for transfers between devices: 345 us -> 99.8 us
  blocking collectives: 78.6 us -> 0 us
  matrix products: 86.7 us -> 24.8 us
  starting transfers between devices: 0.16 us -> 59.7 us
  local copies, waits for them, and re-layouts: 6.53 us -> 54.1 us
  Pallas kernels: 0 us -> 26.5 us
  other arithmetic: 9.28 us -> 21.2 us
  between operations: 13.9 us -> 2.17 us
    psum x4 -> x0, waiting for transfers between devices: 345 us -> none  [the longest x1 134 us: on_device(): lax.psum((wide_left(picked_down, picked_grad, contract_first), mag_part),...]
    ppermute x0 -> x42, waiting for transfers between devices: none -> 99.8 us  [the longest x41 99.8 us: swap(): return lax.ppermute(values, axis, [(i, i ^ flip) for i in range(SIDE)])]
    psum x1 -> x0, blocking collectives: 78.6 us -> none  [on_device(): lax.psum((squares_part, cross_part, gram_part), 'row')]
    dot_general x18 -> x14, matrix products: 86.7 us -> 24.8 us  [dot(): return lax.dot_general(a, b, dims, preferred_element_type=F32)]
    ppermute x0 -> x42, starting transfers between devices: none -> 59.7 us  [the longest x41 59.7 us: swap(): return lax.ppermute(values, axis, [(i, i ^ flip) for i in range(SIDE)])]
    unnamed x24 -> x218, local copies, waits for them, and re-layouts: 5.73 us -> 45.5 us
    pallas_call x0 -> x9, Pallas kernels: none -> 26.5 us  [the longest x8 24.3 us: mixed_part(): pl.pallas_call(mixed_kernel, grid_spec=pltpu.PrefetchScalarGridSpec(num_s...]
    add x0 -> x23, other arithmetic: none -> 9.54 us  [the longest x4 4.8 us: on_device(): got = wide(kept[stream][0]) + wide(arrived[stream])]
  transfers between devices with their start and end apart: 4 -> 42, of which waited for: 4 -> 18; matrix products, arithmetic and copies ran while one was open for 5% -> 18% of each run, Pallas kernels for 0% -> 8%
where the time goes in v1:
time: 289 us; the launch traced here: 288 us
  waiting for transfers between devices  99.8 us (35%)
  starting transfers between devices  59.7 us (21%)
  local copies, waits for them, and re-layouts  54.1 us (19%)
  Pallas kernels  26.5 us (9%)
  matrix products  24.8 us (9%)
  other arithmetic  21.2 us (7%)
    ppermute x41, waiting for transfers between devices, swap(): return lax.ppermute(values, axis, [(i, i ^ flip) for i in range(SIDE)])  99.8 us
    ppermute x41, starting transfers between devices, swap(): return lax.ppermute(values, axis, [(i, i ^ flip) for i in range(SIDE)])  59.7 us
    unnamed x218, local copies, waits for them, and re-layouts  45.5 us
    dot_general x14, matrix products, dot(): return lax.dot_general(a, b, dims, preferred_element_type=F32)  24.8 us
    pallas_call x8, Pallas kernels, mixed_part(): pl.pallas_call(mixed_kernel, grid_spec=pltpu.PrefetchScalarGridSpec(num_s...  24.3 us
  transfers between devices with their start and end apart: 42, of which 18 were waited for; matrix products, arithmetic and copies ran while one was open for 18% of the time, Pallas kernels for 8%

profile of v1, /device:TPU:0, one launch (start us, length us, event | category | flops | bytes accessed | tf_op | source)
XLA Modules:
  0.0 288.3 jit_solution(11354346020198574417)
XLA Ops:
  2.3 4.1 %copy-done.2 = bf16[896,6144]{1,0:T(8,128)(2,1)S(1)} copy-done((bf16[896,6144]{1,0:T(8,128)(2,1)S(1)}, bf16[896,6144]{1,0:T(8,128)(2,1)}, u32[]{:S(2)}) %copy-start.2) | copy-done | bytes 11010072
  30.6 4.1 %copy-done.3 = bf16[896,6144]{1,0:T(8,128)(2,1)S(1)} copy-done((bf16[896,6144]{1,0:T(8,128)(2,1)S(1)}, bf16[896,6144]{1,0:T(8,128)(2,1)}, u32[]{:S(2)}) %copy-start.3) | copy-done | bytes 11010072
  36.2 3.4 %mixed.9 = (bf16[256,1536]{1,0:T(8,128)(2,1)}, f32[8,1536]{1,0:T(8,128)S(1)}) custom-call(s32[2]{0:T(128)S(1)} %get-tuple-element.75.where, bf16[4,128,896]{2,1,0:T(8,128)(2,1)S(1)} %bitcast.59, bf16[4,128,896]{2,1,0:T(8,128)(2,1)S(1)} %bitcast.60, bf16[4,128,128]{2,1,0:T(8,128)(2,1)S(1)} %bitcast.75, bf16[4,128,128]{2,1,0:T(8,128)(2,1)S(1)} %bitcast.76, ...), custom_call_target="tpu_custom_call" | custom-call | flops 805306368 | bytes 4718592 | tf_op jit(solution)/shard_map/mixed/pallas_call | solution.py:124
  39.6 4.1 %copy-done.4 = bf16[896,6144]{1,0:T(8,128)(2,1)S(1)} copy-done((bf16[896,6144]{1,0:T(8,128)(2,1)S(1)}, bf16[896,6144]{1,0:T(8,128)(2,1)}, u32[]{:S(2)}) %copy-start.4) | copy-done | bytes 11010072
  50.3 4.1 %copy-done.5 = bf16[896,6144]{1,0:T(8,128)(2,1)S(1)} copy-done((bf16[896,6144]{1,0:T(8,128)(2,1)S(1)}, bf16[896,6144]{1,0:T(8,128)(2,1)}, u32[]{:S(2)}) %copy-start.5) | copy-done | bytes 11010072
  61.5 3.4 %mixed.13 = (bf16[256,1536]{1,0:T(8,128)(2,1)}, f32[8,1536]{1,0:T(8,128)S(1)}) custom-call(s32[2]{0:T(128)S(1)} %get-tuple-element.79.where, bf16[4,128,896]{2,1,0:T(8,128)(2,1)S(1)} %bitcast.67, bf16[4,128,896]{2,1,0:T(8,128)(2,1)S(1)} %bitcast.68, bf16[4,128,128]{2,1,0:T(8,128)(2,1)S(1)} %bitcast.83, bf16[4,128,128]{2,1,0:T(8,128)(2,1)S(1)} %bitcast.84, ...), custom_call_target="tpu_custom_call" | custom-call | flops 805306368 | bytes 4718592 | tf_op jit(solution)/shard_map/mixed/pallas_call | solution.py:124
  67.8 3.4 %mixed.11 = (bf16[256,1536]{1,0:T(8,128)(2,1)}, f32[8,1536]{1,0:T(8,128)S(1)}) custom-call(s32[2]{0:T(128)S(1)} %get-tuple-element.77.where, bf16[4,128,896]{2,1,0:T(8,128)(2,1)S(1)} %bitcast.71, bf16[4,128,896]{2,1,0:T(8,128)(2,1)S(1)} %bitcast.72, bf16[4,128,128]{2,1,0:T(8,128)(2,1)S(1)} %bitcast.87, bf16[4,128,128]{2,1,0:T(8,128)(2,1)S(1)} %bitcast.88, ...), custom_call_target="tpu_custom_call" | custom-call | flops 805306368 | bytes 4718592 | tf_op jit(solution)/shard_map/mixed/pallas_call | solution.py:124
  91.3 4.1 %collective-permute-start.3 = (bf16[704,128]{1,0:T(8,128)(2,1)S(1)}, bf16[704,128]{1,0:T(8,128)(2,1)}, u32[]{:S(2)}, u32[]{:S(2)}) collective-permute-start(bf16[704,128]{1,0:T(8,128)(2,1)S(1)} %constant_dynamic-update-slice_fusion.111), channel_id=1, source_target_pairs={{0,24},{8,16},{16,8},{24,0},{1,25},{9,17},{17,9},{25,1},{2,26},{10... | collective-permute-start | bytes 540680 | tf_op jit(solution)/shard_map/ppermute | solution.py:29
  101.9 3.7 %collective-permute-done.4 = f32[8,1536]{1,0:T(8,128)S(1)} collective-permute-done((f32[8,1536]{1,0:T(8,128)S(1)}, f32[8,1536]{1,0:T(8,128)S(1)}, u32[]{:S(2)}, u32[]{:S(2)}) %collective-permute-start.4) | collective-permute-done | bytes 49184 | tf_op jit(solution)/shard_map/ppermute | solution.py:29
  112.1 4.5 %collective-permute-done.6 = f32[8,1536]{1,0:T(8,128)S(1)} collective-permute-done((f32[8,1536]{1,0:T(8,128)S(1)}, f32[8,1536]{1,0:T(8,128)S(1)}, u32[]{:S(2)}, u32[]{:S(2)}) %collective-permute-start.6) | collective-permute-done | bytes 49184 | tf_op jit(solution)/shard_map/ppermute | solution.py:29
  135.8 5.0 %collective-permute-done.41 = f32[8,6144]{1,0:T(8,128)S(1)} collective-permute-done((f32[8,6144]{1,0:T(8,128)S(1)}, f32[8,6144]{1,0:T(8,128)S(1)}, u32[]{:S(2)}, u32[]{:S(2)}) %collective-permute-start.41) | collective-permute-done | bytes 196640 | tf_op jit(solution)/shard_map/ppermute | solution.py:29
  141.6 4.5 %multiply_convert_fusion = bf16[512,6144]{1,0:T(8,128)(2,1)} fusion(bf16[512,6144]{1,0:T(8,128)(2,1)S(1)} %bitcast.56, bf16[512,8]{0,1:T(8,128)(2,1)S(1)} %fusion.26, bf16[8,6144]{1,0:T(8,128)(2,1)S(1)} %get-tuple-element.62, bf16[8,6144]{1,0:T(8,128)(2,1)S(1)} %get-tuple-element.61, bf16[8,6144]{1,0:T(8,128)(2,1)S(1)} %get-tuple-element.60), kind=kOutput, calls=%fused_computation | convolution fusion | flops 161390592 | bytes 12886016 | tf_op jit(solution)/shard_map/dot_general | solution.py:37
  146.2 9.7 %fusion.41 = f32[512,896]{1,0:T(8,128)} fusion(bf16[512,6144]{1,0:T(8,128)(2,1)} %multiply_convert_fusion, bf16[896,6144]{1,0:T(8,128)(2,1)S(1)} %bitcast.58), kind=kOutput, calls=%fused_computation.285 | convolution fusion | flops 5637144576 | bytes 19136512 | tf_op jit(solution)/shard_map/dot_general | solution.py:37
  155.9 4.0 %fusion.9 = f32[128,6144]{1,0:T(8,128)S(1)} fusion(bf16[512,6144]{1,0:T(8,128)(2,1)} %multiply_convert_fusion, f32[704,128]{1,0:T(8,128)S(1)} %convert_add_fusion.6), kind=kOutput, calls=%fused_computation.220 | convolution fusion | flops 805568512 | bytes 9699328 | tf_op jit(solution)/shard_map/dot_general | solution.py:37
  177.8 8.4 %collective-permute-done.10 = bf16[128,1536]{1,0:T(8,128)(2,1)S(1)} collective-permute-done((bf16[128,1536]{1,0:T(8,128)(2,1)S(1)}, bf16[128,1536]{1,0:T(8,128)(2,1)S(1)}, u32[]{:S(2)}, u32[]{:S(2)}) %collective-permute-start.10) | collective-permute-done | bytes 393248 | tf_op jit(solution)/shard_map/ppermute | solution.py:29
  187.5 7.7 %collective-permute-done.11 = bf16[128,1536]{1,0:T(8,128)(2,1)S(1)} collective-permute-done((bf16[128,1536]{1,0:T(8,128)(2,1)S(1)}, bf16[128,1536]{1,0:T(8,128)(2,1)S(1)}, u32[]{:S(2)}, u32[]{:S(2)}) %collective-permute-start.11) | collective-permute-done | bytes 393248 | tf_op jit(solution)/shard_map/ppermute | solution.py:29
  199.1 17.4 %collective-permute-done.12 = bf16[256,1536]{1,0:T(8,128)(2,1)S(1)} collective-permute-done((bf16[256,1536]{1,0:T(8,128)(2,1)S(1)}, bf16[256,1536]{1,0:T(8,128)(2,1)S(1)}, u32[]{:S(2)}, u32[]{:S(2)}) %collective-permute-start.12) | collective-permute-done | bytes 786464 | tf_op jit(solution)/shard_map/ppermute | solution.py:29
  221.2 4.8 %collective-permute-done.17 = bf16[128,1536]{1,0:T(8,128)(2,1)S(1)} collective-permute-done((bf16[128,1536]{1,0:T(8,128)(2,1)S(1)}, bf16[128,1536]{1,0:T(8,128)(2,1)S(1)}, u32[]{:S(2)}, u32[]{:S(2)}) %collective-permute-start.17) | collective-permute-done | bytes 393248 | tf_op jit(solution)/shard_map/ppermute | solution.py:29
  230.1 9.5 %collective-permute-done.18 = bf16[256,1536]{1,0:T(8,128)(2,1)S(1)} collective-permute-done((bf16[256,1536]{1,0:T(8,128)(2,1)S(1)}, bf16[256,1536]{1,0:T(8,128)(2,1)S(1)}, u32[]{:S(2)}, u32[]{:S(2)}) %collective-permute-start.18) | collective-permute-done | bytes 786464 | tf_op jit(solution)/shard_map/ppermute | solution.py:29
  242.0 6.0 %collective-permute-done.23 = bf16[128,1536]{1,0:T(8,128)(2,1)S(1)} collective-permute-done((bf16[128,1536]{1,0:T(8,128)(2,1)S(1)}, bf16[128,1536]{1,0:T(8,128)(2,1)S(1)}, u32[]{:S(2)}, u32[]{:S(2)}) %collective-permute-start.23) | collective-permute-done | bytes 393248 | tf_op jit(solution)/shard_map/ppermute | solution.py:29
  253.3 11.9 %collective-permute-done.24 = bf16[256,1536]{1,0:T(8,128)(2,1)S(1)} collective-permute-done((bf16[256,1536]{1,0:T(8,128)(2,1)S(1)}, bf16[256,1536]{1,0:T(8,128)(2,1)S(1)}, u32[]{:S(2)}, u32[]{:S(2)}) %collective-permute-start.24) | collective-permute-done | bytes 786464 | tf_op jit(solution)/shard_map/ppermute | solution.py:29
  270.3 4.3 %collective-permute-done.29 = bf16[128,1536]{1,0:T(8,128)(2,1)S(1)} collective-permute-done((bf16[128,1536]{1,0:T(8,128)(2,1)S(1)}, bf16[128,1536]{1,0:T(8,128)(2,1)S(1)}, u32[]{:S(2)}, u32[]{:S(2)}) %collective-permute-start.29) | collective-permute-done | bytes 393248 | tf_op jit(solution)/shard_map/ppermute | solution.py:29
  276.0 3.4 %pad_maximum_fusion = f32[128,6144]{1,0:T(8,128)} fusion(f32[128,2816]{1,0:T(8,128)S(1)} %slice-done.7, f32[128,3328]{1,0:T(8,128)} %convert_add_fusion.1), kind=kLoop, calls=%fused_computation.3 | loop fusion | flops 786432 | bytes 6291456 | tf_op jit(solution)/shard_map/concatenate | solution.py:284
  280.2 6.5 %collective-permute-done.30 = bf16[256,1536]{1,0:T(8,128)(2,1)S(1)} collective-permute-done((bf16[256,1536]{1,0:T(8,128)(2,1)S(1)}, bf16[256,1536]{1,0:T(8,128)(2,1)S(1)}, u32[]{:S(2)}, u32[]{:S(2)}) %collective-permute-start.30) | collective-permute-done | bytes 786464 | tf_op jit(solution)/shard_map/ppermute | solution.py:29
  (405 shorter events, 143.8 us)
Async XLA Ops:
  26.1 49.7 %collective-permute-start = (bf16[704,128]{1,0:T(8,128)(2,1)}, bf16[704,128]{1,0:T(8,128)(2,1)S(1)}, u32[]{:S(2)}, u32[]{:S(2)}) collective-permute-start(bf16[704,128]{1,0:T(8,128)(2,1)} %constant_dynamic-update-slice_fusion), channel_id=1, source_target_pairs={{0,2},{2,0},{4,6},{6,4},{1,3},{3,1},{5,7},{7,5},{8,10},{10,8},{12,... | collective-permute-start | bytes 540680 | tf_op jit(solution)/shard_map/ppermute | solution.py:29
  95.4 21.5 %collective-permute-start.7 = (bf16[256,1536]{1,0:T(8,128)(2,1)}, bf16[256,1536]{1,0:T(8,128)(2,1)}, u32[]{:S(2)}, u32[]{:S(2)}) collective-permute-start(bf16[256,1536]{1,0:T(8,128)(2,1)} %get-tuple-element.22), channel_id=1, source_target_pairs={{0,2},{2,0},{4,6},{6,4},{1,3},{3,1},{5,7},{7,5},{8,10},{10,8},{12,... | collective-permute-start | bytes 2359304 | tf_op jit(solution)/shard_map/ppermute | solution.py:29
  95.4 29.5 %collective-permute-start.13 = (bf16[256,1536]{1,0:T(8,128)(2,1)}, bf16[256,1536]{1,0:T(8,128)(2,1)}, u32[]{:S(2)}, u32[]{:S(2)}) collective-permute-start(bf16[256,1536]{1,0:T(8,128)(2,1)} %get-tuple-element.24), channel_id=1, source_target_pairs={{0,6},{2,4},{4,2},{6,0},{1,7},{3,5},{5,3},{7,1},{8,14},{10,12},{12... | collective-permute-start | bytes 2359304 | tf_op jit(solution)/shard_map/ppermute | solution.py:29
  97.7 30.4 %collective-permute-start.19 = (bf16[256,1536]{1,0:T(8,128)(2,1)}, bf16[256,1536]{1,0:T(8,128)(2,1)}, u32[]{:S(2)}, u32[]{:S(2)}) collective-permute-start(bf16[256,1536]{1,0:T(8,128)(2,1)} %get-tuple-element.26), channel_id=1, source_target_pairs={{0,8},{8,0},{16,24},{24,16},{1,9},{9,1},{17,25},{25,17},{2,10},{10... | collective-permute-start | bytes 2359304 | tf_op jit(solution)/shard_map/ppermute | solution.py:29
  97.7 35.7 %collective-permute-start.25 = (bf16[256,1536]{1,0:T(8,128)(2,1)}, bf16[256,1536]{1,0:T(8,128)(2,1)S(1)}, u32[]{:S(2)}, u32[]{:S(2)}) collective-permute-start(bf16[256,1536]{1,0:T(8,128)(2,1)} %copy-done.17), channel_id=1, source_target_pairs={{0,24},{8,16},{16,8},{24,0},{1,25},{9,17},{17,9},{25,1},{2,26},{10... | collective-permute-start | bytes 2359304 | tf_op jit(solution)/shard_map/ppermute | solution.py:29
  118.6 43.2 %collective-permute-start.8 = (bf16[128,1536]{1,0:T(8,128)(2,1)S(1)}, bf16[128,1536]{1,0:T(8,128)(2,1)}, u32[]{:S(2)}, u32[]{:S(2)}) collective-permute-start(bf16[128,1536]{1,0:T(8,128)(2,1)S(1)} %slice.1202), channel_id=1, source_target_pairs={{0,6},{2,4},{4,2},{6,0},{1,7},{3,5},{5,3},{7,1},{8,14},{10,12},{12... | collective-permute-start | bytes 1179656 | tf_op jit(solution)/shard_map/ppermute | solution.py:29
  127.3 38.7 %collective-permute-start.14 = (bf16[128,1536]{1,0:T(8,128)(2,1)}, bf16[128,1536]{1,0:T(8,128)(2,1)}, u32[]{:S(2)}, u32[]{:S(2)}) collective-permute-start(bf16[128,1536]{1,0:T(8,128)(2,1)} %slice.1201), channel_id=1, source_target_pairs={{0,2},{2,0},{4,6},{6,4},{1,3},{3,1},{5,7},{7,5},{8,10},{10,8},{12,... | collective-permute-start | bytes 1179656 | tf_op jit(solution)/shard_map/ppermute | solution.py:29
  129.7 40.9 %collective-permute-start.20 = (bf16[128,1536]{1,0:T(8,128)(2,1)S(1)}, bf16[128,1536]{1,0:T(8,128)(2,1)}, u32[]{:S(2)}, u32[]{:S(2)}) collective-permute-start(bf16[128,1536]{1,0:T(8,128)(2,1)S(1)} %slice.1200), channel_id=1, source_target_pairs={{0,24},{8,16},{16,8},{24,0},{1,25},{9,17},{17,9},{25,1},{2,26},{10... | collective-permute-start | bytes 1179656 | tf_op jit(solution)/shard_map/ppermute | solution.py:29
  134.4 40.1 %collective-permute-start.26 = (bf16[128,1536]{1,0:T(8,128)(2,1)}, bf16[128,1536]{1,0:T(8,128)(2,1)}, u32[]{:S(2)}, u32[]{:S(2)}) collective-permute-start(bf16[128,1536]{1,0:T(8,128)(2,1)} %slice.1199), channel_id=1, source_target_pairs={{0,8},{8,0},{16,24},{24,16},{1,9},{9,1},{17,25},{25,17},{2,10},{10... | collective-permute-start | bytes 1179656 | tf_op jit(solution)/shard_map/ppermute | solution.py:29
  164.1 13.0 %collective-permute-start.9 = (bf16[128,1536]{1,0:T(8,128)(2,1)S(1)}, bf16[128,1536]{1,0:T(8,128)(2,1)S(1)}, u32[]{:S(2)}, u32[]{:S(2)}) collective-permute-start(bf16[128,1536]{1,0:T(8,128)(2,1)S(1)} %fusion.6), channel_id=1, source_target_pairs={{0,8},{8,0},{16,24},{24,16},{1,9},{9,1},{17,25},{25,17},{2,10},{10... | collective-permute-start | bytes 1179656 | tf_op jit(solution)/shard_map/ppermute | solution.py:29
  167.2 20.1 %collective-permute-start.15 = (bf16[128,1536]{1,0:T(8,128)(2,1)S(1)}, bf16[128,1536]{1,0:T(8,128)(2,1)S(1)}, u32[]{:S(2)}, u32[]{:S(2)}) collective-permute-start(bf16[128,1536]{1,0:T(8,128)(2,1)S(1)} %fusion.5), channel_id=1, source_target_pairs={{0,24},{8,16},{16,8},{24,0},{1,25},{9,17},{17,9},{25,1},{2,26},{10... | collective-permute-start | bytes 1179656 | tf_op jit(solution)/shard_map/ppermute | solution.py:29
  171.8 23.7 %collective-permute-start.21 = (bf16[128,1536]{1,0:T(8,128)(2,1)S(1)}, bf16[128,1536]{1,0:T(8,128)(2,1)S(1)}, u32[]{:S(2)}, u32[]{:S(2)}) collective-permute-start(bf16[128,1536]{1,0:T(8,128)(2,1)S(1)} %fusion.4), channel_id=1, source_target_pairs={{0,2},{2,0},{4,6},{6,4},{1,3},{3,1},{5,7},{7,5},{8,10},{10,8},{12,... | collective-permute-start | bytes 1179656 | tf_op jit(solution)/shard_map/ppermute | solution.py:29
  175.6 22.3 %collective-permute-start.27 = (bf16[128,1536]{1,0:T(8,128)(2,1)S(1)}, bf16[128,1536]{1,0:T(8,128)(2,1)S(1)}, u32[]{:S(2)}, u32[]{:S(2)}) collective-permute-start(bf16[128,1536]{1,0:T(8,128)(2,1)S(1)} %fusion.3), channel_id=1, source_target_pairs={{0,6},{2,4},{4,2},{6,0},{1,7},{3,5},{5,3},{7,1},{8,14},{10,12},{12... | collective-permute-start | bytes 1179656 | tf_op jit(solution)/shard_map/ppermute | solution.py:29
  177.7 49.2 %collective-permute-start.31 = (bf16[640,896]{1,0:T(8,128)(2,1)S(1)}, bf16[640,896]{1,0:T(8,128)(2,1)S(1)}, u32[]{:S(2)}, u32[]{:S(2)}) collective-permute-start(bf16[640,896]{1,0:T(8,128)(2,1)S(1)} %pad_maximum_fusion.1), channel_id=1, source_target_pairs={{0,1},{1,0},{2,3},{3,2},{4,5},{5,4},{6,7},{7,6},{8,9},{9,8},{10,11... | collective-permute-start | bytes 3440648 | tf_op jit(solution)/shard_map/ppermute | solution.py:274
  186.3 32.9 %collective-permute-start.34 = (bf16[128,3328]{1,0:T(8,128)(2,1)S(1)}, bf16[128,3328]{1,0:T(8,128)(2,1)S(1)}, u32[]{:S(2)}, u32[]{:S(2)}) collective-permute-start(bf16[128,3328]{1,0:T(8,128)(2,1)S(1)} %slice.987), channel_id=1, source_target_pairs={{0,32},{32,0},{64,96},{96,64},{1,33},{33,1},{65,97},{97,65},{2,34}... | collective-permute-start | bytes 2555912 | tf_op jit(solution)/shard_map/ppermute | solution.py:29
  195.2 21.4 %collective-permute-start.16 = (bf16[128,1536]{1,0:T(8,128)(2,1)S(1)}, bf16[128,1536]{1,0:T(8,128)(2,1)S(1)}, u32[]{:S(2)}, u32[]{:S(2)}) collective-permute-start(bf16[128,1536]{1,0:T(8,128)(2,1)S(1)} %add_convert_fusion.6), channel_id=1, source_target_pairs={{0,8},{8,0},{16,24},{24,16},{1,9},{9,1},{17,25},{25,17},{2,10},{10... | collective-permute-start | bytes 1179656 | tf_op jit(solution)/shard_map/ppermute | solution.py:29
  195.5 21.0 %collective-permute-start.12 = (bf16[256,1536]{1,0:T(8,128)(2,1)S(1)}, bf16[256,1536]{1,0:T(8,128)(2,1)S(1)}, u32[]{:S(2)}, u32[]{:S(2)}) collective-permute-start(bf16[256,1536]{1,0:T(8,128)(2,1)S(1)} %pad_maximum_fusion.3), channel_id=1, source_target_pairs={{0,6},{2,4},{4,2},{6,0},{1,7},{3,5},{5,3},{7,1},{8,14},{10,12},{12... | collective-permute-start | bytes 2359304 | tf_op jit(solution)/shard_map/ppermute | solution.py:29
  197.9 41.9 %collective-permute-start.22 = (bf16[128,1536]{1,0:T(8,128)(2,1)S(1)}, bf16[128,1536]{1,0:T(8,128)(2,1)S(1)}, u32[]{:S(2)}, u32[]{:S(2)}) collective-permute-start(bf16[128,1536]{1,0:T(8,128)(2,1)S(1)} %add_convert_fusion.5), channel_id=1, source_target_pairs={{0,6},{2,4},{4,2},{6,0},{1,7},{3,5},{5,3},{7,1},{8,14},{10,12},{12... | collective-permute-start | bytes 1179656 | tf_op jit(solution)/shard_map/ppermute | solution.py:29
  216.5 48.8 %collective-permute-start.28 = (bf16[128,1536]{1,0:T(8,128)(2,1)S(1)}, bf16[128,1536]{1,0:T(8,128)(2,1)S(1)}, u32[]{:S(2)}, u32[]{:S(2)}) collective-permute-start(bf16[128,1536]{1,0:T(8,128)(2,1)S(1)} %add_convert_fusion.4), channel_id=1, source_target_pairs={{0,2},{2,0},{4,6},{6,4},{1,3},{3,1},{5,7},{7,5},{8,10},{10,8},{12,... | collective-permute-start | bytes 1179656 | tf_op jit(solution)/shard_map/ppermute | solution.py:29
  219.4 21.2 %collective-permute-start.35 = (bf16[128,3328]{1,0:T(8,128)(2,1)S(1)}, bf16[128,3328]{1,0:T(8,128)(2,1)S(1)}, u32[]{:S(2)}, u32[]{:S(2)}) collective-permute-start(bf16[128,3328]{1,0:T(8,128)(2,1)S(1)} %add_convert_fusion.3), channel_id=1, source_target_pairs={{0,96},{32,64},{64,32},{96,0},{1,97},{33,65},{65,33},{97,1},{2,98}... | collective-permute-start | bytes 2555912 | tf_op jit(solution)/shard_map/ppermute | solution.py:29
  226.0 13.6 %collective-permute-start.18 = (bf16[256,1536]{1,0:T(8,128)(2,1)S(1)}, bf16[256,1536]{1,0:T(8,128)(2,1)S(1)}, u32[]{:S(2)}, u32[]{:S(2)}) collective-permute-start(bf16[256,1536]{1,0:T(8,128)(2,1)S(1)} %pad_maximum_fusion.4), channel_id=1, source_target_pairs={{0,2},{2,0},{4,6},{6,4},{1,3},{3,1},{5,7},{7,5},{8,10},{10,8},{12,... | collective-permute-start | bytes 2359304 | tf_op jit(solution)/shard_map/ppermute | solution.py:29
  228.3 22.6 %collective-permute-start.32 = (bf16[128,3712]{1,0:T(8,128)(2,1)S(1)}, bf16[128,3712]{1,0:T(8,128)(2,1)S(1)}, u32[]{:S(2)}, u32[]{:S(2)}) collective-permute-start(bf16[128,3712]{1,0:T(8,128)(2,1)S(1)} %pad_maximum_fusion.2), channel_id=1, source_target_pairs={{0,96},{32,64},{64,32},{96,0},{1,97},{33,65},{65,33},{97,1},{2,98}... | collective-permute-start | bytes 2850824 | tf_op jit(solution)/shard_map/ppermute | solution.py:29
  248.0 17.2 %collective-permute-start.24 = (bf16[256,1536]{1,0:T(8,128)(2,1)S(1)}, bf16[256,1536]{1,0:T(8,128)(2,1)S(1)}, u32[]{:S(2)}, u32[]{:S(2)}) collective-permute-start(bf16[256,1536]{1,0:T(8,128)(2,1)S(1)} %pad_maximum_fusion.5), channel_id=1, source_target_pairs={{0,24},{8,16},{16,8},{24,0},{1,25},{9,17},{17,9},{25,1},{2,26},{10... | collective-permute-start | bytes 2359304 | tf_op jit(solution)/shard_map/ppermute | solution.py:29
  251.2 17.5 %collective-permute-start.33 = (bf16[128,3712]{1,0:T(8,128)(2,1)S(1)}, bf16[128,3712]{1,0:T(8,128)(2,1)S(1)}, u32[]{:S(2)}, u32[]{:S(2)}) collective-permute-start(bf16[128,3712]{1,0:T(8,128)(2,1)S(1)} %add_convert_fusion.1), channel_id=1, source_target_pairs={{0,32},{32,0},{64,96},{96,64},{1,33},{33,1},{65,97},{97,65},{2,34}... | collective-permute-start | bytes 2850824 | tf_op jit(solution)/shard_map/ppermute | solution.py:29
  (58 other events, 373.1 us)

commit v2 on v0

v2 whole, which is shorter than its diff:
```python
import functools

import jax
import jax.numpy as jnp
from jax import lax
from jax.experimental import pallas as pl
from jax.experimental.pallas import tpu as pltpu
from jax.sharding import Mesh
from jax.sharding import PartitionSpec as P

BF = jnp.bfloat16
F32 = jnp.float32
SIDE = 4
PLAIN = (((1,), (0,)), ((), ()))
FIRST = (((0,), (0,)), ((), ()))
LAST = (((1,), (1,)), ((), ()))

STREAMS = (
    (("y", 1), ("y", 3), ("z", 1), ("z", 3)),
    (("y", 3), ("y", 1), ("z", 3), ("z", 1)),
    (("z", 1), ("z", 3), ("y", 1), ("y", 3)),
    (("z", 3), ("z", 1), ("y", 3), ("y", 1)),
)
SPAN = 1536


def swap(values, pairing):
    axis, flip = pairing
    return lax.ppermute(values, axis, [(i, i ^ flip) for i in range(SIDE)])


def wide(values):
    return values.astype(F32)


def dot(a, b, dims=PLAIN):
    return lax.dot_general(a, b, dims, preferred_element_type=F32)


def split_parts(values):
    upper = values.astype(BF)
    return upper, (values - wide(upper)).astype(BF)


def round_bf(values):
    return lax.reduce_precision(values, exponent_bits=8, mantissa_bits=7).astype(BF)


def limits(flops, bytes_accessed):
    return dict(
        compiler_params=pltpu.CompilerParams(vmem_limit_bytes=56 << 20),
        cost_estimate=pl.CostEstimate(
            flops=flops, bytes_accessed=bytes_accessed, transcendentals=0
        ),
    )


def forward_kernel(at, lengths, owners, tokens, maps, frozen, up, grad, *rest):
    n = len(STREAMS)
    outs = [rest[3 * s : 3 * s + 3] for s in range(n)]
    hot3, slots, low, hot, total = rest[3 * n :]
    j = pl.program_id(0)
    rows = tokens.shape[0]
    block = rows // SIDE

    @pl.when(j == 0)
    def _():
        flat = slots.shape[1]
        first = at[0] * rows
        down = first + lax.broadcasted_iota(jnp.int32, slots.shape, 0)
        along = first + lax.broadcasted_iota(jnp.int32, hot.shape, 1)
        by_row, by_col = jnp.zeros_like(down), jnp.zeros_like(along)
        begin = jnp.int32(0)
        for tenant in range(lengths.shape[0]):
            by_row = jnp.where(down >= begin, owners[tenant], by_row)
            by_col = jnp.where(along >= begin, owners[tenant], by_col)
            begin = begin + lengths[tenant]
        column = lax.broadcasted_iota(jnp.int32, slots.shape, 1)
        held = jnp.where(by_row == column // (flat // at[1]), 1.0, 0.0)
        slots[...] = held.astype(BF)
        same = by_row[:, : hot3.shape[1]] == column[:, : hot3.shape[1]] % hot.shape[0]
        hot3[...] = jnp.where(same, 1.0, 0.0).astype(BF)
        same = by_col == lax.broadcasted_iota(jnp.int32, hot.shape, 0)
        hot[...] = jnp.where(same, 1.0, 0.0).astype(BF)
        low[...] = (dot(tokens[...], maps[...]) * held).astype(BF)

    total[...] = dot(tokens[...], frozen[...]) + dot(low[...], up[...])
    mag = dot(hot[...], (total[...] * wide(grad[...])).astype(BF)).astype(BF)
    tall = mag.shape[0]

    for s in range(n):

        @pl.when(j == s)
        def _(s=s):
            away, high, near = outs[s]
            away[block : block + tall, :] = mag
            high[:tall, :] = mag
            near[block:, :] = mag
            places = ((away, 0), (away, block + tall), (near, 0), (high, tall))
            for slot, (ref, first) in enumerate(places):
                spot = pl.multiple_of(at[3 + SIDE * s + slot] * block, block)
                ref[first : first + block, :] = total[pl.ds(spot, block), :].astype(BF)


def forward(at, lengths, owners, tokens, maps, frozen, up, grad):
    rows, depth = tokens.shape
    flat, cols = up.shape
    block = rows // SIDE
    width = cols // len(STREAMS)
    tall = 16

    def whole(shape):
        return pl.BlockSpec(shape, lambda j, *_: (0, 0))

    def moving(height):
        return pl.BlockSpec((height, width), lambda j, *_: (0, j))

    heights = (2 * block + tall, block + tall, block + tall) * len(STREAMS)
    shapes = [(height, width) for height in heights] + [(rows, 3 * tall), (rows, flat)]
    found = pl.pallas_call(
        forward_kernel,
        grid_spec=pltpu.PrefetchScalarGridSpec(
            num_scalar_prefetch=3,
            grid=(len(STREAMS),),
            in_specs=[
                whole((rows, depth)),
                whole((depth, flat)),
                moving(depth),
                moving(flat),
                moving(rows),
            ],
            out_specs=[whole(shape) for shape in shapes],
            scratch_shapes=[
                pltpu.VMEM((rows, flat), BF),
                pltpu.VMEM((tall, rows), BF),
                pltpu.VMEM((rows, width), F32),
            ],
        ),
        out_shape=[jax.ShapeDtypeStruct(shape, BF) for shape in shapes],
        name="forward",
        **limits(2 * rows * (depth + 2 * flat) * cols, 2 * cols * (depth + 2 * rows)),
    )(at, lengths, owners, tokens, maps, frozen, up, grad)
    return [found[3 * s : 3 * s + 3] for s in range(len(STREAMS))], found[-2], found[-1]


def squares_kernel(adapters, tokens, maps, slots, frozen, up, small, left, gram):
    j = pl.program_id(0)
    rows = tokens.shape[0]
    flat = up.shape[0]
    rank = flat // adapters
    pieces = frozen.shape[1] // flat
    size = pieces * adapters

    @pl.when(j == 0)
    def _():
        down = maps[...]
        left[...] = wide(down).T.astype(BF)
        small[:rows, :] = (dot(tokens[...], down) * wide(slots[...])).astype(BF)
        products = dot(left[...], down)
        by_row = lax.broadcasted_iota(jnp.int32, (flat, flat), 0) // rank
        by_col = lax.broadcasted_iota(jnp.int32, (flat, flat), 1) // rank
        upper, lower = split_parts(jnp.where(by_row == by_col, products, 0.0))
        gram[:flat, :] = upper
        gram[flat:, :] = lower

    weights, outer = frozen[...], up[...]
    gram_up = dot(gram[...], outer)
    terms = wide(outer) * (2.0 * dot(left[...], weights) + gram_up[:flat] + gram_up[flat:])
    value = jnp.sum(jnp.square(wide(weights)), axis=0, keepdims=True)
    value = value + jnp.sum(terms.reshape(adapters, rank, -1), axis=1)
    value = jnp.concatenate([value[:, i * flat : (i + 1) * flat] for i in range(pieces)], axis=0)
    small[pl.ds(pl.multiple_of(rows + j * size, 16), size), :] = value.astype(BF)


def column_squares(tokens, maps, slots, frozen, up, adapters):
    rows, depth = tokens.shape
    flat, cols = up.shape

    def whole(values):
        return pl.BlockSpec(values.shape, lambda j: (0, 0))

    def moving(height):
        return pl.BlockSpec((height, SPAN), lambda j: (0, j))

    shape = (rows + cols * adapters // flat, flat)
    return pl.pallas_call(
        functools.partial(squares_kernel, adapters),
        grid=(cols // SPAN,),
        in_specs=[whole(tokens), whole(maps), whole(slots), moving(depth), moving(flat)],
        out_specs=pl.BlockSpec(shape, lambda j: (0, 0)),
        out_shape=jax.ShapeDtypeStruct(shape, BF),
        scratch_shapes=[pltpu.VMEM((flat, depth), BF), pltpu.VMEM((2 * flat, flat), BF)],
        name="squares",
        **limits(2 * flat * depth * cols, 2 * cols * depth),
    )(tokens, maps, slots, frozen, up)


def place(at, parts, height, out_shape, onto=None, after=()):
    flat = [values for part in parts for values in part]
    count = len(flat) // len(STREAMS)

    def kernel(at, *refs):
        out, sems = refs[-2:]
        width = out.shape[1] // len(STREAMS)
        copies = []
        for s in range(len(STREAMS)):
            for values in refs[s * count : (s + 1) * count]:
                for first in range(0, values.shape[0], height):
                    spot = pl.multiple_of(at[len(copies)] * height, height)
                    copies.append(
                        pltpu.make_async_copy(
                            values.at[pl.ds(first, height), :],
                            out.at[pl.ds(spot, height), pl.ds(s * width, width)],
                            sems.at[len(copies)],
                        )
                    )
        for copy in copies:
            copy.start()
        for copy in copies:
            copy.wait()

    anywhere = pl.BlockSpec(memory_space=pl.ANY)
    more = list(after) + ([onto] if onto is not None else [])
    return pl.pallas_call(
        kernel,
        in_specs=[pl.BlockSpec(memory_space=pltpu.SMEM)]
        + [pl.BlockSpec(memory_space=pltpu.VMEM)] * len(flat)
        + [anywhere] * len(more),
        out_specs=anywhere,
        out_shape=out_shape,
        scratch_shapes=[pltpu.SemaphoreType.DMA((2 * len(STREAMS),))],
        input_output_aliases={1 + len(flat) + len(after): 0} if onto is not None else {},
        compiler_params=pltpu.CompilerParams(vmem_limit_bytes=12 << 20),
        name="place",
    )(at, *flat, *more)


def table_kernel(rows, mine, got, magnitude, table, norm, down):
    adapters, cols = magnitude.shape
    flat = mine.shape[1]
    total = wide(mine[...]) + wide(got[...])
    down[...] = total[:rows].astype(BF)
    for i in range(cols // flat):
        first = i * flat
        here = jnp.sqrt(total[rows + i * adapters : rows + (i + 1) * adapters] + 1e-06)
        norm[:, first : first + flat] = here
        scale = magnitude[:, first : first + flat] / here
        for part in range(3):
            taken = wide(scale.astype(BF))
            scale = scale - taken
            padded = jnp.concatenate([taken, jnp.zeros_like(taken)], axis=0)
            table[16 * part : 16 * part + 16, first : first + flat] = padded.astype(BF)


def grad_up_kernel(at, grad, table, hot, down, out):
    scaled = (wide(grad[...]) * dot(hot[...], table[...])).astype(BF)
    out[...] = dot(down[...], scaled, FIRST)


def grad_up_part(at, grad, table, hot, down, share):
    flat = down.shape[1]

    def mine(values):
        return pl.BlockSpec((values.shape[0], share), lambda j, at: (0, at[2]))

    def whole(values):
        return pl.BlockSpec(values.shape, lambda j, at: (0, 0))

    return pl.pallas_call(
        grad_up_kernel,
        grid_spec=pltpu.PrefetchScalarGridSpec(
            num_scalar_prefetch=1,
            grid=(1,),
            in_specs=[mine(grad), mine(table), whole(hot), whole(down)],
            out_specs=pl.BlockSpec((flat, share), lambda j, at: (0, 0)),
        ),
        out_shape=jax.ShapeDtypeStruct((flat, share), F32),
        name="grad_up",
        **limits(0, 3 * grad.shape[0] * share),
    )(at, grad, table, hot, down)


def backward_kernel(grad, table, hot, frozen, up, slots, tokens, maps, sent, back, total):
    j = pl.program_id(0)
    rows = hot.shape[0]

    @pl.when(j == 0)
    def _():
        back[...] = jnp.zeros_like(back)
        total[...] = jnp.zeros_like(total)

    scaled = (wide(grad[...]) * dot(hot[...], table[...])).astype(BF)
    back[...] += dot(scaled, up[...], LAST)
    total[...] += dot(scaled, frozen[...], LAST)

    @pl.when(j == pl.num_programs(0) - 1)
    def _():
        upper, lower = split_parts(back[...] * wide(slots[...]))
        down_maps = maps[...]
        full = total[...] + dot(upper, down_maps, LAST) + dot(lower, down_maps, LAST)
        sent[:rows, :] = full.astype(BF)
        values = tokens[...]
        sent[rows:, :] = (dot(upper, values, FIRST) + dot(lower, values, FIRST)).astype(BF)


def backward(grad, table, hot, frozen, up, slots, tokens, maps):
    rows, depth = tokens.shape
    flat, cols = up.shape

    def whole(values):
        return pl.BlockSpec(values.shape, lambda j: (0, 0))

    def moving(height):
        return pl.BlockSpec((height, SPAN), lambda j: (0, j))

    return pl.pallas_call(
        backward_kernel,
        grid=(cols // SPAN,),
        in_specs=[
            moving(rows),
            moving(table.shape[0]),
            whole(hot),
            moving(depth),
            moving(flat),
            whole(slots),
            whole(tokens),
            whole(maps),
        ],
        out_specs=pl.BlockSpec((rows + flat, depth), lambda j: (0, 0)),
        out_shape=jax.ShapeDtypeStruct((rows + flat, depth), BF),
        scratch_shapes=[pltpu.VMEM((rows, flat), F32), pltpu.VMEM((rows, depth), F32)],
        name="backward",
        **limits(2 * rows * (depth + 2 * flat) * cols, 2 * cols * (depth + rows)),
    )(grad, table, hot, frozen, up, slots, tokens, maps)


def on_device(
    tokens, frozen, adapter_down, adapter_up, magnitude, grad_out, tenant_lengths, tenant_adapter
):
    tok_rows, depth = tokens.shape
    adapters, cols = magnitude.shape
    flat = adapter_down.shape[1]
    block = tok_rows // SIDE
    width = cols // len(STREAMS)
    spot = {axis: lax.axis_index(axis) for axis in ("dp", "z", "y")}

    spots = [spot["dp"], jnp.int32(adapters), spot["z"] * SIDE + spot["y"]]
    early, late = [], []
    for one, two, _, _ in STREAMS:
        me = spot[one[0]]
        there = me ^ one[1]
        spots += [there, there ^ two[1], me, me ^ two[1]]
        early += [me, there]
        late += [me ^ two[1], there ^ two[1]]
    at, early, late = (jnp.stack(v).astype(jnp.int32) for v in (spots, early, late))
    streams, hot3, slots = forward(
        at, tenant_lengths, tenant_adapter, tokens, adapter_down, frozen, adapter_up, grad_out
    )
    small = column_squares(tokens, adapter_down, slots, frozen, adapter_up, adapters)

    def exchange(values, step):
        return [swap(v, order[step]) for v, order in zip(values, STREAMS, strict=True)]

    first = exchange([away for away, _, _ in streams], 0)
    for step, pairing in enumerate((("y", 1), ("z", 1), ("y", 3), ("z", 3))):
        if step == 0:
            small, _ = lax.optimization_barrier((small, first))
        got = swap(small, pairing)
        if step < 3:
            small = round_bf(wide(small) + wide(got))
    table, col_norm, down = pl.pallas_call(
        functools.partial(table_kernel, tok_rows),
        out_shape=[
            jax.ShapeDtypeStruct((48, cols), BF),
            jax.ShapeDtypeStruct((adapters, cols), F32),
            jax.ShapeDtypeStruct((tok_rows, flat), BF),
        ],
        name="table",
        compiler_params=pltpu.CompilerParams(vmem_limit_bytes=12 << 20),
    )(small, got, magnitude)

    tall = hot3.shape[1] // 3
    sums = [
        round_bf(wide(high) + wide(got[block:]))
        for (_, high, _), got in zip(streams, first, strict=True)
    ]
    second = exchange(sums, 1)
    sums = [
        round_bf(
            jnp.concatenate(
                [
                    wide(near[:block]) + wide(got[:block]) + wide(more[tall:]),
                    wide(summed[:tall]) + wide(more[:tall]),
                ],
                axis=0,
            )
        )
        for (_, _, near), got, summed, more in zip(streams, first, sums, second, strict=True)
    ]
    got = exchange(sums, 2)
    sums = [round_bf(wide(a) + wide(b)) for a, b in zip(sums, got, strict=True)]
    got = exchange(sums, 3)
    done, mags = [], []
    for s, (a, b) in enumerate(zip(sums, got, strict=True)):
        me = spot[STREAMS[s][0][0]]
        rows = lax.dynamic_slice_in_dim(hot3, me * block, block, 0)
        scale = dot(rows, table[:, s * width : (s + 1) * width])
        done.append((scale * (wide(a[:block]) + wide(b[:block]))).astype(BF))
        mags.append(wide(a[block : block + adapters]) + wide(b[block : block + adapters]))
    near = exchange(done, 0)
    sent = backward(grad_out, table, hot3, frozen, adapter_up, slots, tokens, adapter_down)
    near, sent = lax.optimization_barrier((near, sent))
    pairs = [jnp.concatenate(both, axis=0) for both in zip(done, near, strict=True)]
    far = exchange(pairs, 1)
    mag = jnp.concatenate(mags, axis=1)
    for flip in (1, 3):
        mag = mag + swap(mag, ("dp", flip))

    grad_up = grad_up_part(at, grad_out, table, hot3, down, cols // SIDE**2)
    for flip in (1, 3):
        grad_up = grad_up + swap(grad_up, ("dp", flip))
    grad_up = lax.all_gather(round_bf(grad_up), ("z", "y"), axis=1, tiled=True).astype(F32)
    total = wide(sent) + wide(lax.ppermute(sent, "col", [(0, 1), (1, 0)]))
    input_grad = total[:tok_rows].astype(BF)
    grad_down = total[tok_rows:]
    for flip in (1, 3):
        share = round_bf(grad_down)
        grad_down = wide(share) + wide(swap(share, ("dp", flip)))
    whole = jax.ShapeDtypeStruct((tok_rows, cols), BF)
    adapted = place(early, list(zip(done, near, strict=True)), block, whole)
    adapted = place(late, [[v] for v in far], block, whole, onto=adapted, after=(grad_up,))
    return (adapted, input_grad, grad_down.T, grad_up, mag / col_norm)


def solution(mesh):
    assert mesh.axis_names == ("dp", "row", "col")
    grid = Mesh(mesh.devices.reshape(SIDE, SIDE, SIDE, 2), ("dp", "z", "y", "col"))
    row = ("z", "y")
    placed = (
        P("dp", row),
        P(row, "col"),
        P(row, None),
        P(None, "col"),
        P(None, "col"),
        P("dp", "col"),
        P(),
        P(),
    )
    return jax.shard_map(
        on_device,
        mesh=grid,
        in_specs=placed,
        out_specs=(P("dp", "col"), P("dp", row), P(row, None), P(None, "col"), P(None, "col")),
        check_vma=False,
    )
```

time: 541 us -> 188 us (0.35)
  waiting for transfers between devices: 345 us -> 52 us
  matrix products: 86.7 us -> 0.98 us
  blocking collectives: 78.6 us -> 0 us
  starting transfers between devices: 0.16 us -> 52.9 us
  Pallas kernels: 0 us -> 51.3 us
    psum x4 -> x0, waiting for transfers between devices: 345 us -> none  [the longest x1 134 us: on_device(): lax.psum((wide_left(picked_down, picked_grad, contract_first), mag_part),...]
    dot_general x18 -> x4, matrix products: 86.7 us -> 0.98 us  [dot(): return lax.dot_general(a, b, dims, preferred_element_type=F32)]
    psum x1 -> x0, blocking collectives: 78.6 us -> none  [on_device(): lax.psum((squares_part, cross_part, gram_part), 'row')]
    ppermute x0 -> x35, starting transfers between devices: none -> 52.8 us  [the longest x34 52.8 us: swap(): return lax.ppermute(values, axis, [(i, i ^ flip) for i in range(SIDE)])]
    pallas_call x0 -> x7, Pallas kernels: none -> 51.3 us  [the longest x1 17.9 us: forward(): pl.pallas_call(forward_kernel, grid_spec=pltpu.PrefetchScalarGridSpec(num...]
    ppermute x0 -> x35, waiting for transfers between devices: none -> 38 us  [the longest x34 38 us: swap(): return lax.ppermute(values, axis, [(i, i ^ flip) for i in range(SIDE)])]
    all_gather x0 -> x1, waiting for transfers between devices: none -> 14 us  [on_device(): lax.all_gather(round_bf(grad_up), ('z', 'y'), axis=1, tiled=True)]
    reduce_sum x3 -> x0, other arithmetic: 6.62 us -> none  [the longest x1 6.44 us: on_device(): squares_part = jnp.sum(jnp.square(frozen.astype(jnp.float32)), axis=0)]
  transfers between devices with their start and end apart: 4 -> 36, of which waited for: 4 -> 12; matrix products, arithmetic and copies ran while one was open for 5% -> 7% of each run, Pallas kernels for 0% -> 15%
where the time goes in v2:
time: 188 us; the launch traced here: 187 us
  starting transfers between devices  52.9 us (28%)
  waiting for transfers between devices  52 us (28%)
  Pallas kernels  51.3 us (27%)
  between operations  14.5 us (8%)
  other arithmetic  9.82 us (5%)
  local copies, waits for them, and re-layouts  5.42 us (3%)
    ppermute x34, starting transfers between devices, swap(): return lax.ppermute(values, axis, [(i, i ^ flip) for i in range(SIDE)])  52.8 us
    ppermute x34, waiting for transfers between devices, swap(): return lax.ppermute(values, axis, [(i, i ^ flip) for i in range(SIDE)])  38 us
    pallas_call x1, Pallas kernels, forward(): pl.pallas_call(forward_kernel, grid_spec=pltpu.PrefetchScalarGridSpec(num...  17.9 us
    pallas_call x1, Pallas kernels, backward(): pl.pallas_call(backward_kernel, grid=(cols // SPAN,), in_specs=[moving(ro...  15.4 us
    all_gather x1, waiting for transfers between devices, on_device(): lax.all_gather(round_bf(grad_up), ('z', 'y'), axis=1, tiled=True)  14 us
    pallas_call x1, Pallas kernels, column_squares(): pl.pallas_call(functools.partial(squares_kernel, adapters), grid=(cols //...  8.14 us
    pallas_call x2, Pallas kernels, place(): pl.pallas_call(kernel, in_specs=[pl.BlockSpec(memory_space=pltpu.SMEM)] +...  6.7 us
  transfers between devices with their start and end apart: 36, of which 12 were waited for; matrix products, arithmetic and copies ran while one was open for 7% of the time, Pallas kernels for 15%

profile of v2, /device:TPU:0, one launch (start us, length us, event | category | flops | bytes accessed | tf_op | source)
XLA Modules:
  0.0 186.9 jit_solution(10254904166503302184)
XLA Ops:
  7.9 17.9 %forward.1 = (bf16[272,1536]{1,0:T(8,128)(2,1)}, bf16[144,1536]{1,0:T(8,128)(2,1)}, bf16[144,1536]{1,0:T(8,128)(2,1)}, bf16[272,1536]{1,0:T(8,128)(2,1)}, bf16[1...) custom-call(s32[19]{0:T(128)} %stack.80.at, ...), custom_call_target="tpu_custom_call" | custom-call | flops 7247757312 | bytes 23592960 | tf_op jit(solution)/shard_map/forward/pallas_call | solution.py:120
  27.6 2.2 %collective-permute-start.1 = (bf16[272,1536]{1,0:T(8,128)(2,1)}, bf16[272,1536]{1,0:T(8,128)(2,1)S(1)}, u32[]{:S(2)}, u32[]{:S(2)}) collective-permute-start(bf16[272,1536]{1,0:T(8,128)(2,1)} %get-tuple-element.31), channel_id=1, source_target_pairs={{0,6},{2,4},{4,2},{6,0},{1,7},{3,5},{5,3},{7,1},{8,14},{10,12},{12... | collective-permute-start | bytes 2506760 | tf_op jit(solution)/shard_map/ppermute | solution.py:29
  31.7 2.5 %collective-permute-start.3 = (bf16[272,1536]{1,0:T(8,128)(2,1)}, bf16[272,1536]{1,0:T(8,128)(2,1)S(1)}, u32[]{:S(2)}, u32[]{:S(2)}) collective-permute-start(bf16[272,1536]{1,0:T(8,128)(2,1)} %get-tuple-element.33), channel_id=1, source_target_pairs={{0,24},{8,16},{16,8},{24,0},{1,25},{9,17},{17,9},{25,1},{2,26},{10... | collective-permute-start | bytes 2506760 | tf_op jit(solution)/shard_map/ppermute | solution.py:29
  34.4 8.1 %squares.1 = bf16[896,128]{1,0:T(8,128)(2,1)} custom-call(bf16[512,896]{1,0:T(8,128)(2,1)} %tokens.5, bf16[896,128]{1,0:T(8,128)(2,1)} %maps.5, bf16[512,128]{1,0:T(8,128)(2,1)} %get-tuple-element.29.slots, bf16[896,6144]{1,0:T(8,128)(2,1)} %frozen.5, bf16[128,6144]{1,0:T(8,128)(2,1)} %up.5), custom_call_target="tpu_custom_call" | custom-call | flops 1409286144 | bytes 11010048 | tf_op jit(solution)/shard_map/squares/pallas_call | solution.py:186
  42.5 3.9 %collective-permute-done = bf16[272,1536]{1,0:T(8,128)(2,1)S(1)} collective-permute-done((bf16[272,1536]{1,0:T(8,128)(2,1)}, bf16[272,1536]{1,0:T(8,128)(2,1)S(1)}, u32[]{:S(2)}, u32[]{:S(2)}) %collective-permute-start) | collective-permute-done | bytes 835616 | tf_op jit(solution)/shard_map/ppermute | solution.py:29
  46.5 3.3 %collective-permute-start.8 = (bf16[144,1536]{1,0:T(8,128)(2,1)S(1)}, bf16[144,1536]{1,0:T(8,128)(2,1)S(1)}, u32[]{:S(2)}, u32[]{:S(2)}) collective-permute-start(bf16[144,1536]{1,0:T(8,128)(2,1)S(1)} %reduce-precision_convert_fusion.7), channel_id=1, source_target_pairs={{0,6},{2,4},{4,2},{6,0},{1,7},{3,5},{5,3},{7,1},{8,14},{10,12},{12... | collective-permute-start | bytes 1327112 | tf_op jit(solution)/shard_map/ppermute | solution.py:29
  50.2 4.1 %collective-permute-start.16 = (bf16[144,1536]{1,0:T(8,128)(2,1)S(1)}, bf16[144,1536]{1,0:T(8,128)(2,1)S(1)}, u32[]{:S(2)}, u32[]{:S(2)}) collective-permute-start(bf16[144,1536]{1,0:T(8,128)(2,1)S(1)} %reduce-precision_convert_fusion.3), channel_id=1, source_target_pairs={{0,24},{8,16},{16,8},{24,0},{1,25},{9,17},{17,9},{25,1},{2,26},{10... | collective-permute-start | bytes 1327112 | tf_op jit(solution)/shard_map/ppermute | solution.py:29
  56.4 9.2 %collective-permute-done.4 = bf16[896,128]{1,0:T(8,128)(2,1)S(1)} collective-permute-done((bf16[896,128]{1,0:T(8,128)(2,1)S(1)}, bf16[896,128]{1,0:T(8,128)(2,1)S(1)}, u32[]{:S(2)}, u32[]{:S(2)}) %collective-permute-start.4) | collective-permute-done | bytes 229408 | tf_op jit(solution)/shard_map/ppermute | solution.py:29
  65.7 2.0 %collective-permute-start.5 = (bf16[896,128]{1,0:T(8,128)(2,1)S(1)}, bf16[896,128]{1,0:T(8,128)(2,1)S(1)}, u32[]{:S(2)}, u32[]{:S(2)}) collective-permute-start(bf16[896,128]{1,0:T(8,128)(2,1)S(1)} %reduce-precision_convert_fusion.11), channel_id=1, source_target_pairs={{0,8},{8,0},{16,24},{24,16},{1,9},{9,1},{17,25},{25,17},{2,10},{10... | collective-permute-start | bytes 688136 | tf_op jit(solution)/shard_map/ppermute | solution.py:29
  68.9 3.5 %collective-permute-start.13 = (bf16[144,1536]{1,0:T(8,128)(2,1)S(1)}, bf16[144,1536]{1,0:T(8,128)(2,1)S(1)}, u32[]{:S(2)}, u32[]{:S(2)}) collective-permute-start(bf16[144,1536]{1,0:T(8,128)(2,1)S(1)} %fusion.5), channel_id=1, source_target_pairs={{0,24},{8,16},{16,8},{24,0},{1,25},{9,17},{17,9},{25,1},{2,26},{10... | collective-permute-start | bytes 1327112 | tf_op jit(solution)/shard_map/ppermute | solution.py:29
  77.8 6.3 %collective-permute-done.6 = bf16[896,128]{1,0:T(8,128)(2,1)S(1)} collective-permute-done((bf16[896,128]{1,0:T(8,128)(2,1)S(1)}, bf16[896,128]{1,0:T(8,128)(2,1)S(1)}, u32[]{:S(2)}, u32[]{:S(2)}) %collective-permute-start.6) | collective-permute-done | bytes 229408 | tf_op jit(solution)/shard_map/ppermute | solution.py:29
  84.2 2.0 %collective-permute-start.7 = (bf16[896,128]{1,0:T(8,128)(2,1)S(1)}, bf16[896,128]{1,0:T(8,128)(2,1)S(1)}, u32[]{:S(2)}, u32[]{:S(2)}) collective-permute-start(bf16[896,128]{1,0:T(8,128)(2,1)S(1)} %reduce-precision_convert_fusion.9.mine), channel_id=1, source_target_pairs={{0,24},{8,16},{16,8},{24,0},{1,25},{9,17},{17,9},{25,1},{2,26},{10... | collective-permute-start | bytes 688136 | tf_op jit(solution)/shard_map/ppermute | solution.py:29
  89.5 2.7 %collective-permute-done.21 = bf16[144,1536]{1,0:T(8,128)(2,1)S(1)} collective-permute-done((bf16[144,1536]{1,0:T(8,128)(2,1)S(1)}, bf16[144,1536]{1,0:T(8,128)(2,1)S(1)}, u32[]{:S(2)}, u32[]{:S(2)}) %collective-permute-start.21) | collective-permute-done | bytes 442400 | tf_op jit(solution)/shard_map/ppermute | solution.py:29
  94.5 2.9 %grad_up.1 = f32[128,384]{1,0:T(8,128)} custom-call(s32[19]{0:T(128)} %stack.80.at, bf16[512,6144]{1,0:T(8,128)(2,1)} %grad.5, bf16[48,6144]{1,0:T(8,128)(2,1)} %copy-done.1, bf16[512,48]{1,0:T(8,128)(2,1)} %get-tuple-element.28.hot, bf16[512,128]{1,0:T(8,128)(2,1)} %copy-done.4), custom_call_target="tpu_custom_call" | custom-call | bytes 589824 | tf_op jit(solution)/shard_map/grad_up/pallas_call | solution.py:269
  99.0 15.4 %backward.1 = bf16[640,896]{1,0:T(8,128)(2,1)} custom-call(bf16[512,6144]{1,0:T(8,128)(2,1)} %grad.5, bf16[48,6144]{1,0:T(8,128)(2,1)} %copy-done.1, bf16[512,48]{1,0:T(8,128)(2,1)} %get-tuple-element.28.hot, bf16[896,6144]{1,0:T(8,128)(2,1)} %frozen.5, bf16[128,6144]{1,0:T(8,128)(2,1)} %up.5, bf16[512,128]{1,0:T(8,128)(2,1)} %get-tuple-element.29.slots, ...), custom_call_target="tpu_custom_call" | custom-call | flops 7247757312 | bytes 17301504 | tf_op jit(solution)/shard_map/backward/pallas_call | solution.py:316
  114.4 3.4 %collective-permute-start.29 = (f32[128,384]{1,0:T(8,128)S(1)}, f32[128,384]{1,0:T(8,128)S(1)}, u32[]{:S(2)}, u32[]{:S(2)}) collective-permute-start(f32[128,384]{1,0:T(8,128)S(1)} %add.155), channel_id=1, source_target_pairs={{0,96},{32,64},{64,32},{96,0},{1,97},{33,65},{65,33},{97,1},{2,98}... | collective-permute-start | bytes 589832 | tf_op jit(solution)/shard_map/ppermute | solution.py:29
  122.3 3.2 %collective-permute-start.23 = (bf16[128,1536]{1,0:T(8,128)(2,1)S(1)}, bf16[128,1536]{1,0:T(8,128)(2,1)S(1)}, u32[]{:S(2)}, u32[]{:S(2)}) collective-permute-start(bf16[128,1536]{1,0:T(8,128)(2,1)S(1)} %fusion.3.refs_6_), channel_id=1, source_target_pairs={{0,24},{8,16},{16,8},{24,0},{1,25},{9,17},{17,9},{25,1},{2,26},{10... | collective-permute-start | bytes 1179656 | tf_op jit(solution)/shard_map/ppermute | solution.py:29
  126.9 2.3 %collective-permute-done.15.refs_3_ = bf16[128,1536]{1,0:T(8,128)(2,1)S(1)} collective-permute-done((bf16[128,1536]{1,0:T(8,128)(2,1)S(1)}, bf16[128,1536]{1,0:T(8,128)(2,1)S(1)}, u32[]{:S(2)}, u32[]{:S(2)}) %collective-permute-start.15) | collective-permute-done | bytes 393248 | tf_op jit(solution)/shard_map/ppermute | solution.py:29
  139.4 2.3 %place.2.refs_5_ = bf16[512,6144]{1,0:T(8,128)(2,1)} custom-call(s32[8]{0:T(128)S(1)} %stack.81.at, bf16[128,1536]{1,0:T(8,128)(2,1)S(1)} %fusion.refs_0_, bf16[128,1536]{1,0:T(8,128)(2,1)S(1)} %collective-permute-done.11.refs_1_, bf16[128,1536]{1,0:T(8,128)(2,1)S(1)} %fusion.1.refs_2_, bf16[128,1536]{1,0:T(8,128)(2,1)S(1)} %collective-permute-done.15.refs_3_, ...), custom_call_target="tpu_custom_call" | custom-call | tf_op jit(solution)/shard_map/place/pallas_call | solution.py:224
  142.2 7.0 %collective-permute-done.31 = bf16[128,896]{1,0:T(8,128)(2,1)S(1)} collective-permute-done((bf16[128,896]{1,0:T(8,128)(2,1)S(1)}, bf16[128,896]{1,0:T(8,128)(2,1)S(1)}, u32[]{:S(2)}, u32[]{:S(2)}) %collective-permute-start.31) | collective-permute-done | bytes 229408 | tf_op jit(solution)/shard_map/ppermute | solution.py:29
  151.1 3.0 %collective-permute-start.32 = (bf16[128,896]{1,0:T(8,128)(2,1)S(1)}, bf16[128,896]{1,0:T(8,128)(2,1)S(1)}, u32[]{:S(2)}, u32[]{:S(2)}) collective-permute-start(bf16[128,896]{1,0:T(8,128)(2,1)S(1)} %reduce-precision_convert_fusion.8), channel_id=1, source_target_pairs={{0,96},{32,64},{64,32},{96,0},{1,97},{33,65},{65,33},{97,1},{2,98}... | collective-permute-start | bytes 688136 | tf_op jit(solution)/shard_map/ppermute | solution.py:29
  155.9 2.9 %collective-permute-done.32 = bf16[128,896]{1,0:T(8,128)(2,1)S(1)} collective-permute-done((bf16[128,896]{1,0:T(8,128)(2,1)S(1)}, bf16[128,896]{1,0:T(8,128)(2,1)S(1)}, u32[]{:S(2)}, u32[]{:S(2)}) %collective-permute-start.32) | collective-permute-done | bytes 229408 | tf_op jit(solution)/shard_map/ppermute | solution.py:29
  159.8 14.0 %all-gather.2.cloned.1.call-done = bf16[128,6144]{1,0:T(8,128)(2,1)} async-done(((bf16[128,384]{1,0:T(8,128)(2,1)}), bf16[128,6144]{1,0:T(8,128)(2,1)}) %all-gather.2.cloned.1.call-update) | async-done | bytes 1572880 | tf_op jit(solution)/shard_map/all_gather | solution.py:422
  175.6 4.4 %place.3 = bf16[512,6144]{1,0:T(8,128)(2,1)} custom-call(s32[8]{0:T(128)S(1)} %stack.75.at, bf16[256,1536]{1,0:T(8,128)(2,1)S(1)} %collective-permute-done.24.refs_0_, bf16[256,1536]{1,0:T(8,128)(2,1)} %collective-permute-done.25.refs_1_, bf16[256,1536]{1,0:T(8,128)(2,1)} %collective-permute-done.26.refs_2_, ...), custom_call_target="tpu_custom_call", output_to_operand_aliasing={{}: (6, {})} | custom-call | tf_op jit(solution)/shard_map/place/pallas_call | solution.py:224
  (140 shorter events, 43.9 us)
Async XLA Ops:
  7.2 166.6 %all-gather.2.cloned.1.call-start = ((), (), s32[]{:S(2)}) async-start(), calls=%async_computation | async-start | bytes 1671168 | tf_op jit(solution)/shard_map/all_gather | solution.py:422
  25.9 20.5 %collective-permute-start = (bf16[272,1536]{1,0:T(8,128)(2,1)}, bf16[272,1536]{1,0:T(8,128)(2,1)S(1)}, u32[]{:S(2)}, u32[]{:S(2)}) collective-permute-start(bf16[272,1536]{1,0:T(8,128)(2,1)} %get-tuple-element.30), channel_id=1, source_target_pairs={{0,2},{2,0},{4,6},{6,4},{1,3},{3,1},{5,7},{7,5},{8,10},{10,8},{12,... | collective-permute-start | bytes 2506760 | tf_op jit(solution)/shard_map/ppermute | solution.py:29
  27.6 22.2 %collective-permute-start.1 = (bf16[272,1536]{1,0:T(8,128)(2,1)}, bf16[272,1536]{1,0:T(8,128)(2,1)S(1)}, u32[]{:S(2)}, u32[]{:S(2)}) collective-permute-start(bf16[272,1536]{1,0:T(8,128)(2,1)} %get-tuple-element.31), channel_id=1, source_target_pairs={{0,6},{2,4},{4,2},{6,0},{1,7},{3,5},{5,3},{7,1},{8,14},{10,12},{12... | collective-permute-start | bytes 2506760 | tf_op jit(solution)/shard_map/ppermute | solution.py:29
  29.8 20.3 %collective-permute-start.2 = (bf16[272,1536]{1,0:T(8,128)(2,1)}, bf16[272,1536]{1,0:T(8,128)(2,1)S(1)}, u32[]{:S(2)}, u32[]{:S(2)}) collective-permute-start(bf16[272,1536]{1,0:T(8,128)(2,1)} %get-tuple-element.32), channel_id=1, source_target_pairs={{0,8},{8,0},{16,24},{24,16},{1,9},{9,1},{17,25},{25,17},{2,10},{10... | collective-permute-start | bytes 2506760 | tf_op jit(solution)/shard_map/ppermute | solution.py:29
  31.7 22.7 %collective-permute-start.3 = (bf16[272,1536]{1,0:T(8,128)(2,1)}, bf16[272,1536]{1,0:T(8,128)(2,1)S(1)}, u32[]{:S(2)}, u32[]{:S(2)}) collective-permute-start(bf16[272,1536]{1,0:T(8,128)(2,1)} %get-tuple-element.33), channel_id=1, source_target_pairs={{0,24},{8,16},{16,8},{24,0},{1,25},{9,17},{17,9},{25,1},{2,26},{10... | collective-permute-start | bytes 2506760 | tf_op jit(solution)/shard_map/ppermute | solution.py:29
  46.5 21.2 %collective-permute-start.8 = (bf16[144,1536]{1,0:T(8,128)(2,1)S(1)}, bf16[144,1536]{1,0:T(8,128)(2,1)S(1)}, u32[]{:S(2)}, u32[]{:S(2)}) collective-permute-start(bf16[144,1536]{1,0:T(8,128)(2,1)S(1)} %reduce-precision_convert_fusion.7), channel_id=1, source_target_pairs={{0,6},{2,4},{4,2},{6,0},{1,7},{3,5},{5,3},{7,1},{8,14},{10,12},{12... | collective-permute-start | bytes 1327112 | tf_op jit(solution)/shard_map/ppermute | solution.py:29
  49.9 18.2 %collective-permute-start.12 = (bf16[144,1536]{1,0:T(8,128)(2,1)S(1)}, bf16[144,1536]{1,0:T(8,128)(2,1)S(1)}, u32[]{:S(2)}, u32[]{:S(2)}) collective-permute-start(bf16[144,1536]{1,0:T(8,128)(2,1)S(1)} %reduce-precision_convert_fusion.5), channel_id=1, source_target_pairs={{0,2},{2,0},{4,6},{6,4},{1,3},{3,1},{5,7},{7,5},{8,10},{10,8},{12,... | collective-permute-start | bytes 1327112 | tf_op jit(solution)/shard_map/ppermute | solution.py:29
  50.2 22.2 %collective-permute-start.16 = (bf16[144,1536]{1,0:T(8,128)(2,1)S(1)}, bf16[144,1536]{1,0:T(8,128)(2,1)S(1)}, u32[]{:S(2)}, u32[]{:S(2)}) collective-permute-start(bf16[144,1536]{1,0:T(8,128)(2,1)S(1)} %reduce-precision_convert_fusion.3), channel_id=1, source_target_pairs={{0,24},{8,16},{16,8},{24,0},{1,25},{9,17},{17,9},{25,1},{2,26},{10... | collective-permute-start | bytes 1327112 | tf_op jit(solution)/shard_map/ppermute | solution.py:29
  56.3 16.7 %collective-permute-start.20 = (bf16[144,1536]{1,0:T(8,128)(2,1)S(1)}, bf16[144,1536]{1,0:T(8,128)(2,1)S(1)}, u32[]{:S(2)}, u32[]{:S(2)}) collective-permute-start(bf16[144,1536]{1,0:T(8,128)(2,1)S(1)} %reduce-precision_convert_fusion.1), channel_id=1, source_target_pairs={{0,8},{8,0},{16,24},{24,16},{1,9},{9,1},{17,25},{25,17},{2,10},{10... | collective-permute-start | bytes 1327112 | tf_op jit(solution)/shard_map/ppermute | solution.py:29
  67.9 18.3 %collective-permute-start.9 = (bf16[144,1536]{1,0:T(8,128)(2,1)S(1)}, bf16[144,1536]{1,0:T(8,128)(2,1)S(1)}, u32[]{:S(2)}, u32[]{:S(2)}) collective-permute-start(bf16[144,1536]{1,0:T(8,128)(2,1)S(1)} %fusion.4), channel_id=1, source_target_pairs={{0,8},{8,0},{16,24},{24,16},{1,9},{9,1},{17,25},{25,17},{2,10},{10... | collective-permute-start | bytes 1327112 | tf_op jit(solution)/shard_map/ppermute | solution.py:29
  68.9 18.8 %collective-permute-start.13 = (bf16[144,1536]{1,0:T(8,128)(2,1)S(1)}, bf16[144,1536]{1,0:T(8,128)(2,1)S(1)}, u32[]{:S(2)}, u32[]{:S(2)}) collective-permute-start(bf16[144,1536]{1,0:T(8,128)(2,1)S(1)} %fusion.5), channel_id=1, source_target_pairs={{0,24},{8,16},{16,8},{24,0},{1,25},{9,17},{17,9},{25,1},{2,26},{10... | collective-permute-start | bytes 1327112 | tf_op jit(solution)/shard_map/ppermute | solution.py:29
  72.7 15.3 %collective-permute-start.17 = (bf16[144,1536]{1,0:T(8,128)(2,1)S(1)}, bf16[144,1536]{1,0:T(8,128)(2,1)S(1)}, u32[]{:S(2)}, u32[]{:S(2)}) collective-permute-start(bf16[144,1536]{1,0:T(8,128)(2,1)S(1)} %fusion.6), channel_id=1, source_target_pairs={{0,2},{2,0},{4,6},{6,4},{1,3},{3,1},{5,7},{7,5},{8,10},{10,8},{12,... | collective-permute-start | bytes 1327112 | tf_op jit(solution)/shard_map/ppermute | solution.py:29
  75.9 16.2 %collective-permute-start.21 = (bf16[144,1536]{1,0:T(8,128)(2,1)S(1)}, bf16[144,1536]{1,0:T(8,128)(2,1)S(1)}, u32[]{:S(2)}, u32[]{:S(2)}) collective-permute-start(bf16[144,1536]{1,0:T(8,128)(2,1)S(1)} %fusion.7), channel_id=1, source_target_pairs={{0,6},{2,4},{4,2},{6,0},{1,7},{3,5},{5,3},{7,1},{8,14},{10,12},{12... | collective-permute-start | bytes 1327112 | tf_op jit(solution)/shard_map/ppermute | solution.py:29
  86.3 31.5 %collective-permute-start.10 = (bf16[144,1536]{1,0:T(8,128)(2,1)S(1)}, bf16[144,1536]{1,0:T(8,128)(2,1)S(1)}, u32[]{:S(2)}, u32[]{:S(2)}) collective-permute-start(bf16[144,1536]{1,0:T(8,128)(2,1)S(1)} %reduce-precision_convert_fusion.6), channel_id=1, source_target_pairs={{0,24},{8,16},{16,8},{24,0},{1,25},{9,17},{17,9},{25,1},{2,26},{10... | collective-permute-start | bytes 1327112 | tf_op jit(solution)/shard_map/ppermute | solution.py:29
  87.8 32.1 %collective-permute-start.14 = (bf16[144,1536]{1,0:T(8,128)(2,1)S(1)}, bf16[144,1536]{1,0:T(8,128)(2,1)S(1)}, u32[]{:S(2)}, u32[]{:S(2)}) collective-permute-start(bf16[144,1536]{1,0:T(8,128)(2,1)S(1)} %reduce-precision_convert_fusion.4), channel_id=1, source_target_pairs={{0,8},{8,0},{16,24},{24,16},{1,9},{9,1},{17,25},{25,17},{2,10},{10... | collective-permute-start | bytes 1327112 | tf_op jit(solution)/shard_map/ppermute | solution.py:29
  88.1 33.6 %collective-permute-start.18 = (bf16[144,1536]{1,0:T(8,128)(2,1)S(1)}, bf16[144,1536]{1,0:T(8,128)(2,1)S(1)}, u32[]{:S(2)}, u32[]{:S(2)}) collective-permute-start(bf16[144,1536]{1,0:T(8,128)(2,1)S(1)} %reduce-precision_convert_fusion.2), channel_id=1, source_target_pairs={{0,6},{2,4},{4,2},{6,0},{1,7},{3,5},{5,3},{7,1},{8,14},{10,12},{12... | collective-permute-start | bytes 1327112 | tf_op jit(solution)/shard_map/ppermute | solution.py:29
  92.3 29.7 %collective-permute-start.22 = (bf16[144,1536]{1,0:T(8,128)(2,1)S(1)}, bf16[144,1536]{1,0:T(8,128)(2,1)S(1)}, u32[]{:S(2)}, u32[]{:S(2)}) collective-permute-start(bf16[144,1536]{1,0:T(8,128)(2,1)S(1)} %reduce-precision_convert_fusion), channel_id=1, source_target_pairs={{0,2},{2,0},{4,6},{6,4},{1,3},{3,1},{5,7},{7,5},{8,10},{10,8},{12,... | collective-permute-start | bytes 1327112 | tf_op jit(solution)/shard_map/ppermute | solution.py:29
  97.4 17.0 %collective-permute-start.28 = (f32[128,384]{1,0:T(8,128)}, f32[128,384]{1,0:T(8,128)S(1)}, u32[]{:S(2)}, u32[]{:S(2)}) collective-permute-start(f32[128,384]{1,0:T(8,128)} %grad_up.1), channel_id=1, source_target_pairs={{0,32},{32,0},{64,96},{96,64},{1,33},{33,1},{65,97},{97,65},{2,34}... | collective-permute-start | bytes 589832 | tf_op jit(solution)/shard_map/ppermute | solution.py:29
  114.4 11.8 %collective-permute-start.29 = (f32[128,384]{1,0:T(8,128)S(1)}, f32[128,384]{1,0:T(8,128)S(1)}, u32[]{:S(2)}, u32[]{:S(2)}) collective-permute-start(f32[128,384]{1,0:T(8,128)S(1)} %add.155), channel_id=1, source_target_pairs={{0,96},{32,64},{64,32},{96,0},{1,97},{33,65},{65,33},{97,1},{2,98}... | collective-permute-start | bytes 589832 | tf_op jit(solution)/shard_map/ppermute | solution.py:29
  133.1 18.0 %collective-permute-start.34 = (f32[8,6144]{1,0:T(8,128)S(1)}, f32[8,6144]{1,0:T(8,128)S(1)}, u32[]{:S(2)}, u32[]{:S(2)}) collective-permute-start(f32[8,6144]{1,0:T(8,128)S(1)} %fusion.21), channel_id=1, source_target_pairs={{0,96},{32,64},{64,32},{96,0},{1,97},{33,65},{65,33},{97,1},{2,98}... | collective-permute-start | bytes 589832 | tf_op jit(solution)/shard_map/ppermute | solution.py:29
  135.1 40.4 %collective-permute-start.27 = (bf16[256,1536]{1,0:T(8,128)(2,1)}, bf16[256,1536]{1,0:T(8,128)(2,1)}, u32[]{:S(2)}, u32[]{:S(2)}) collective-permute-start(bf16[256,1536]{1,0:T(8,128)(2,1)} %pad_maximum_fusion.3), channel_id=1, source_target_pairs={{0,8},{8,0},{16,24},{24,16},{1,9},{9,1},{17,25},{25,17},{2,10},{10... | collective-permute-start | bytes 2359304 | tf_op jit(solution)/shard_map/ppermute | solution.py:29
  136.5 39.0 %collective-permute-start.26 = (bf16[256,1536]{1,0:T(8,128)(2,1)}, bf16[256,1536]{1,0:T(8,128)(2,1)}, u32[]{:S(2)}, u32[]{:S(2)}) collective-permute-start(bf16[256,1536]{1,0:T(8,128)(2,1)} %pad_maximum_fusion.2), channel_id=1, source_target_pairs={{0,24},{8,16},{16,8},{24,0},{1,25},{9,17},{17,9},{25,1},{2,26},{10... | collective-permute-start | bytes 2359304 | tf_op jit(solution)/shard_map/ppermute | solution.py:29
  139.1 36.4 %collective-permute-start.25 = (bf16[256,1536]{1,0:T(8,128)(2,1)}, bf16[256,1536]{1,0:T(8,128)(2,1)}, u32[]{:S(2)}, u32[]{:S(2)}) collective-permute-start(bf16[256,1536]{1,0:T(8,128)(2,1)} %pad_maximum_fusion.1), channel_id=1, source_target_pairs={{0,2},{2,0},{4,6},{6,4},{1,3},{3,1},{5,7},{7,5},{8,10},{10,8},{12,... | collective-permute-start | bytes 2359304 | tf_op jit(solution)/shard_map/ppermute | solution.py:29
  149.2 26.4 %collective-permute-start.24 = (bf16[256,1536]{1,0:T(8,128)(2,1)S(1)}, bf16[256,1536]{1,0:T(8,128)(2,1)S(1)}, u32[]{:S(2)}, u32[]{:S(2)}) collective-permute-start(bf16[256,1536]{1,0:T(8,128)(2,1)S(1)} %pad_maximum_fusion), channel_id=1, source_target_pairs={{0,6},{2,4},{4,2},{6,0},{1,7},{3,5},{5,3},{7,1},{8,14},{10,12},{12... | collective-permute-start | bytes 2359304 | tf_op jit(solution)/shard_map/ppermute | solution.py:29
  (29 other events, 243.4 us)
Sparse Core Ops, SparseCore 0:
  127.0 46.7 all-gather.1

commit v3 on v2

--- a/solution.py
+++ b/solution.py
@@ -195,22 +195,22 @@
     )(tokens, maps, slots, frozen, up)
 
 
-def place(at, parts, height, out_shape, onto=None, after=()):
+def place(at, parts, height, out_shape, onto=None, after=(), begin=0):
     flat = [values for part in parts for values in part]
-    count = len(flat) // len(STREAMS)
+    count = len(flat) // len(parts)
 
     def kernel(at, *refs):
         out, sems = refs[-2:]
         width = out.shape[1] // len(STREAMS)
         copies = []
-        for s in range(len(STREAMS)):
+        for s in range(len(parts)):
             for values in refs[s * count : (s + 1) * count]:
                 for first in range(0, values.shape[0], height):
                     spot = pl.multiple_of(at[len(copies)] * height, height)
                     copies.append(
                         pltpu.make_async_copy(
                             values.at[pl.ds(first, height), :],
-                            out.at[pl.ds(spot, height), pl.ds(s * width, width)],
+                            out.at[pl.ds(spot, height), pl.ds((begin + s) * width, width)],
                             sems.at[len(copies)],
                         )
                     )
@@ -228,7 +228,7 @@
         + [anywhere] * len(more),
         out_specs=anywhere,
         out_shape=out_shape,
-        scratch_shapes=[pltpu.SemaphoreType.DMA((2 * len(STREAMS),))],
+        scratch_shapes=[pltpu.SemaphoreType.DMA((2 * len(parts),))],
         input_output_aliases={1 + len(flat) + len(after): 0} if onto is not None else {},
         compiler_params=pltpu.CompilerParams(vmem_limit_bytes=12 << 20),
         name="place",
@@ -280,58 +280,102 @@
     )(at, grad, table, hot, down)
 
 
-def backward_kernel(grad, table, hot, frozen, up, slots, tokens, maps, sent, back, total):
+def back_kernel(grad, table, hot, up, slots, tokens, maps, *rest):
+    parts, (packed, low, scaled, back) = rest[:-4], rest[-4:]
     j = pl.program_id(0)
-    rows = hot.shape[0]
+    adapters = parts[0].shape[0] // 2
+    depth = tokens.shape[1]
 
     @pl.when(j == 0)
     def _():
         back[...] = jnp.zeros_like(back)
-        total[...] = jnp.zeros_like(total)
-
-    scaled = (wide(grad[...]) * dot(hot[...], table[...])).astype(BF)
-    back[...] += dot(scaled, up[...], LAST)
-    total[...] += dot(scaled, frozen[...], LAST)
+
+    scaled[...] = (wide(grad[...]) * dot(hot[...], table[...])).astype(BF)
+    back[...] += dot(scaled[...], up[...], LAST)
 
     @pl.when(j == pl.num_programs(0) - 1)
     def _():
         upper, lower = split_parts(back[...] * wide(slots[...]))
-        down_maps = maps[...]
-        full = total[...] + dot(upper, down_maps, LAST) + dot(lower, down_maps, LAST)
-        sent[:rows, :] = full.astype(BF)
+        low[...] = dot(upper, maps[...], LAST) + dot(lower, maps[...], LAST)
         values = tokens[...]
-        sent[rows:, :] = (dot(upper, values, FIRST) + dot(lower, values, FIRST)).astype(BF)
-
-
-def backward(grad, table, hot, frozen, up, slots, tokens, maps):
-    rows, depth = tokens.shape
-    flat, cols = up.shape
-
-    def whole(values):
-        return pl.BlockSpec(values.shape, lambda j: (0, 0))
-
-    def moving(height):
-        return pl.BlockSpec((height, SPAN), lambda j: (0, j))
+        packed[:, :depth] = (dot(upper, values, FIRST) + dot(lower, values, FIRST)).astype(BF)
+        size = packed.shape[1] - depth
+        for s in range(len(STREAMS)):
+            total = wide(parts[2 * s][...]) + wide(parts[2 * s + 1][...])
+            for q in range(total.shape[1] // size // 2):
+                first = 2 * q * size
+                both = [total[:adapters, first + k * size : first + (k + 1) * size] for k in (0, 1)]
+                at = (s * (total.shape[1] // size) + 2 * q) * adapters
+                packed[at : at + 2 * adapters, depth:] = jnp.concatenate(both, axis=0).astype(BF)
+
+
+def back_part(grad, table, hot, up, slots, tokens, maps, parts, share):
+    rows, cols = grad.shape
+    depth, flat = maps.shape
+    tall = hot.shape[1] // 3
+
+    def whole(shape):
+        return pl.BlockSpec(shape, lambda j: (0, 0))
+
+    def moving(values):
+        return pl.BlockSpec((values.shape[0], SPAN), lambda j: (0, j))
+
+    def foot(values):
+        return pl.BlockSpec((tall, values.shape[1]), lambda j: (values.shape[0] // tall - 1, 0))
+
+    return pl.pallas_call(
+        back_kernel,
+        grid=(cols // SPAN,),
+        in_specs=[moving(grad), moving(table), whole(hot.shape), moving(up)]
+        + [whole(values.shape) for values in (slots, tokens, maps)]
+        + [foot(values) for values in parts],
+        out_specs=[whole((flat, depth + share)), whole((rows, depth)), moving(grad)],
+        out_shape=[
+            jax.ShapeDtypeStruct((flat, depth + share), BF),
+            jax.ShapeDtypeStruct((rows, depth), F32),
+            jax.ShapeDtypeStruct((rows, cols), BF),
+        ],
+        scratch_shapes=[pltpu.VMEM((rows, flat), F32)],
+        name="back",
+        **limits(2 * rows * 2 * flat * cols, 2 * cols * rows),
+    )(grad, table, hot, up, slots, tokens, maps, *parts)
+
+
+def backward_kernel(scaled, frozen, start, out, total):
+    j = pl.program_id(0)
+
+    @pl.when(j == 0)
+    def _():
+        total[...] = start[...]
+
+    total[...] += dot(scaled[...], frozen[...], LAST)
+
+    @pl.when(j == pl.num_programs(0) - 1)
+    def _():
+        out[...] = total[...].astype(BF)
+
+
+def backward(scaled, frozen, start):
+    rows, cols = scaled.shape
+    depth = frozen.shape[0]
+    span = cols // 3
+
+    def whole(shape):
+        return pl.BlockSpec(shape, lambda j: (0, 0))
+
+    def moving(values):
+        return pl.BlockSpec((values.shape[0], span), lambda j: (0, j))
 
     return pl.pallas_call(
         backward_kernel,
-        grid=(cols // SPAN,),
-        in_specs=[
-            moving(rows),
-            moving(table.shape[0]),
-            whole(hot),
-            moving(depth),
-            moving(flat),
-            whole(slots),
-            whole(tokens),
-            whole(maps),
-        ],
-        out_specs=pl.BlockSpec((rows + flat, depth), lambda j: (0, 0)),
-        out_shape=jax.ShapeDtypeStruct((rows + flat, depth), BF),
-        scratch_shapes=[pltpu.VMEM((rows, flat), F32), pltpu.VMEM((rows, depth), F32)],
+        grid=(3,),
+        in_specs=[moving(scaled), moving(frozen), whole(start.shape)],
+        out_specs=whole(start.shape),
+        out_shape=jax.ShapeDtypeStruct(start.shape, BF),
+        scratch_shapes=[pltpu.VMEM((rows, depth), F32)],
         name="backward",
-        **limits(2 * rows * (depth + 2 * flat) * cols, 2 * cols * (depth + rows)),
-    )(grad, table, hot, frozen, up, slots, tokens, maps)
+        **limits(2 * rows * depth * cols, 2 * cols * (depth + rows)),
+    )(scaled, frozen, start)
 
 
 def on_device(
@@ -364,7 +408,7 @@
     first = exchange([away for away, _, _ in streams], 0)
     for step, pairing in enumerate((("y", 1), ("z", 1), ("y", 3), ("z", 3))):
         if step == 0:
-            small, _ = lax.optimization_barrier((small, first))
+            small, _ = lax.optimization_barrier((small, first[0]))
         got = swap(small, pairing)
         if step < 3:
             small = round_bf(wide(small) + wide(got))
@@ -400,35 +444,42 @@
     got = exchange(sums, 2)
     sums = [round_bf(wide(a) + wide(b)) for a, b in zip(sums, got, strict=True)]
     got = exchange(sums, 3)
-    done, mags = [], []
+
+    grad_up = grad_up_part(at, grad_out, table, hot3, down, cols // SIDE**2)
+    for flip in (1, 3):
+        grad_up = grad_up + swap(grad_up, ("dp", flip))
+    share = round_bf(grad_up)
+
+    done = []
     for s, (a, b) in enumerate(zip(sums, got, strict=True)):
         me = spot[STREAMS[s][0][0]]
         rows = lax.dynamic_slice_in_dim(hot3, me * block, block, 0)
         scale = dot(rows, table[:, s * width : (s + 1) * width])
         done.append((scale * (wide(a[:block]) + wide(b[:block]))).astype(BF))
-        mags.append(wide(a[block : block + adapters]) + wide(b[block : block + adapters]))
     near = exchange(done, 0)
-    sent = backward(grad_out, table, hot3, frozen, adapter_up, slots, tokens, adapter_down)
-    near, sent = lax.optimization_barrier((near, sent))
+    parts = [v for both in zip(sums, got, strict=True) for v in both]
+    packed, low, scaled = back_part(
+        grad_out, table, hot3, adapter_up, slots, tokens, adapter_down, parts, cols // SIDE**2
+    )
+    near, packed, low = lax.optimization_barrier((near, packed, low))
+    packed = round_bf(wide(packed) + wide(swap(packed, ("dp", 1))))
+    low, packed = lax.optimization_barrier((low, packed))
     pairs = [jnp.concatenate(both, axis=0) for both in zip(done, near, strict=True)]
     far = exchange(pairs, 1)
-    mag = jnp.concatenate(mags, axis=1)
-    for flip in (1, 3):
-        mag = mag + swap(mag, ("dp", flip))
-
-    grad_up = grad_up_part(at, grad_out, table, hot3, down, cols // SIDE**2)
-    for flip in (1, 3):
-        grad_up = grad_up + swap(grad_up, ("dp", flip))
-    grad_up = lax.all_gather(round_bf(grad_up), ("z", "y"), axis=1, tiled=True).astype(F32)
-    total = wide(sent) + wide(lax.ppermute(sent, "col", [(0, 1), (1, 0)]))
+    grad_up = lax.all_gather(share, ("z", "y"), axis=1, tiled=True).astype(F32)
+    packed = wide(packed) + wide(swap(packed, ("dp", 3)))
+    mag = packed[:, depth:].reshape(-1, adapters, packed.shape[1] - depth)
+    mag = mag.transpose(1, 0, 2).reshape(adapters, cols)
+    sent = backward(scaled, frozen, low)
+    sent = jnp.concatenate([sent, round_bf(packed[:, :depth])] * 2, axis=0)
+    both = wide(lax.all_to_all(sent, "col", 0, 0, tiled=True))
+    total = both[: tok_rows + flat] + both[tok_rows + flat :]
     input_grad = total[:tok_rows].astype(BF)
     grad_down = total[tok_rows:]
-    for flip in (1, 3):
-        share = round_bf(grad_down)
-        grad_down = wide(share) + wide(swap(share, ("dp", flip)))
     whole = jax.ShapeDtypeStruct((tok_rows, cols), BF)
     adapted = place(early, list(zip(done, near, strict=True)), block, whole)
-    adapted = place(late, [[v] for v in far], block, whole, onto=adapted, after=(grad_up,))
+    after = (grad_up, input_grad)
+    adapted = place(late, [[v] for v in far], block, whole, onto=adapted, after=after)
     return (adapted, input_grad, grad_down.T, grad_up, mag / col_norm)
 
 

time: 188 us -> 173 us (0.920)
  waiting for transfers between devices: 52 us -> 21.4 us
  Pallas kernels: 51.3 us -> 58.7 us
  blocking collectives: 0 us -> 5.58 us
  other arithmetic: 9.82 us -> 14.6 us
  starting transfers between devices: 52.9 us -> 50.1 us
    ppermute x34 -> x32, waiting for transfers between devices: 38 us -> 21.3 us  [swap(): return lax.ppermute(values, axis, [(i, i ^ flip) for i in range(SIDE)])]
    all_gather x1, waiting for transfers between devices: 14 us -> 0.02 us  [on_device(): grad_up = lax.all_gather(share, ('z', 'y'), axis=1, tiled=True).astype(F32)]
    pallas_call x1 -> x2, Pallas kernels: 15.4 us -> 22.5 us  [the longest x1 11.8 us: backward(): pl.pallas_call(backward_kernel, grid=(3,), in_specs=[moving(scaled), movi...]
    all_to_all x0 -> x1, blocking collectives: none -> 5.58 us  [on_device(): both = wide(lax.all_to_all(sent, 'col', 0, 0, tiled=True))]
    ppermute x34 -> x32, starting transfers between devices: 52.8 us -> 50 us  [swap(): return lax.ppermute(values, axis, [(i, i ^ flip) for i in range(SIDE)])]
    convert_element_type x18, other arithmetic: 1.97 us -> 4.02 us  [round_bf(): lax.reduce_precision(values, exponent_bits=8, mantissa_bits=7).astype(BF)]
    unnamed x35 -> x55, local copies, waits for them, and re-layouts: 3.53 us -> 4.34 us
  transfers between devices with their start and end apart: 36 -> 33, of which waited for: 12 -> 7; matrix products, arithmetic and copies ran while one was open for 7% -> 10% of each run, Pallas kernels for 15% -> 21%
where the time goes in v3:
time: 173 us; the launch traced here: 171 us
  Pallas kernels  58.7 us (34%)
  starting transfers between devices  50.1 us (29%)
  waiting for transfers between devices  21.4 us (12%)
  other arithmetic  14.6 us (8%)
  between operations  14.6 us (8%)
  blocking collectives  5.58 us (3%)
  local copies, waits for them, and re-layouts  5.29 us (3%)
    ppermute x32, starting transfers between devices, swap(): return lax.ppermute(values, axis, [(i, i ^ flip) for i in range(SIDE)])  50 us
    ppermute x32, waiting for transfers between devices, swap(): return lax.ppermute(values, axis, [(i, i ^ flip) for i in range(SIDE)])  21.3 us
    pallas_call x1, Pallas kernels, forward(): pl.pallas_call(forward_kernel, grid_spec=pltpu.PrefetchScalarGridSpec(num...  18 us
    pallas_call x1, Pallas kernels, backward(): pl.pallas_call(backward_kernel, grid=(3,), in_specs=[moving(scaled), movi...  11.8 us
    pallas_call x1, Pallas kernels, back_part(): pl.pallas_call(back_kernel, grid=(cols // SPAN,), in_specs=[moving(grad),...  10.7 us
    pallas_call x1, Pallas kernels, column_squares(): pl.pallas_call(functools.partial(squares_kernel, adapters), grid=(cols //...  8.15 us
    pallas_call x2, Pallas kernels, place(): pl.pallas_call(kernel, in_specs=[pl.BlockSpec(memory_space=pltpu.SMEM)] +...  6.93 us
    all_to_all x1, blocking collectives, on_device(): both = wide(lax.all_to_all(sent, 'col', 0, 0, tiled=True))  5.58 us
  transfers between devices with their start and end apart: 33, of which 7 were waited for; matrix products, arithmetic and copies ran while one was open for 10% of the time, Pallas kernels for 21%

profile of v3, /device:TPU:0, one launch (start us, length us, event | category | flops | bytes accessed | tf_op | source)
XLA Modules:
  0.0 171.2 jit_solution(7511300827919936865)
XLA Ops:
  7.9 18.0 %forward.1 = (bf16[272,1536]{1,0:T(8,128)(2,1)}, bf16[144,1536]{1,0:T(8,128)(2,1)}, bf16[144,1536]{1,0:T(8,128)(2,1)}, bf16[272,1536]{1,0:T(8,128)(2,1)}, bf16[1...) custom-call(s32[19]{0:T(128)} %stack.80.at, ...), custom_call_target="tpu_custom_call" | custom-call | flops 7247757312 | bytes 23592960 | tf_op jit(solution)/shard_map/forward/pallas_call | solution.py:120
  27.6 2.2 %collective-permute-start.9 = (bf16[272,1536]{1,0:T(8,128)(2,1)}, bf16[272,1536]{1,0:T(8,128)(2,1)S(1)}, u32[]{:S(2)}, u32[]{:S(2)}) collective-permute-start(bf16[272,1536]{1,0:T(8,128)(2,1)} %get-tuple-element.42), channel_id=1, source_target_pairs={{0,6},{2,4},{4,2},{6,0},{1,7},{3,5},{5,3},{7,1},{8,14},{10,12},{12... | collective-permute-start | bytes 2506760 | tf_op jit(solution)/shard_map/ppermute | solution.py:29
  31.7 2.5 %collective-permute-start.19 = (bf16[272,1536]{1,0:T(8,128)(2,1)}, bf16[272,1536]{1,0:T(8,128)(2,1)S(1)}, u32[]{:S(2)}, u32[]{:S(2)}) collective-permute-start(bf16[272,1536]{1,0:T(8,128)(2,1)} %get-tuple-element.48), channel_id=1, source_target_pairs={{0,24},{8,16},{16,8},{24,0},{1,25},{9,17},{17,9},{25,1},{2,26},{10... | collective-permute-start | bytes 2506760 | tf_op jit(solution)/shard_map/ppermute | solution.py:29
  34.3 8.1 %squares.1 = bf16[896,128]{1,0:T(8,128)(2,1)} custom-call(bf16[512,896]{1,0:T(8,128)(2,1)} %tokens.5, bf16[896,128]{1,0:T(8,128)(2,1)} %maps.5, bf16[512,128]{1,0:T(8,128)(2,1)} %get-tuple-element.35.slots, bf16[896,6144]{1,0:T(8,128)(2,1)} %frozen.5, bf16[128,6144]{1,0:T(8,128)(2,1)} %up.5), custom_call_target="tpu_custom_call" | custom-call | flops 1409286144 | bytes 11010048 | tf_op jit(solution)/shard_map/squares/pallas_call | solution.py:186
  42.4 4.1 %collective-permute-done = bf16[272,1536]{1,0:T(8,128)(2,1)} collective-permute-done((bf16[272,1536]{1,0:T(8,128)(2,1)}, bf16[272,1536]{1,0:T(8,128)(2,1)}, u32[]{:S(2)}, u32[]{:S(2)}) %collective-permute-start) | collective-permute-done | bytes 835616 | tf_op jit(solution)/shard_map/ppermute | solution.py:29
  49.4 2.3 %collective-permute-start.5 = (bf16[144,1536]{1,0:T(8,128)(2,1)S(1)}, bf16[144,1536]{1,0:T(8,128)(2,1)S(1)}, u32[]{:S(2)}, u32[]{:S(2)}) collective-permute-start(bf16[144,1536]{1,0:T(8,128)(2,1)S(1)} %reduce-precision_convert_fusion.7), channel_id=1, source_target_pairs={{0,6},{2,4},{4,2},{6,0},{1,7},{3,5},{5,3},{7,1},{8,14},{10,12},{12... | collective-permute-start | bytes 1327112 | tf_op jit(solution)/shard_map/ppermute | solution.py:29
  52.7 4.1 %collective-permute-start.15 = (bf16[144,1536]{1,0:T(8,128)(2,1)S(1)}, bf16[144,1536]{1,0:T(8,128)(2,1)S(1)}, u32[]{:S(2)}, u32[]{:S(2)}) collective-permute-start(bf16[144,1536]{1,0:T(8,128)(2,1)S(1)} %reduce-precision_convert_fusion.3), channel_id=1, source_target_pairs={{0,24},{8,16},{16,8},{24,0},{1,25},{9,17},{17,9},{25,1},{2,26},{10... | collective-permute-start | bytes 1327112 | tf_op jit(solution)/shard_map/ppermute | solution.py:29
  57.1 2.1 %collective-permute-start.2 = (bf16[896,128]{1,0:T(8,128)(2,1)S(1)}, bf16[896,128]{1,0:T(8,128)(2,1)S(1)}, u32[]{:S(2)}, u32[]{:S(2)}) collective-permute-start(bf16[896,128]{1,0:T(8,128)(2,1)S(1)} %reduce-precision_convert_fusion.11), channel_id=1, source_target_pairs={{0,8},{8,0},{16,24},{24,16},{1,9},{9,1},{17,25},{25,17},{2,10},{10... | collective-permute-start | bytes 688136 | tf_op jit(solution)/shard_map/ppermute | solution.py:29
  59.2 2.3 %collective-permute-done.5 = bf16[144,1536]{1,0:T(8,128)(2,1)S(1)} collective-permute-done((bf16[144,1536]{1,0:T(8,128)(2,1)S(1)}, bf16[144,1536]{1,0:T(8,128)(2,1)S(1)}, u32[]{:S(2)}, u32[]{:S(2)}) %collective-permute-start.5) | collective-permute-done | bytes 442400 | tf_op jit(solution)/shard_map/ppermute | solution.py:29
  64.9 2.6 %collective-permute-start.11 = (bf16[144,1536]{1,0:T(8,128)(2,1)S(1)}, bf16[144,1536]{1,0:T(8,128)(2,1)S(1)}, u32[]{:S(2)}, u32[]{:S(2)}) collective-permute-start(bf16[144,1536]{1,0:T(8,128)(2,1)S(1)} %fusion.6), channel_id=1, source_target_pairs={{0,24},{8,16},{16,8},{24,0},{1,25},{9,17},{17,9},{25,1},{2,26},{10... | collective-permute-start | bytes 1327112 | tf_op jit(solution)/shard_map/ppermute | solution.py:29
  70.2 4.8 %collective-permute-done.2 = bf16[896,128]{1,0:T(8,128)(2,1)S(1)} collective-permute-done((bf16[896,128]{1,0:T(8,128)(2,1)S(1)}, bf16[896,128]{1,0:T(8,128)(2,1)S(1)}, u32[]{:S(2)}, u32[]{:S(2)}) %collective-permute-start.2) | collective-permute-done | bytes 229408 | tf_op jit(solution)/shard_map/ppermute | solution.py:29
  75.8 2.7 %collective-permute-start.21 = (bf16[144,1536]{1,0:T(8,128)(2,1)S(1)}, bf16[144,1536]{1,0:T(8,128)(2,1)S(1)}, u32[]{:S(2)}, u32[]{:S(2)}) collective-permute-start(bf16[144,1536]{1,0:T(8,128)(2,1)S(1)} %fusion.8), channel_id=1, source_target_pairs={{0,6},{2,4},{4,2},{6,0},{1,7},{3,5},{5,3},{7,1},{8,14},{10,12},{12... | collective-permute-start | bytes 1327112 | tf_op jit(solution)/shard_map/ppermute | solution.py:29
  78.5 3.9 %collective-permute-done.3 = bf16[896,128]{1,0:T(8,128)(2,1)S(1)} collective-permute-done((bf16[896,128]{1,0:T(8,128)(2,1)S(1)}, bf16[896,128]{1,0:T(8,128)(2,1)S(1)}, u32[]{:S(2)}, u32[]{:S(2)}) %collective-permute-start.3) | collective-permute-done | bytes 229408 | tf_op jit(solution)/shard_map/ppermute | solution.py:29
  83.2 2.8 %collective-permute-start.7 = (bf16[144,1536]{1,0:T(8,128)(2,1)S(1)}, bf16[144,1536]{1,0:T(8,128)(2,1)S(1)}, u32[]{:S(2)}, u32[]{:S(2)}) collective-permute-start(bf16[144,1536]{1,0:T(8,128)(2,1)S(1)} %reduce-precision_convert_fusion.6.rest_0_), channel_id=1, source_target_pairs={{0,24},{8,16},{16,8},{24,0},{1,25},{9,17},{17,9},{25,1},{2,26},{10... | collective-permute-start | bytes 1327112 | tf_op jit(solution)/shard_map/ppermute | solution.py:29
  91.4 2.9 %grad_up.1 = f32[128,384]{1,0:T(8,128)} custom-call(s32[19]{0:T(128)} %stack.80.at, bf16[512,6144]{1,0:T(8,128)(2,1)} %grad.5, bf16[48,6144]{1,0:T(8,128)(2,1)} %copy-done.2, bf16[512,48]{1,0:T(8,128)(2,1)} %get-tuple-element.34.hot, bf16[512,128]{1,0:T(8,128)(2,1)} %copy-done.5), custom_call_target="tpu_custom_call" | custom-call | bytes 589824 | tf_op jit(solution)/shard_map/grad_up/pallas_call | solution.py:269
  97.0 3.2 %collective-permute-done.28 = f32[128,384]{1,0:T(8,128)S(1)} collective-permute-done((f32[128,384]{1,0:T(8,128)}, f32[128,384]{1,0:T(8,128)S(1)}, u32[]{:S(2)}, u32[]{:S(2)}) %collective-permute-start.28) | collective-permute-done | bytes 196640 | tf_op jit(solution)/shard_map/ppermute | solution.py:29
  101.9 2.8 %collective-permute-start.29 = (f32[128,384]{1,0:T(8,128)}, f32[128,384]{1,0:T(8,128)}, u32[]{:S(2)}, u32[]{:S(2)}) collective-permute-start(f32[128,384]{1,0:T(8,128)} %add.138), channel_id=1, source_target_pairs={{0,96},{32,64},{64,32},{96,0},{1,97},{33,65},{65,33},{97,1},{2,98}... | collective-permute-start | bytes 589832 | tf_op jit(solution)/shard_map/ppermute | solution.py:29
  111.2 10.7 %back.1 = (bf16[128,1280]{1,0:T(8,128)(2,1)}, f32[512,896]{1,0:T(8,128)}, bf16[512,6144]{1,0:T(8,128)(2,1)}) custom-call(bf16[512,6144]{1,0:T(8,128)(2,1)} %grad.5, bf16[48,6144]{1,0:T(8,128)(2,1)} %copy-done.2, bf16[512,48]{1,0:T(8,128)(2,1)} %get-tuple-element.34.hot, bf16[128,6144]{1,0:T(8,128)(2,1)} %up.5, bf16[512,128]{1,0:T(8,128)(2,1)} %get-tuple-element.35.slots, ...), custom_call_target="tpu_custom_call" | custom-call | flops 1610612736 | bytes 6291456 | tf_op jit(solution)/shard_map/back/pallas_call | solution.py:326
  126.4 2.6 %collective-permute-start.26 = (bf16[256,1536]{1,0:T(8,128)(2,1)}, bf16[256,1536]{1,0:T(8,128)(2,1)}, u32[]{:S(2)}, u32[]{:S(2)}) collective-permute-start(bf16[256,1536]{1,0:T(8,128)(2,1)} %pad_maximum_fusion.3), channel_id=1, source_target_pairs={{0,24},{8,16},{16,8},{24,0},{1,25},{9,17},{17,9},{25,1},{2,26},{10... | collective-permute-start | bytes 2359304 | tf_op jit(solution)/shard_map/ppermute | solution.py:29
  130.5 2.1 %collective-permute-start.24 = (bf16[256,1536]{1,0:T(8,128)(2,1)}, bf16[256,1536]{1,0:T(8,128)(2,1)}, u32[]{:S(2)}, u32[]{:S(2)}) collective-permute-start(bf16[256,1536]{1,0:T(8,128)(2,1)} %pad_maximum_fusion.1), channel_id=1, source_target_pairs={{0,6},{2,4},{4,2},{6,0},{1,7},{3,5},{5,3},{7,1},{8,14},{10,12},{12... | collective-permute-start | bytes 2359304 | tf_op jit(solution)/shard_map/ppermute | solution.py:29
  132.6 2.3 %place.2.refs_6_ = bf16[512,6144]{1,0:T(8,128)(2,1)} custom-call(s32[8]{0:T(128)S(1)} %stack.81.at, bf16[128,1536]{1,0:T(8,128)(2,1)S(1)} %fusion.refs_0_, bf16[128,1536]{1,0:T(8,128)(2,1)S(1)} %collective-permute-done.8.refs_1_, bf16[128,1536]{1,0:T(8,128)(2,1)S(1)} %fusion.1.refs_2_, bf16[128,1536]{1,0:T(8,128)(2,1)S(1)} %collective-permute-done.13.refs_3_, ...), custom_call_target="tpu_custom_call" | custom-call | tf_op jit(solution)/shard_map/place/pallas_call | solution.py:224
  136.2 11.8 %backward.1 = bf16[512,896]{1,0:T(8,128)(2,1)} custom-call(bf16[512,6144]{1,0:T(8,128)(2,1)} %get-tuple-element.57.scaled, bf16[896,6144]{1,0:T(8,128)(2,1)} %frozen.5, f32[512,896]{1,0:T(8,128)} %get-tuple-element.60.start), custom_call_target="tpu_custom_call" | custom-call | flops 5637144576 | bytes 17301504 | tf_op jit(solution)/shard_map/backward/pallas_call | solution.py:369
  149.6 5.6 %all_to_all.9 = bf16[2,640,896]{2,1,0:T(8,128)(2,1)S(1)} all-to-all(bf16[2,640,896]{2,1,0:T(8,128)(2,1)S(1)} %bitcast.24), channel_id=1, replica_groups=mesh['dp'=4,'z'=4,'y'=4,'col'=2] {'col'}, dimensions={0} | all-to-all | bytes 4587520 | tf_op jit(solution)/shard_map/all_to_all | solution.py:475
  159.7 4.7 %place.3 = bf16[512,6144]{1,0:T(8,128)(2,1)} custom-call(s32[8]{0:T(128)S(1)} %stack.75.at, bf16[256,1536]{1,0:T(8,128)(2,1)} %collective-permute-done.24.refs_0_, bf16[256,1536]{1,0:T(8,128)(2,1)} %collective-permute-done.25.refs_1_, bf16[256,1536]{1,0:T(8,128)(2,1)} %collective-permute-done.26.refs_2_, ...), custom_call_target="tpu_custom_call", output_to_operand_aliasing={{}: (7, {})} | custom-call | tf_op jit(solution)/shard_map/place/pallas_call | solution.py:224
  (155 shorter events, 45.6 us)
Async XLA Ops:
  7.2 150.4 %all-gather.2.cloned.1.call-start = ((), (), s32[]{:S(2)}) async-start(), calls=%async_computation.1 | async-start | bytes 1671168 | tf_op jit(solution)/shard_map/all_gather | solution.py:469
  25.9 20.6 %collective-permute-start = (bf16[272,1536]{1,0:T(8,128)(2,1)}, bf16[272,1536]{1,0:T(8,128)(2,1)}, u32[]{:S(2)}, u32[]{:S(2)}) collective-permute-start(bf16[272,1536]{1,0:T(8,128)(2,1)} %get-tuple-element.36), channel_id=1, source_target_pairs={{0,2},{2,0},{4,6},{6,4},{1,3},{3,1},{5,7},{7,5},{8,10},{10,8},{12,... | collective-permute-start | bytes 2506760 | tf_op jit(solution)/shard_map/ppermute | solution.py:29
  27.6 24.0 %collective-permute-start.9 = (bf16[272,1536]{1,0:T(8,128)(2,1)}, bf16[272,1536]{1,0:T(8,128)(2,1)S(1)}, u32[]{:S(2)}, u32[]{:S(2)}) collective-permute-start(bf16[272,1536]{1,0:T(8,128)(2,1)} %get-tuple-element.42), channel_id=1, source_target_pairs={{0,6},{2,4},{4,2},{6,0},{1,7},{3,5},{5,3},{7,1},{8,14},{10,12},{12... | collective-permute-start | bytes 2506760 | tf_op jit(solution)/shard_map/ppermute | solution.py:29
  29.8 22.7 %collective-permute-start.14 = (bf16[272,1536]{1,0:T(8,128)(2,1)}, bf16[272,1536]{1,0:T(8,128)(2,1)S(1)}, u32[]{:S(2)}, u32[]{:S(2)}) collective-permute-start(bf16[272,1536]{1,0:T(8,128)(2,1)} %get-tuple-element.45), channel_id=1, source_target_pairs={{0,8},{8,0},{16,24},{24,16},{1,9},{9,1},{17,25},{25,17},{2,10},{10... | collective-permute-start | bytes 2506760 | tf_op jit(solution)/shard_map/ppermute | solution.py:29
  31.7 25.1 %collective-permute-start.19 = (bf16[272,1536]{1,0:T(8,128)(2,1)}, bf16[272,1536]{1,0:T(8,128)(2,1)S(1)}, u32[]{:S(2)}, u32[]{:S(2)}) collective-permute-start(bf16[272,1536]{1,0:T(8,128)(2,1)} %get-tuple-element.48), channel_id=1, source_target_pairs={{0,24},{8,16},{16,8},{24,0},{1,25},{9,17},{17,9},{25,1},{2,26},{10... | collective-permute-start | bytes 2506760 | tf_op jit(solution)/shard_map/ppermute | solution.py:29
  52.7 14.8 %collective-permute-start.15 = (bf16[144,1536]{1,0:T(8,128)(2,1)S(1)}, bf16[144,1536]{1,0:T(8,128)(2,1)S(1)}, u32[]{:S(2)}, u32[]{:S(2)}) collective-permute-start(bf16[144,1536]{1,0:T(8,128)(2,1)S(1)} %reduce-precision_convert_fusion.3), channel_id=1, source_target_pairs={{0,24},{8,16},{16,8},{24,0},{1,25},{9,17},{17,9},{25,1},{2,26},{10... | collective-permute-start | bytes 1327112 | tf_op jit(solution)/shard_map/ppermute | solution.py:29
  56.9 13.2 %collective-permute-start.20 = (bf16[144,1536]{1,0:T(8,128)(2,1)S(1)}, bf16[144,1536]{1,0:T(8,128)(2,1)S(1)}, u32[]{:S(2)}, u32[]{:S(2)}) collective-permute-start(bf16[144,1536]{1,0:T(8,128)(2,1)S(1)} %reduce-precision_convert_fusion.1), channel_id=1, source_target_pairs={{0,8},{8,0},{16,24},{24,16},{1,9},{9,1},{17,25},{25,17},{2,10},{10... | collective-permute-start | bytes 1327112 | tf_op jit(solution)/shard_map/ppermute | solution.py:29
  57.1 17.9 %collective-permute-start.2 = (bf16[896,128]{1,0:T(8,128)(2,1)S(1)}, bf16[896,128]{1,0:T(8,128)(2,1)S(1)}, u32[]{:S(2)}, u32[]{:S(2)}) collective-permute-start(bf16[896,128]{1,0:T(8,128)(2,1)S(1)} %reduce-precision_convert_fusion.11), channel_id=1, source_target_pairs={{0,8},{8,0},{16,24},{24,16},{1,9},{9,1},{17,25},{25,17},{2,10},{10... | collective-permute-start | bytes 688136 | tf_op jit(solution)/shard_map/ppermute | solution.py:29
  62.7 20.4 %collective-permute-start.6 = (bf16[144,1536]{1,0:T(8,128)(2,1)S(1)}, bf16[144,1536]{1,0:T(8,128)(2,1)S(1)}, u32[]{:S(2)}, u32[]{:S(2)}) collective-permute-start(bf16[144,1536]{1,0:T(8,128)(2,1)S(1)} %fusion.5), channel_id=1, source_target_pairs={{0,8},{8,0},{16,24},{24,16},{1,9},{9,1},{17,25},{25,17},{2,10},{10... | collective-permute-start | bytes 1327112 | tf_op jit(solution)/shard_map/ppermute | solution.py:29
  64.9 21.1 %collective-permute-start.11 = (bf16[144,1536]{1,0:T(8,128)(2,1)S(1)}, bf16[144,1536]{1,0:T(8,128)(2,1)S(1)}, u32[]{:S(2)}, u32[]{:S(2)}) collective-permute-start(bf16[144,1536]{1,0:T(8,128)(2,1)S(1)} %fusion.6), channel_id=1, source_target_pairs={{0,24},{8,16},{16,8},{24,0},{1,25},{9,17},{17,9},{25,1},{2,26},{10... | collective-permute-start | bytes 1327112 | tf_op jit(solution)/shard_map/ppermute | solution.py:29
  67.7 18.5 %collective-permute-start.16 = (bf16[144,1536]{1,0:T(8,128)(2,1)S(1)}, bf16[144,1536]{1,0:T(8,128)(2,1)S(1)}, u32[]{:S(2)}, u32[]{:S(2)}) collective-permute-start(bf16[144,1536]{1,0:T(8,128)(2,1)S(1)} %fusion.7), channel_id=1, source_target_pairs={{0,2},{2,0},{4,6},{6,4},{1,3},{3,1},{5,7},{7,5},{8,10},{10,8},{12,... | collective-permute-start | bytes 1327112 | tf_op jit(solution)/shard_map/ppermute | solution.py:29
  75.8 20.0 %collective-permute-start.21 = (bf16[144,1536]{1,0:T(8,128)(2,1)S(1)}, bf16[144,1536]{1,0:T(8,128)(2,1)S(1)}, u32[]{:S(2)}, u32[]{:S(2)}) collective-permute-start(bf16[144,1536]{1,0:T(8,128)(2,1)S(1)} %fusion.8), channel_id=1, source_target_pairs={{0,6},{2,4},{4,2},{6,0},{1,7},{3,5},{5,3},{7,1},{8,14},{10,12},{12... | collective-permute-start | bytes 1327112 | tf_op jit(solution)/shard_map/ppermute | solution.py:29
  83.2 21.4 %collective-permute-start.7 = (bf16[144,1536]{1,0:T(8,128)(2,1)S(1)}, bf16[144,1536]{1,0:T(8,128)(2,1)S(1)}, u32[]{:S(2)}, u32[]{:S(2)}) collective-permute-start(bf16[144,1536]{1,0:T(8,128)(2,1)S(1)} %reduce-precision_convert_fusion.6.rest_0_), channel_id=1, source_target_pairs={{0,24},{8,16},{16,8},{24,0},{1,25},{9,17},{17,9},{25,1},{2,26},{10... | collective-permute-start | bytes 1327112 | tf_op jit(solution)/shard_map/ppermute | solution.py:29
  86.1 19.9 %collective-permute-start.12 = (bf16[144,1536]{1,0:T(8,128)(2,1)S(1)}, bf16[144,1536]{1,0:T(8,128)(2,1)S(1)}, u32[]{:S(2)}, u32[]{:S(2)}) collective-permute-start(bf16[144,1536]{1,0:T(8,128)(2,1)S(1)} %reduce-precision_convert_fusion.4.rest_2_), channel_id=1, source_target_pairs={{0,8},{8,0},{16,24},{24,16},{1,9},{9,1},{17,25},{25,17},{2,10},{10... | collective-permute-start | bytes 1327112 | tf_op jit(solution)/shard_map/ppermute | solution.py:29
  86.3 21.0 %collective-permute-start.17 = (bf16[144,1536]{1,0:T(8,128)(2,1)S(1)}, bf16[144,1536]{1,0:T(8,128)(2,1)S(1)}, u32[]{:S(2)}, u32[]{:S(2)}) collective-permute-start(bf16[144,1536]{1,0:T(8,128)(2,1)S(1)} %reduce-precision_convert_fusion.2.rest_4_), channel_id=1, source_target_pairs={{0,6},{2,4},{4,2},{6,0},{1,7},{3,5},{5,3},{7,1},{8,14},{10,12},{12... | collective-permute-start | bytes 1327112 | tf_op jit(solution)/shard_map/ppermute | solution.py:29
  104.9 17.0 %collective-permute-start.8 = (bf16[128,1536]{1,0:T(8,128)(2,1)S(1)}, bf16[128,1536]{1,0:T(8,128)(2,1)S(1)}, u32[]{:S(2)}, u32[]{:S(2)}) collective-permute-start(bf16[128,1536]{1,0:T(8,128)(2,1)S(1)} %fusion.refs_0_), channel_id=1, source_target_pairs={{0,2},{2,0},{4,6},{6,4},{1,3},{3,1},{5,7},{7,5},{8,10},{10,8},{12,... | collective-permute-start | bytes 1179656 | tf_op jit(solution)/shard_map/ppermute | solution.py:29
  106.2 15.7 %collective-permute-start.13 = (bf16[128,1536]{1,0:T(8,128)(2,1)S(1)}, bf16[128,1536]{1,0:T(8,128)(2,1)S(1)}, u32[]{:S(2)}, u32[]{:S(2)}) collective-permute-start(bf16[128,1536]{1,0:T(8,128)(2,1)S(1)} %fusion.1.refs_2_), channel_id=1, source_target_pairs={{0,6},{2,4},{4,2},{6,0},{1,7},{3,5},{5,3},{7,1},{8,14},{10,12},{12... | collective-permute-start | bytes 1179656 | tf_op jit(solution)/shard_map/ppermute | solution.py:29
  107.6 14.3 %collective-permute-start.18 = (bf16[128,1536]{1,0:T(8,128)(2,1)S(1)}, bf16[128,1536]{1,0:T(8,128)(2,1)S(1)}, u32[]{:S(2)}, u32[]{:S(2)}) collective-permute-start(bf16[128,1536]{1,0:T(8,128)(2,1)S(1)} %fusion.2.refs_4_), channel_id=1, source_target_pairs={{0,8},{8,0},{16,24},{24,16},{1,9},{9,1},{17,25},{25,17},{2,10},{10... | collective-permute-start | bytes 1179656 | tf_op jit(solution)/shard_map/ppermute | solution.py:29
  108.5 13.4 %collective-permute-start.23 = (bf16[128,1536]{1,0:T(8,128)(2,1)S(1)}, bf16[128,1536]{1,0:T(8,128)(2,1)S(1)}, u32[]{:S(2)}, u32[]{:S(2)}) collective-permute-start(bf16[128,1536]{1,0:T(8,128)(2,1)S(1)} %fusion.3.refs_6_), channel_id=1, source_target_pairs={{0,24},{8,16},{16,8},{24,0},{1,25},{9,17},{17,9},{25,1},{2,26},{10... | collective-permute-start | bytes 1179656 | tf_op jit(solution)/shard_map/ppermute | solution.py:29
  125.2 34.4 %collective-permute-start.27 = (bf16[256,1536]{1,0:T(8,128)(2,1)}, bf16[256,1536]{1,0:T(8,128)(2,1)}, u32[]{:S(2)}, u32[]{:S(2)}) collective-permute-start(bf16[256,1536]{1,0:T(8,128)(2,1)} %pad_maximum_fusion.4), channel_id=1, source_target_pairs={{0,8},{8,0},{16,24},{24,16},{1,9},{9,1},{17,25},{25,17},{2,10},{10... | collective-permute-start | bytes 2359304 | tf_op jit(solution)/shard_map/ppermute | solution.py:29
  126.4 33.2 %collective-permute-start.26 = (bf16[256,1536]{1,0:T(8,128)(2,1)}, bf16[256,1536]{1,0:T(8,128)(2,1)}, u32[]{:S(2)}, u32[]{:S(2)}) collective-permute-start(bf16[256,1536]{1,0:T(8,128)(2,1)} %pad_maximum_fusion.3), channel_id=1, source_target_pairs={{0,24},{8,16},{16,8},{24,0},{1,25},{9,17},{17,9},{25,1},{2,26},{10... | collective-permute-start | bytes 2359304 | tf_op jit(solution)/shard_map/ppermute | solution.py:29
  129.0 30.6 %collective-permute-start.25 = (bf16[256,1536]{1,0:T(8,128)(2,1)}, bf16[256,1536]{1,0:T(8,128)(2,1)}, u32[]{:S(2)}, u32[]{:S(2)}) collective-permute-start(bf16[256,1536]{1,0:T(8,128)(2,1)} %pad_maximum_fusion.2), channel_id=1, source_target_pairs={{0,2},{2,0},{4,6},{6,4},{1,3},{3,1},{5,7},{7,5},{8,10},{10,8},{12,... | collective-permute-start | bytes 2359304 | tf_op jit(solution)/shard_map/ppermute | solution.py:29
  130.5 29.1 %collective-permute-start.24 = (bf16[256,1536]{1,0:T(8,128)(2,1)}, bf16[256,1536]{1,0:T(8,128)(2,1)}, u32[]{:S(2)}, u32[]{:S(2)}) collective-permute-start(bf16[256,1536]{1,0:T(8,128)(2,1)} %pad_maximum_fusion.1), channel_id=1, source_target_pairs={{0,6},{2,4},{4,2},{6,0},{1,7},{3,5},{5,3},{7,1},{8,14},{10,12},{12... | collective-permute-start | bytes 2359304 | tf_op jit(solution)/shard_map/ppermute | solution.py:29
  135.0 13.0 %collective-permute-start.31 = (bf16[128,1280]{1,0:T(8,128)(2,1)S(1)}, bf16[128,1280]{1,0:T(8,128)(2,1)S(1)}, u32[]{:S(2)}, u32[]{:S(2)}) collective-permute-start(bf16[128,1280]{1,0:T(8,128)(2,1)S(1)} %reduce-precision_convert_fusion.8), channel_id=1, source_target_pairs={{0,96},{32,64},{64,32},{96,0},{1,97},{33,65},{65,33},{97,1},{2,98}... | collective-permute-start | bytes 983048 | tf_op jit(solution)/shard_map/ppermute | solution.py:29
  (37 other events, 311.0 us)
Sparse Core Ops, SparseCore 0:
  111.4 44.4 all-gather.1

commit v4 on v3

--- a/solution.py
+++ b/solution.py
@@ -58,7 +58,7 @@
 def forward_kernel(at, lengths, owners, tokens, maps, frozen, up, grad, *rest):
     n = len(STREAMS)
     outs = [rest[3 * s : 3 * s + 3] for s in range(n)]
-    hot3, slots, low, hot, total = rest[3 * n :]
+    hot3, slots, low, hot, stage, sems = rest[3 * n :]
     j = pl.program_id(0)
     rows = tokens.shape[0]
     block = rows // SIDE
@@ -84,22 +84,36 @@
         hot[...] = jnp.where(same, 1.0, 0.0).astype(BF)
         low[...] = (dot(tokens[...], maps[...]) * held).astype(BF)
 
-    total[...] = dot(tokens[...], frozen[...]) + dot(low[...], up[...])
-    mag = dot(hot[...], (total[...] * wide(grad[...])).astype(BF)).astype(BF)
+    total = dot(tokens[...], frozen[...]) + dot(low[...], up[...])
+    mag = dot(hot[...], (total * wide(grad[...])).astype(BF)).astype(BF)
     tall = mag.shape[0]
+
+    def copies(s):
+        first = 0
+        for part, out in enumerate((outs[s][2], outs[s][0], outs[s][1])):
+            height = out.shape[0]
+            held = stage.at[s % 2, pl.ds(first, height), :]
+            yield pltpu.make_async_copy(held, out, sems.at[s % 2, part])
+            first += height
 
     for s in range(n):
 
         @pl.when(j == s)
         def _(s=s):
-            away, high, near = outs[s]
-            away[block : block + tall, :] = mag
-            high[:tall, :] = mag
-            near[block:, :] = mag
-            places = ((away, 0), (away, block + tall), (near, 0), (high, tall))
-            for slot, (ref, first) in enumerate(places):
-                spot = pl.multiple_of(at[3 + SIDE * s + slot] * block, block)
-                ref[first : first + block, :] = total[pl.ds(spot, block), :].astype(BF)
+            if s >= 2:
+                for copy in copies(s - 2):
+                    copy.wait()
+            for first in (block, 2 * block + tall, 3 * block + 2 * tall):
+                stage[s % 2, first : first + tall, :] = mag
+            for which in range(SIDE):
+                spot = pl.multiple_of(at[3 + SIDE * s + which], 16)
+                rows_of = total[which * block : (which + 1) * block]
+                stage[s % 2, pl.ds(spot, block), :] = rows_of.astype(BF)
+            for copy in copies(s):
+                copy.start()
+            if s == n - 1:
+                for copy in (*copies(s - 1), *copies(s)):
+                    copy.wait()
 
 
 def forward(at, lengths, owners, tokens, maps, frozen, up, grad):
@@ -129,11 +143,13 @@
                 moving(flat),
                 moving(rows),
             ],
-            out_specs=[whole(shape) for shape in shapes],
+            out_specs=[pl.BlockSpec(memory_space=pl.ANY)] * len(heights)
+            + [whole(shape) for shape in shapes[len(heights) :]],
             scratch_shapes=[
                 pltpu.VMEM((rows, flat), BF),
                 pltpu.VMEM((tall, rows), BF),
-                pltpu.VMEM((rows, width), F32),
+                pltpu.VMEM((2, rows + 3 * tall, width), BF),
+                pltpu.SemaphoreType.DMA((2, 3)),
             ],
         ),
         out_shape=[jax.ShapeDtypeStruct(shape, BF) for shape in shapes],
@@ -235,6 +251,57 @@
     )(at, *flat, *more)
 
 
+def place_last(at, parts, height, out_shape, onto, after):
+    flat = [values for part in parts for values in part]
+    count = len(flat) // len(parts)
+
+    def kernel(at, *refs):
+        out, held, sems = refs[-3:]
+        width = out.shape[1] // len(STREAMS)
+        loads, stores = [], []
+        for s in range(len(parts)):
+            for values in refs[s * count : (s + 1) * count]:
+                for first in range(0, values.shape[0], height):
+                    n = len(stores)
+                    spot = pl.multiple_of(at[n] * height, height)
+                    loads.append(
+                        pltpu.make_async_copy(
+                            values.at[pl.ds(first, height), :], held.at[n], sems.at[0, n]
+                        )
+                    )
+                    stores.append(
+                        pltpu.make_async_copy(
+                            held.at[n],
+                            out.at[pl.ds(spot, height), pl.ds(s * width, width)],
+                            sems.at[1, n],
+                        )
+                    )
+        for load in loads:
+            load.start()
+        for load, store in zip(loads, stores, strict=True):
+            load.wait()
+            store.start()
+        for store in stores:
+            store.wait()
+
+    anywhere = pl.BlockSpec(memory_space=pl.ANY)
+    more = [*after, onto]
+    return pl.pallas_call(
+        kernel,
+        in_specs=[pl.BlockSpec(memory_space=pltpu.SMEM)]
+        + [anywhere] * (len(flat) + len(more)),
+        out_specs=anywhere,
+        out_shape=out_shape,
+        scratch_shapes=[
+            pltpu.VMEM((2 * len(parts), height, flat[0].shape[1]), BF),
+            pltpu.SemaphoreType.DMA((2, 2 * len(parts))),
+        ],
+        input_output_aliases={1 + len(flat) + len(after): 0},
+        compiler_params=pltpu.CompilerParams(vmem_limit_bytes=12 << 20),
+        name="place_last",
+    )(at, *flat, *more)
+
+
 def table_kernel(rows, mine, got, magnitude, table, norm, down):
     adapters, cols = magnitude.shape
     flat = mine.shape[1]
@@ -393,7 +460,10 @@
     for one, two, _, _ in STREAMS:
         me = spot[one[0]]
         there = me ^ one[1]
-        spots += [there, there ^ two[1], me, me ^ two[1]]
+        for which in range(SIDE):
+            rest = jnp.where(which == me, 0, 3 * block + 48)
+            rest = jnp.where(which == there ^ two[1], 2 * block + 32, rest)
+            spots.append(jnp.where(which == there, block + 16, rest))
         early += [me, there]
         late += [me ^ two[1], there ^ two[1]]
     at, early, late = (jnp.stack(v).astype(jnp.int32) for v in (spots, early, late))
@@ -479,7 +549,7 @@
     whole = jax.ShapeDtypeStruct((tok_rows, cols), BF)
     adapted = place(early, list(zip(done, near, strict=True)), block, whole)
     after = (grad_up, input_grad)
-    adapted = place(late, [[v] for v in far], block, whole, onto=adapted, after=after)
+    adapted = place_last(late, [[v] for v in far], block, whole, adapted, after)
     return (adapted, input_grad, grad_down.T, grad_up, mag / col_norm)
 
 

time: 173 us -> 171 us (0.988)
    pallas_call x2 -> x1, Pallas kernels: 6.93 us -> 2.26 us  [place(): pl.pallas_call(kernel, in_specs=[pl.BlockSpec(memory_space=pltpu.SMEM)] +...]
    pallas_call x0 -> x1, Pallas kernels: none -> 3.89 us  [place_last(): pl.pallas_call(kernel, in_specs=[pl.BlockSpec(memory_space=pltpu.SMEM)] +...]
where the time goes in v4:
time: 171 us; the launch traced here: 169 us
  Pallas kernels  57 us (33%)
  starting transfers between devices  50.1 us (29%)
  waiting for transfers between devices  21.4 us (13%)
  between operations  14.8 us (9%)
  other arithmetic  14.6 us (9%)
  blocking collectives  5.58 us (3%)
  local copies, waits for them, and re-layouts  4.79 us (3%)
    ppermute x32, starting transfers between devices, swap(): return lax.ppermute(values, axis, [(i, i ^ flip) for i in range(SIDE)])  50 us
    ppermute x32, waiting for transfers between devices, swap(): return lax.ppermute(values, axis, [(i, i ^ flip) for i in range(SIDE)])  21.4 us
    pallas_call x1, Pallas kernels, forward(): pl.pallas_call(forward_kernel, grid_spec=pltpu.PrefetchScalarGridSpec(num...  17.2 us
    pallas_call x1, Pallas kernels, backward(): pl.pallas_call(backward_kernel, grid=(3,), in_specs=[moving(scaled), movi...  11.8 us
    pallas_call x1, Pallas kernels, back_part(): pl.pallas_call(back_kernel, grid=(cols // SPAN,), in_specs=[moving(grad),...  10.7 us
    pallas_call x1, Pallas kernels, column_squares(): pl.pallas_call(functools.partial(squares_kernel, adapters), grid=(cols //...  8.14 us
    all_to_all x1, blocking collectives, on_device(): both = wide(lax.all_to_all(sent, 'col', 0, 0, tiled=True))  5.58 us
    convert_element_type x18, other arithmetic, round_bf(): lax.reduce_precision(values, exponent_bits=8, mantissa_bits=7).astype(BF)  4.02 us
  transfers between devices with their start and end apart: 33, of which 7 were waited for; matrix products, arithmetic and copies ran while one was open for 10% of the time, Pallas kernels for 21%

profile of v4, /device:TPU:0, one launch (start us, length us, event | category | flops | bytes accessed | tf_op | source)
XLA Modules:
  0.0 169.4 jit_solution(8177305173671882496)
XLA Ops:
  8.1 17.2 %forward.1 = (bf16[272,1536]{1,0:T(8,128)(2,1)}, bf16[144,1536]{1,0:T(8,128)(2,1)}, bf16[144,1536]{1,0:T(8,128)(2,1)}, bf16[272,1536]{1,0:T(8,128)(2,1)}, bf16[1...) custom-call(s32[19]{0:T(128)} %stack.126.at, ...), custom_call_target="tpu_custom_call" | custom-call | flops 7247757312 | bytes 23592960 | tf_op jit(solution)/shard_map/forward/pallas_call | solution.py:134
  27.0 2.2 %collective-permute-start.9 = (bf16[272,1536]{1,0:T(8,128)(2,1)}, bf16[272,1536]{1,0:T(8,128)(2,1)S(1)}, u32[]{:S(2)}, u32[]{:S(2)}) collective-permute-start(bf16[272,1536]{1,0:T(8,128)(2,1)} %get-tuple-element.42), channel_id=1, source_target_pairs={{0,6},{2,4},{4,2},{6,0},{1,7},{3,5},{5,3},{7,1},{8,14},{10,12},{12... | collective-permute-start | bytes 2506760 | tf_op jit(solution)/shard_map/ppermute | solution.py:29
  31.1 2.5 %collective-permute-start.19 = (bf16[272,1536]{1,0:T(8,128)(2,1)}, bf16[272,1536]{1,0:T(8,128)(2,1)S(1)}, u32[]{:S(2)}, u32[]{:S(2)}) collective-permute-start(bf16[272,1536]{1,0:T(8,128)(2,1)} %get-tuple-element.48), channel_id=1, source_target_pairs={{0,24},{8,16},{16,8},{24,0},{1,25},{9,17},{17,9},{25,1},{2,26},{10... | collective-permute-start | bytes 2506760 | tf_op jit(solution)/shard_map/ppermute | solution.py:29
  33.6 8.1 %squares.1 = bf16[896,128]{1,0:T(8,128)(2,1)} custom-call(bf16[512,896]{1,0:T(8,128)(2,1)} %tokens.5, bf16[896,128]{1,0:T(8,128)(2,1)} %maps.5, bf16[512,128]{1,0:T(8,128)(2,1)} %get-tuple-element.35.slots, bf16[896,6144]{1,0:T(8,128)(2,1)} %frozen.5, bf16[128,6144]{1,0:T(8,128)(2,1)} %up.5), custom_call_target="tpu_custom_call" | custom-call | flops 1409286144 | bytes 11010048 | tf_op jit(solution)/shard_map/squares/pallas_call | solution.py:202
  41.8 4.1 %collective-permute-done = bf16[272,1536]{1,0:T(8,128)(2,1)} collective-permute-done((bf16[272,1536]{1,0:T(8,128)(2,1)}, bf16[272,1536]{1,0:T(8,128)(2,1)}, u32[]{:S(2)}, u32[]{:S(2)}) %collective-permute-start) | collective-permute-done | bytes 835616 | tf_op jit(solution)/shard_map/ppermute | solution.py:29
  48.8 2.3 %collective-permute-start.5 = (bf16[144,1536]{1,0:T(8,128)(2,1)S(1)}, bf16[144,1536]{1,0:T(8,128)(2,1)S(1)}, u32[]{:S(2)}, u32[]{:S(2)}) collective-permute-start(bf16[144,1536]{1,0:T(8,128)(2,1)S(1)} %reduce-precision_convert_fusion.7), channel_id=1, source_target_pairs={{0,6},{2,4},{4,2},{6,0},{1,7},{3,5},{5,3},{7,1},{8,14},{10,12},{12... | collective-permute-start | bytes 1327112 | tf_op jit(solution)/shard_map/ppermute | solution.py:29
  52.0 4.1 %collective-permute-start.15 = (bf16[144,1536]{1,0:T(8,128)(2,1)S(1)}, bf16[144,1536]{1,0:T(8,128)(2,1)S(1)}, u32[]{:S(2)}, u32[]{:S(2)}) collective-permute-start(bf16[144,1536]{1,0:T(8,128)(2,1)S(1)} %reduce-precision_convert_fusion.3), channel_id=1, source_target_pairs={{0,24},{8,16},{16,8},{24,0},{1,25},{9,17},{17,9},{25,1},{2,26},{10... | collective-permute-start | bytes 1327112 | tf_op jit(solution)/shard_map/ppermute | solution.py:29
  56.5 2.1 %collective-permute-start.2 = (bf16[896,128]{1,0:T(8,128)(2,1)S(1)}, bf16[896,128]{1,0:T(8,128)(2,1)S(1)}, u32[]{:S(2)}, u32[]{:S(2)}) collective-permute-start(bf16[896,128]{1,0:T(8,128)(2,1)S(1)} %reduce-precision_convert_fusion.11), channel_id=1, source_target_pairs={{0,8},{8,0},{16,24},{24,16},{1,9},{9,1},{17,25},{25,17},{2,10},{10... | collective-permute-start | bytes 688136 | tf_op jit(solution)/shard_map/ppermute | solution.py:29
  58.5 2.3 %collective-permute-done.5 = bf16[144,1536]{1,0:T(8,128)(2,1)S(1)} collective-permute-done((bf16[144,1536]{1,0:T(8,128)(2,1)S(1)}, bf16[144,1536]{1,0:T(8,128)(2,1)S(1)}, u32[]{:S(2)}, u32[]{:S(2)}) %collective-permute-start.5) | collective-permute-done | bytes 442400 | tf_op jit(solution)/shard_map/ppermute | solution.py:29
  64.2 2.6 %collective-permute-start.11 = (bf16[144,1536]{1,0:T(8,128)(2,1)S(1)}, bf16[144,1536]{1,0:T(8,128)(2,1)S(1)}, u32[]{:S(2)}, u32[]{:S(2)}) collective-permute-start(bf16[144,1536]{1,0:T(8,128)(2,1)S(1)} %fusion.6), channel_id=1, source_target_pairs={{0,24},{8,16},{16,8},{24,0},{1,25},{9,17},{17,9},{25,1},{2,26},{10... | collective-permute-start | bytes 1327112 | tf_op jit(solution)/shard_map/ppermute | solution.py:29
  69.6 4.8 %collective-permute-done.2 = bf16[896,128]{1,0:T(8,128)(2,1)S(1)} collective-permute-done((bf16[896,128]{1,0:T(8,128)(2,1)S(1)}, bf16[896,128]{1,0:T(8,128)(2,1)S(1)}, u32[]{:S(2)}, u32[]{:S(2)}) %collective-permute-start.2) | collective-permute-done | bytes 229408 | tf_op jit(solution)/shard_map/ppermute | solution.py:29
  75.2 2.7 %collective-permute-start.21 = (bf16[144,1536]{1,0:T(8,128)(2,1)S(1)}, bf16[144,1536]{1,0:T(8,128)(2,1)S(1)}, u32[]{:S(2)}, u32[]{:S(2)}) collective-permute-start(bf16[144,1536]{1,0:T(8,128)(2,1)S(1)} %fusion.8), channel_id=1, source_target_pairs={{0,6},{2,4},{4,2},{6,0},{1,7},{3,5},{5,3},{7,1},{8,14},{10,12},{12... | collective-permute-start | bytes 1327112 | tf_op jit(solution)/shard_map/ppermute | solution.py:29
  77.9 3.9 %collective-permute-done.3 = bf16[896,128]{1,0:T(8,128)(2,1)S(1)} collective-permute-done((bf16[896,128]{1,0:T(8,128)(2,1)S(1)}, bf16[896,128]{1,0:T(8,128)(2,1)S(1)}, u32[]{:S(2)}, u32[]{:S(2)}) %collective-permute-start.3) | collective-permute-done | bytes 229408 | tf_op jit(solution)/shard_map/ppermute | solution.py:29
  82.6 2.8 %collective-permute-start.7 = (bf16[144,1536]{1,0:T(8,128)(2,1)S(1)}, bf16[144,1536]{1,0:T(8,128)(2,1)S(1)}, u32[]{:S(2)}, u32[]{:S(2)}) collective-permute-start(bf16[144,1536]{1,0:T(8,128)(2,1)S(1)} %reduce-precision_convert_fusion.6.rest_0_), channel_id=1, source_target_pairs={{0,24},{8,16},{16,8},{24,0},{1,25},{9,17},{17,9},{25,1},{2,26},{10... | collective-permute-start | bytes 1327112 | tf_op jit(solution)/shard_map/ppermute | solution.py:29
  90.8 2.9 %grad_up.1 = f32[128,384]{1,0:T(8,128)} custom-call(s32[19]{0:T(128)} %stack.126.at, bf16[512,6144]{1,0:T(8,128)(2,1)} %grad.5, bf16[48,6144]{1,0:T(8,128)(2,1)} %copy-done.2, bf16[512,48]{1,0:T(8,128)(2,1)} %get-tuple-element.34.hot, bf16[512,128]{1,0:T(8,128)(2,1)} %copy-done.5), custom_call_target="tpu_custom_call" | custom-call | bytes 589824 | tf_op jit(solution)/shard_map/grad_up/pallas_call | solution.py:336
  96.4 3.2 %collective-permute-done.28 = f32[128,384]{1,0:T(8,128)S(1)} collective-permute-done((f32[128,384]{1,0:T(8,128)}, f32[128,384]{1,0:T(8,128)S(1)}, u32[]{:S(2)}, u32[]{:S(2)}) %collective-permute-start.28) | collective-permute-done | bytes 196640 | tf_op jit(solution)/shard_map/ppermute | solution.py:29
  101.2 2.8 %collective-permute-start.29 = (f32[128,384]{1,0:T(8,128)}, f32[128,384]{1,0:T(8,128)}, u32[]{:S(2)}, u32[]{:S(2)}) collective-permute-start(f32[128,384]{1,0:T(8,128)} %add.138), channel_id=1, source_target_pairs={{0,96},{32,64},{64,32},{96,0},{1,97},{33,65},{65,33},{97,1},{2,98}... | collective-permute-start | bytes 589832 | tf_op jit(solution)/shard_map/ppermute | solution.py:29
  110.2 10.7 %back.1 = (bf16[128,1280]{1,0:T(8,128)(2,1)}, f32[512,896]{1,0:T(8,128)}, bf16[512,6144]{1,0:T(8,128)(2,1)}) custom-call(bf16[512,6144]{1,0:T(8,128)(2,1)} %grad.5, bf16[48,6144]{1,0:T(8,128)(2,1)} %copy-done.2, bf16[512,48]{1,0:T(8,128)(2,1)} %get-tuple-element.34.hot, bf16[128,6144]{1,0:T(8,128)(2,1)} %up.5, bf16[512,128]{1,0:T(8,128)(2,1)} %get-tuple-element.35.slots, ...), custom_call_target="tpu_custom_call" | custom-call | flops 1610612736 | bytes 6291456 | tf_op jit(solution)/shard_map/back/pallas_call | solution.py:393
  125.7 2.2 %collective-permute-start.26 = (bf16[256,1536]{1,0:T(8,128)(2,1)}, bf16[256,1536]{1,0:T(8,128)(2,1)}, u32[]{:S(2)}, u32[]{:S(2)}) collective-permute-start(bf16[256,1536]{1,0:T(8,128)(2,1)} %pad_maximum_fusion.3), channel_id=1, source_target_pairs={{0,24},{8,16},{16,8},{24,0},{1,25},{9,17},{17,9},{25,1},{2,26},{10... | collective-permute-start | bytes 2359304 | tf_op jit(solution)/shard_map/ppermute | solution.py:29
  129.5 2.0 %collective-permute-start.24 = (bf16[256,1536]{1,0:T(8,128)(2,1)}, bf16[256,1536]{1,0:T(8,128)(2,1)}, u32[]{:S(2)}, u32[]{:S(2)}) collective-permute-start(bf16[256,1536]{1,0:T(8,128)(2,1)} %pad_maximum_fusion.1), channel_id=1, source_target_pairs={{0,6},{2,4},{4,2},{6,0},{1,7},{3,5},{5,3},{7,1},{8,14},{10,12},{12... | collective-permute-start | bytes 2359304 | tf_op jit(solution)/shard_map/ppermute | solution.py:29
  131.5 2.3 %place.1.refs_6_ = bf16[512,6144]{1,0:T(8,128)(2,1)} custom-call(s32[8]{0:T(128)S(1)} %stack.129.at, bf16[128,1536]{1,0:T(8,128)(2,1)S(1)} %fusion.refs_0_, bf16[128,1536]{1,0:T(8,128)(2,1)S(1)} %collective-permute-done.8.refs_1_, bf16[128,1536]{1,0:T(8,128)(2,1)S(1)} %fusion.1.refs_2_, bf16[128,1536]{1,0:T(8,128)(2,1)S(1)} %collective-permute-done.13.refs_3_, ...), custom_call_target="tpu_custom_call" | custom-call | tf_op jit(solution)/shard_map/place/pallas_call | solution.py:240
  135.1 11.8 %backward.1 = bf16[512,896]{1,0:T(8,128)(2,1)} custom-call(bf16[512,6144]{1,0:T(8,128)(2,1)} %get-tuple-element.57.scaled, bf16[896,6144]{1,0:T(8,128)(2,1)} %frozen.5, f32[512,896]{1,0:T(8,128)} %get-tuple-element.60.start), custom_call_target="tpu_custom_call" | custom-call | flops 5637144576 | bytes 17301504 | tf_op jit(solution)/shard_map/backward/pallas_call | solution.py:436
  148.5 5.6 %all_to_all.9 = bf16[2,640,896]{2,1,0:T(8,128)(2,1)S(1)} all-to-all(bf16[2,640,896]{2,1,0:T(8,128)(2,1)S(1)} %bitcast.40), channel_id=1, replica_groups=mesh['dp'=4,'z'=4,'y'=4,'col'=2] {'col'}, dimensions={0} | all-to-all | bytes 4587520 | tf_op jit(solution)/shard_map/all_to_all | solution.py:545
  158.6 3.9 %place_last.1 = bf16[512,6144]{1,0:T(8,128)(2,1)} custom-call(s32[8]{0:T(128)S(1)} %stack.107.at, bf16[256,1536]{1,0:T(8,128)(2,1)} %collective-permute-done.24.refs_0_, bf16[256,1536]{1,0:T(8,128)(2,1)} %collective-permute-done.25.refs_1_, bf16[256,1536]{1,0:T(8,128)(2,1)} %collective-permute-done.26.refs_2_, ...), custom_call_target="tpu_custom_call", output_to_operand_aliasing={{}: (7, {})} | custom-call | tf_op jit(solution)/shard_map/place_last/pallas_call | solution.py:289
  (155 shorter events, 45.5 us)
Async XLA Ops:
  7.2 149.3 %all-gather.2.cloned.1.call-start = ((), (), s32[]{:S(2)}) async-start(), calls=%async_computation.1 | async-start | bytes 1671168 | tf_op jit(solution)/shard_map/all_gather | solution.py:539
  25.3 20.7 %collective-permute-start = (bf16[272,1536]{1,0:T(8,128)(2,1)}, bf16[272,1536]{1,0:T(8,128)(2,1)}, u32[]{:S(2)}, u32[]{:S(2)}) collective-permute-start(bf16[272,1536]{1,0:T(8,128)(2,1)} %get-tuple-element.36), channel_id=1, source_target_pairs={{0,2},{2,0},{4,6},{6,4},{1,3},{3,1},{5,7},{7,5},{8,10},{10,8},{12,... | collective-permute-start | bytes 2506760 | tf_op jit(solution)/shard_map/ppermute | solution.py:29
  27.0 24.0 %collective-permute-start.9 = (bf16[272,1536]{1,0:T(8,128)(2,1)}, bf16[272,1536]{1,0:T(8,128)(2,1)S(1)}, u32[]{:S(2)}, u32[]{:S(2)}) collective-permute-start(bf16[272,1536]{1,0:T(8,128)(2,1)} %get-tuple-element.42), channel_id=1, source_target_pairs={{0,6},{2,4},{4,2},{6,0},{1,7},{3,5},{5,3},{7,1},{8,14},{10,12},{12... | collective-permute-start | bytes 2506760 | tf_op jit(solution)/shard_map/ppermute | solution.py:29
  29.2 22.7 %collective-permute-start.14 = (bf16[272,1536]{1,0:T(8,128)(2,1)}, bf16[272,1536]{1,0:T(8,128)(2,1)S(1)}, u32[]{:S(2)}, u32[]{:S(2)}) collective-permute-start(bf16[272,1536]{1,0:T(8,128)(2,1)} %get-tuple-element.45), channel_id=1, source_target_pairs={{0,8},{8,0},{16,24},{24,16},{1,9},{9,1},{17,25},{25,17},{2,10},{10... | collective-permute-start | bytes 2506760 | tf_op jit(solution)/shard_map/ppermute | solution.py:29
  31.1 25.1 %collective-permute-start.19 = (bf16[272,1536]{1,0:T(8,128)(2,1)}, bf16[272,1536]{1,0:T(8,128)(2,1)S(1)}, u32[]{:S(2)}, u32[]{:S(2)}) collective-permute-start(bf16[272,1536]{1,0:T(8,128)(2,1)} %get-tuple-element.48), channel_id=1, source_target_pairs={{0,24},{8,16},{16,8},{24,0},{1,25},{9,17},{17,9},{25,1},{2,26},{10... | collective-permute-start | bytes 2506760 | tf_op jit(solution)/shard_map/ppermute | solution.py:29
  52.0 14.8 %collective-permute-start.15 = (bf16[144,1536]{1,0:T(8,128)(2,1)S(1)}, bf16[144,1536]{1,0:T(8,128)(2,1)S(1)}, u32[]{:S(2)}, u32[]{:S(2)}) collective-permute-start(bf16[144,1536]{1,0:T(8,128)(2,1)S(1)} %reduce-precision_convert_fusion.3), channel_id=1, source_target_pairs={{0,24},{8,16},{16,8},{24,0},{1,25},{9,17},{17,9},{25,1},{2,26},{10... | collective-permute-start | bytes 1327112 | tf_op jit(solution)/shard_map/ppermute | solution.py:29
  56.3 13.2 %collective-permute-start.20 = (bf16[144,1536]{1,0:T(8,128)(2,1)S(1)}, bf16[144,1536]{1,0:T(8,128)(2,1)S(1)}, u32[]{:S(2)}, u32[]{:S(2)}) collective-permute-start(bf16[144,1536]{1,0:T(8,128)(2,1)S(1)} %reduce-precision_convert_fusion.1), channel_id=1, source_target_pairs={{0,8},{8,0},{16,24},{24,16},{1,9},{9,1},{17,25},{25,17},{2,10},{10... | collective-permute-start | bytes 1327112 | tf_op jit(solution)/shard_map/ppermute | solution.py:29
  56.5 17.9 %collective-permute-start.2 = (bf16[896,128]{1,0:T(8,128)(2,1)S(1)}, bf16[896,128]{1,0:T(8,128)(2,1)S(1)}, u32[]{:S(2)}, u32[]{:S(2)}) collective-permute-start(bf16[896,128]{1,0:T(8,128)(2,1)S(1)} %reduce-precision_convert_fusion.11), channel_id=1, source_target_pairs={{0,8},{8,0},{16,24},{24,16},{1,9},{9,1},{17,25},{25,17},{2,10},{10... | collective-permute-start | bytes 688136 | tf_op jit(solution)/shard_map/ppermute | solution.py:29
  62.1 20.4 %collective-permute-start.6 = (bf16[144,1536]{1,0:T(8,128)(2,1)S(1)}, bf16[144,1536]{1,0:T(8,128)(2,1)S(1)}, u32[]{:S(2)}, u32[]{:S(2)}) collective-permute-start(bf16[144,1536]{1,0:T(8,128)(2,1)S(1)} %fusion.5), channel_id=1, source_target_pairs={{0,8},{8,0},{16,24},{24,16},{1,9},{9,1},{17,25},{25,17},{2,10},{10... | collective-permute-start | bytes 1327112 | tf_op jit(solution)/shard_map/ppermute | solution.py:29
  64.2 21.1 %collective-permute-start.11 = (bf16[144,1536]{1,0:T(8,128)(2,1)S(1)}, bf16[144,1536]{1,0:T(8,128)(2,1)S(1)}, u32[]{:S(2)}, u32[]{:S(2)}) collective-permute-start(bf16[144,1536]{1,0:T(8,128)(2,1)S(1)} %fusion.6), channel_id=1, source_target_pairs={{0,24},{8,16},{16,8},{24,0},{1,25},{9,17},{17,9},{25,1},{2,26},{10... | collective-permute-start | bytes 1327112 | tf_op jit(solution)/shard_map/ppermute | solution.py:29
  67.1 18.5 %collective-permute-start.16 = (bf16[144,1536]{1,0:T(8,128)(2,1)S(1)}, bf16[144,1536]{1,0:T(8,128)(2,1)S(1)}, u32[]{:S(2)}, u32[]{:S(2)}) collective-permute-start(bf16[144,1536]{1,0:T(8,128)(2,1)S(1)} %fusion.7), channel_id=1, source_target_pairs={{0,2},{2,0},{4,6},{6,4},{1,3},{3,1},{5,7},{7,5},{8,10},{10,8},{12,... | collective-permute-start | bytes 1327112 | tf_op jit(solution)/shard_map/ppermute | solution.py:29
  75.2 20.0 %collective-permute-start.21 = (bf16[144,1536]{1,0:T(8,128)(2,1)S(1)}, bf16[144,1536]{1,0:T(8,128)(2,1)S(1)}, u32[]{:S(2)}, u32[]{:S(2)}) collective-permute-start(bf16[144,1536]{1,0:T(8,128)(2,1)S(1)} %fusion.8), channel_id=1, source_target_pairs={{0,6},{2,4},{4,2},{6,0},{1,7},{3,5},{5,3},{7,1},{8,14},{10,12},{12... | collective-permute-start | bytes 1327112 | tf_op jit(solution)/shard_map/ppermute | solution.py:29
  82.6 21.4 %collective-permute-start.7 = (bf16[144,1536]{1,0:T(8,128)(2,1)S(1)}, bf16[144,1536]{1,0:T(8,128)(2,1)S(1)}, u32[]{:S(2)}, u32[]{:S(2)}) collective-permute-start(bf16[144,1536]{1,0:T(8,128)(2,1)S(1)} %reduce-precision_convert_fusion.6.rest_0_), channel_id=1, source_target_pairs={{0,24},{8,16},{16,8},{24,0},{1,25},{9,17},{17,9},{25,1},{2,26},{10... | collective-permute-start | bytes 1327112 | tf_op jit(solution)/shard_map/ppermute | solution.py:29
  85.5 19.9 %collective-permute-start.12 = (bf16[144,1536]{1,0:T(8,128)(2,1)S(1)}, bf16[144,1536]{1,0:T(8,128)(2,1)S(1)}, u32[]{:S(2)}, u32[]{:S(2)}) collective-permute-start(bf16[144,1536]{1,0:T(8,128)(2,1)S(1)} %reduce-precision_convert_fusion.4.rest_2_), channel_id=1, source_target_pairs={{0,8},{8,0},{16,24},{24,16},{1,9},{9,1},{17,25},{25,17},{2,10},{10... | collective-permute-start | bytes 1327112 | tf_op jit(solution)/shard_map/ppermute | solution.py:29
  85.7 21.0 %collective-permute-start.17 = (bf16[144,1536]{1,0:T(8,128)(2,1)S(1)}, bf16[144,1536]{1,0:T(8,128)(2,1)S(1)}, u32[]{:S(2)}, u32[]{:S(2)}) collective-permute-start(bf16[144,1536]{1,0:T(8,128)(2,1)S(1)} %reduce-precision_convert_fusion.2.rest_4_), channel_id=1, source_target_pairs={{0,6},{2,4},{4,2},{6,0},{1,7},{3,5},{5,3},{7,1},{8,14},{10,12},{12... | collective-permute-start | bytes 1327112 | tf_op jit(solution)/shard_map/ppermute | solution.py:29
  104.3 16.6 %collective-permute-start.8 = (bf16[128,1536]{1,0:T(8,128)(2,1)S(1)}, bf16[128,1536]{1,0:T(8,128)(2,1)S(1)}, u32[]{:S(2)}, u32[]{:S(2)}) collective-permute-start(bf16[128,1536]{1,0:T(8,128)(2,1)S(1)} %fusion.refs_0_), channel_id=1, source_target_pairs={{0,2},{2,0},{4,6},{6,4},{1,3},{3,1},{5,7},{7,5},{8,10},{10,8},{12,... | collective-permute-start | bytes 1179656 | tf_op jit(solution)/shard_map/ppermute | solution.py:29
  105.6 15.3 %collective-permute-start.13 = (bf16[128,1536]{1,0:T(8,128)(2,1)S(1)}, bf16[128,1536]{1,0:T(8,128)(2,1)S(1)}, u32[]{:S(2)}, u32[]{:S(2)}) collective-permute-start(bf16[128,1536]{1,0:T(8,128)(2,1)S(1)} %fusion.1.refs_2_), channel_id=1, source_target_pairs={{0,6},{2,4},{4,2},{6,0},{1,7},{3,5},{5,3},{7,1},{8,14},{10,12},{12... | collective-permute-start | bytes 1179656 | tf_op jit(solution)/shard_map/ppermute | solution.py:29
  107.0 13.9 %collective-permute-start.18 = (bf16[128,1536]{1,0:T(8,128)(2,1)S(1)}, bf16[128,1536]{1,0:T(8,128)(2,1)S(1)}, u32[]{:S(2)}, u32[]{:S(2)}) collective-permute-start(bf16[128,1536]{1,0:T(8,128)(2,1)S(1)} %fusion.2.refs_4_), channel_id=1, source_target_pairs={{0,8},{8,0},{16,24},{24,16},{1,9},{9,1},{17,25},{25,17},{2,10},{10... | collective-permute-start | bytes 1179656 | tf_op jit(solution)/shard_map/ppermute | solution.py:29
  107.4 13.5 %collective-permute-start.23 = (bf16[128,1536]{1,0:T(8,128)(2,1)S(1)}, bf16[128,1536]{1,0:T(8,128)(2,1)S(1)}, u32[]{:S(2)}, u32[]{:S(2)}) collective-permute-start(bf16[128,1536]{1,0:T(8,128)(2,1)S(1)} %fusion.3.refs_6_), channel_id=1, source_target_pairs={{0,24},{8,16},{16,8},{24,0},{1,25},{9,17},{17,9},{25,1},{2,26},{10... | collective-permute-start | bytes 1179656 | tf_op jit(solution)/shard_map/ppermute | solution.py:29
  124.2 34.4 %collective-permute-start.27 = (bf16[256,1536]{1,0:T(8,128)(2,1)}, bf16[256,1536]{1,0:T(8,128)(2,1)}, u32[]{:S(2)}, u32[]{:S(2)}) collective-permute-start(bf16[256,1536]{1,0:T(8,128)(2,1)} %pad_maximum_fusion.4), channel_id=1, source_target_pairs={{0,8},{8,0},{16,24},{24,16},{1,9},{9,1},{17,25},{25,17},{2,10},{10... | collective-permute-start | bytes 2359304 | tf_op jit(solution)/shard_map/ppermute | solution.py:29
  125.7 32.8 %collective-permute-start.26 = (bf16[256,1536]{1,0:T(8,128)(2,1)}, bf16[256,1536]{1,0:T(8,128)(2,1)}, u32[]{:S(2)}, u32[]{:S(2)}) collective-permute-start(bf16[256,1536]{1,0:T(8,128)(2,1)} %pad_maximum_fusion.3), channel_id=1, source_target_pairs={{0,24},{8,16},{16,8},{24,0},{1,25},{9,17},{17,9},{25,1},{2,26},{10... | collective-permute-start | bytes 2359304 | tf_op jit(solution)/shard_map/ppermute | solution.py:29
  127.9 30.6 %collective-permute-start.25 = (bf16[256,1536]{1,0:T(8,128)(2,1)}, bf16[256,1536]{1,0:T(8,128)(2,1)}, u32[]{:S(2)}, u32[]{:S(2)}) collective-permute-start(bf16[256,1536]{1,0:T(8,128)(2,1)} %pad_maximum_fusion.2), channel_id=1, source_target_pairs={{0,2},{2,0},{4,6},{6,4},{1,3},{3,1},{5,7},{7,5},{8,10},{10,8},{12,... | collective-permute-start | bytes 2359304 | tf_op jit(solution)/shard_map/ppermute | solution.py:29
  129.5 29.1 %collective-permute-start.24 = (bf16[256,1536]{1,0:T(8,128)(2,1)}, bf16[256,1536]{1,0:T(8,128)(2,1)}, u32[]{:S(2)}, u32[]{:S(2)}) collective-permute-start(bf16[256,1536]{1,0:T(8,128)(2,1)} %pad_maximum_fusion.1), channel_id=1, source_target_pairs={{0,6},{2,4},{4,2},{6,0},{1,7},{3,5},{5,3},{7,1},{8,14},{10,12},{12... | collective-permute-start | bytes 2359304 | tf_op jit(solution)/shard_map/ppermute | solution.py:29
  133.9 13.0 %collective-permute-start.31 = (bf16[128,1280]{1,0:T(8,128)(2,1)S(1)}, bf16[128,1280]{1,0:T(8,128)(2,1)S(1)}, u32[]{:S(2)}, u32[]{:S(2)}) collective-permute-start(bf16[128,1280]{1,0:T(8,128)(2,1)S(1)} %reduce-precision_convert_fusion.8), channel_id=1, source_target_pairs={{0,96},{32,64},{64,32},{96,0},{1,97},{33,65},{65,33},{97,1},{2,98}... | collective-permute-start | bytes 983048 | tf_op jit(solution)/shard_map/ppermute | solution.py:29
  (37 other events, 311.8 us)
Sparse Core Ops, SparseCore 0:
  110.3 44.4 all-gather.1

commit v5 on v4

--- a/solution.py
+++ b/solution.py
@@ -321,7 +321,7 @@
 
 def grad_up_kernel(at, grad, table, hot, down, out):
     scaled = (wide(grad[...]) * dot(hot[...], table[...])).astype(BF)
-    out[...] = dot(down[...], scaled, FIRST)
+    out[...] = dot(down[...], scaled, FIRST).astype(BF)
 
 
 def grad_up_part(at, grad, table, hot, down, share):
@@ -341,7 +341,7 @@
             in_specs=[mine(grad), mine(table), whole(hot), whole(down)],
             out_specs=pl.BlockSpec((flat, share), lambda j, at: (0, 0)),
         ),
-        out_shape=jax.ShapeDtypeStruct((flat, share), F32),
+        out_shape=jax.ShapeDtypeStruct((flat, share), BF),
         name="grad_up",
         **limits(0, 3 * grad.shape[0] * share),
     )(at, grad, table, hot, down)
@@ -516,9 +516,9 @@
     got = exchange(sums, 3)
 
     grad_up = grad_up_part(at, grad_out, table, hot3, down, cols // SIDE**2)
+    share = grad_up
     for flip in (1, 3):
-        grad_up = grad_up + swap(grad_up, ("dp", flip))
-    share = round_bf(grad_up)
+        share = round_bf(wide(share) + wide(swap(share, ("dp", flip))))
 
     done = []
     for s, (a, b) in enumerate(zip(sums, got, strict=True)):
@@ -548,7 +548,7 @@
     grad_down = total[tok_rows:]
     whole = jax.ShapeDtypeStruct((tok_rows, cols), BF)
     adapted = place(early, list(zip(done, near, strict=True)), block, whole)
-    after = (grad_up, input_grad)
+    after = (grad_up,)
     adapted = place_last(late, [[v] for v in far], block, whole, adapted, after)
     return (adapted, input_grad, grad_down.T, grad_up, mag / col_norm)
 

time: 171 us -> 169 us (0.988)
  other arithmetic: 14.6 us -> 10.6 us
  waiting for transfers between devices: 21.4 us -> 19.2 us
  starting transfers between devices: 50.1 us -> 52.3 us
  local copies, waits for them, and re-layouts: 4.79 us -> 6.97 us
    ppermute x32, waiting for transfers between devices: 21.4 us -> 19.2 us  [swap(): return lax.ppermute(values, axis, [(i, i ^ flip) for i in range(SIDE)])]
    ppermute x32, starting transfers between devices: 50 us -> 52.2 us  [swap(): return lax.ppermute(values, axis, [(i, i ^ flip) for i in range(SIDE)])]
    unnamed x55 -> x51, local copies, waits for them, and re-layouts: 3.83 us -> 5.1 us
    convert_element_type x18 -> x19, other arithmetic: 4.02 us -> 2.91 us  [round_bf(): lax.reduce_precision(values, exponent_bits=8, mantissa_bits=7).astype(BF)]
  transfers between devices with their start and end apart: 33 -> 33, of which waited for: 7 -> 6; matrix products, arithmetic and copies ran while one was open for 10% -> 8% of each run, Pallas kernels for 21% -> 22%
where the time goes in v5:
time: 169 us; the launch traced here: 168 us
  Pallas kernels  57.3 us (34%)
  starting transfers between devices  52.3 us (31%)
  waiting for transfers between devices  19.2 us (11%)
  between operations  14.8 us (9%)
  other arithmetic  10.6 us (6%)
  local copies, waits for them, and re-layouts  6.97 us (4%)
  blocking collectives  5.58 us (3%)
    ppermute x32, starting transfers between devices, swap(): return lax.ppermute(values, axis, [(i, i ^ flip) for i in range(SIDE)])  52.2 us
    ppermute x32, waiting for transfers between devices, swap(): return lax.ppermute(values, axis, [(i, i ^ flip) for i in range(SIDE)])  19.2 us
    pallas_call x1, Pallas kernels, forward(): pl.pallas_call(forward_kernel, grid_spec=pltpu.PrefetchScalarGridSpec(num...  17.2 us
    pallas_call x1, Pallas kernels, backward(): pl.pallas_call(backward_kernel, grid=(3,), in_specs=[moving(scaled), movi...  11.8 us
    pallas_call x1, Pallas kernels, back_part(): pl.pallas_call(back_kernel, grid=(cols // SPAN,), in_specs=[moving(grad),...  10.7 us
    pallas_call x1, Pallas kernels, column_squares(): pl.pallas_call(functools.partial(squares_kernel, adapters), grid=(cols //...  8.15 us
    all_to_all x1, blocking collectives, on_device(): both = wide(lax.all_to_all(sent, 'col', 0, 0, tiled=True))  5.58 us
    unnamed x51, local copies, waits for them, and re-layouts  5.1 us
  transfers between devices with their start and end apart: 33, of which 6 were waited for; matrix products, arithmetic and copies ran while one was open for 8% of the time, Pallas kernels for 22%

profile of v5, /device:TPU:0, one launch (start us, length us, event | category | flops | bytes accessed | tf_op | source)
XLA Modules:
  0.0 167.6 jit_solution(15286782339103881410)
XLA Ops:
  8.1 17.2 %forward.1 = (bf16[272,1536]{1,0:T(8,128)(2,1)}, bf16[144,1536]{1,0:T(8,128)(2,1)}, bf16[144,1536]{1,0:T(8,128)(2,1)}, bf16[272,1536]{1,0:T(8,128)(2,1)}, bf16[1...) custom-call(s32[19]{0:T(128)} %stack.126.at, ...), custom_call_target="tpu_custom_call" | custom-call | flops 7247757312 | bytes 23592960 | tf_op jit(solution)/shard_map/forward/pallas_call | solution.py:134
  27.1 2.2 %collective-permute-start.9 = (bf16[272,1536]{1,0:T(8,128)(2,1)}, bf16[272,1536]{1,0:T(8,128)(2,1)S(1)}, u32[]{:S(2)}, u32[]{:S(2)}) collective-permute-start(bf16[272,1536]{1,0:T(8,128)(2,1)} %get-tuple-element.42), channel_id=1, source_target_pairs={{0,6},{2,4},{4,2},{6,0},{1,7},{3,5},{5,3},{7,1},{8,14},{10,12},{12... | collective-permute-start | bytes 2506760 | tf_op jit(solution)/shard_map/ppermute | solution.py:29
  31.2 2.5 %collective-permute-start.19 = (bf16[272,1536]{1,0:T(8,128)(2,1)}, bf16[272,1536]{1,0:T(8,128)(2,1)S(1)}, u32[]{:S(2)}, u32[]{:S(2)}) collective-permute-start(bf16[272,1536]{1,0:T(8,128)(2,1)} %get-tuple-element.48), channel_id=1, source_target_pairs={{0,24},{8,16},{16,8},{24,0},{1,25},{9,17},{17,9},{25,1},{2,26},{10... | collective-permute-start | bytes 2506760 | tf_op jit(solution)/shard_map/ppermute | solution.py:29
  33.7 8.1 %squares.1 = bf16[896,128]{1,0:T(8,128)(2,1)} custom-call(bf16[512,896]{1,0:T(8,128)(2,1)} %tokens.5, bf16[896,128]{1,0:T(8,128)(2,1)} %maps.5, bf16[512,128]{1,0:T(8,128)(2,1)} %get-tuple-element.35.slots, bf16[896,6144]{1,0:T(8,128)(2,1)} %frozen.5, bf16[128,6144]{1,0:T(8,128)(2,1)} %up.5), custom_call_target="tpu_custom_call" | custom-call | flops 1409286144 | bytes 11010048 | tf_op jit(solution)/shard_map/squares/pallas_call | solution.py:202
  41.8 4.0 %collective-permute-done = bf16[272,1536]{1,0:T(8,128)(2,1)S(1)} collective-permute-done((bf16[272,1536]{1,0:T(8,128)(2,1)}, bf16[272,1536]{1,0:T(8,128)(2,1)S(1)}, u32[]{:S(2)}, u32[]{:S(2)}) %collective-permute-start) | collective-permute-done | bytes 835616 | tf_op jit(solution)/shard_map/ppermute | solution.py:29
  47.7 2.3 %collective-permute-start.5 = (bf16[144,1536]{1,0:T(8,128)(2,1)S(1)}, bf16[144,1536]{1,0:T(8,128)(2,1)S(1)}, u32[]{:S(2)}, u32[]{:S(2)}) collective-permute-start(bf16[144,1536]{1,0:T(8,128)(2,1)S(1)} %reduce-precision_convert_fusion.7), channel_id=1, source_target_pairs={{0,6},{2,4},{4,2},{6,0},{1,7},{3,5},{5,3},{7,1},{8,14},{10,12},{12... | collective-permute-start | bytes 1327112 | tf_op jit(solution)/shard_map/ppermute | solution.py:29
  51.0 4.1 %collective-permute-start.15 = (bf16[144,1536]{1,0:T(8,128)(2,1)S(1)}, bf16[144,1536]{1,0:T(8,128)(2,1)S(1)}, u32[]{:S(2)}, u32[]{:S(2)}) collective-permute-start(bf16[144,1536]{1,0:T(8,128)(2,1)S(1)} %reduce-precision_convert_fusion.3), channel_id=1, source_target_pairs={{0,24},{8,16},{16,8},{24,0},{1,25},{9,17},{17,9},{25,1},{2,26},{10... | collective-permute-start | bytes 1327112 | tf_op jit(solution)/shard_map/ppermute | solution.py:29
  55.4 2.1 %collective-permute-start.2 = (bf16[896,128]{1,0:T(8,128)(2,1)S(1)}, bf16[896,128]{1,0:T(8,128)(2,1)S(1)}, u32[]{:S(2)}, u32[]{:S(2)}) collective-permute-start(bf16[896,128]{1,0:T(8,128)(2,1)S(1)} %reduce-precision_convert_fusion.11), channel_id=1, source_target_pairs={{0,8},{8,0},{16,24},{24,16},{1,9},{9,1},{17,25},{25,17},{2,10},{10... | collective-permute-start | bytes 688136 | tf_op jit(solution)/shard_map/ppermute | solution.py:29
  57.5 2.3 %collective-permute-done.5 = bf16[144,1536]{1,0:T(8,128)(2,1)S(1)} collective-permute-done((bf16[144,1536]{1,0:T(8,128)(2,1)S(1)}, bf16[144,1536]{1,0:T(8,128)(2,1)S(1)}, u32[]{:S(2)}, u32[]{:S(2)}) %collective-permute-start.5) | collective-permute-done | bytes 442400 | tf_op jit(solution)/shard_map/ppermute | solution.py:29
  62.2 4.3 %collective-permute-start.11 = (bf16[144,1536]{1,0:T(8,128)(2,1)S(1)}, bf16[144,1536]{1,0:T(8,128)(2,1)S(1)}, u32[]{:S(2)}, u32[]{:S(2)}) collective-permute-start(bf16[144,1536]{1,0:T(8,128)(2,1)S(1)} %fusion.6), channel_id=1, source_target_pairs={{0,24},{8,16},{16,8},{24,0},{1,25},{9,17},{17,9},{25,1},{2,26},{10... | collective-permute-start | bytes 1327112 | tf_op jit(solution)/shard_map/ppermute | solution.py:29
  68.6 4.8 %collective-permute-done.2 = bf16[896,128]{1,0:T(8,128)(2,1)S(1)} collective-permute-done((bf16[896,128]{1,0:T(8,128)(2,1)S(1)}, bf16[896,128]{1,0:T(8,128)(2,1)S(1)}, u32[]{:S(2)}, u32[]{:S(2)}) %collective-permute-start.2) | collective-permute-done | bytes 229408 | tf_op jit(solution)/shard_map/ppermute | solution.py:29
  74.1 2.7 %collective-permute-start.21 = (bf16[144,1536]{1,0:T(8,128)(2,1)S(1)}, bf16[144,1536]{1,0:T(8,128)(2,1)S(1)}, u32[]{:S(2)}, u32[]{:S(2)}) collective-permute-start(bf16[144,1536]{1,0:T(8,128)(2,1)S(1)} %fusion.8), channel_id=1, source_target_pairs={{0,6},{2,4},{4,2},{6,0},{1,7},{3,5},{5,3},{7,1},{8,14},{10,12},{12... | collective-permute-start | bytes 1327112 | tf_op jit(solution)/shard_map/ppermute | solution.py:29
  76.8 3.9 %collective-permute-done.3 = bf16[896,128]{1,0:T(8,128)(2,1)S(1)} collective-permute-done((bf16[896,128]{1,0:T(8,128)(2,1)S(1)}, bf16[896,128]{1,0:T(8,128)(2,1)S(1)}, u32[]{:S(2)}, u32[]{:S(2)}) %collective-permute-start.3) | collective-permute-done | bytes 229408 | tf_op jit(solution)/shard_map/ppermute | solution.py:29
  81.5 2.8 %collective-permute-start.7 = (bf16[144,1536]{1,0:T(8,128)(2,1)S(1)}, bf16[144,1536]{1,0:T(8,128)(2,1)S(1)}, u32[]{:S(2)}, u32[]{:S(2)}) collective-permute-start(bf16[144,1536]{1,0:T(8,128)(2,1)S(1)} %reduce-precision_convert_fusion.6.rest_0_), channel_id=1, source_target_pairs={{0,24},{8,16},{16,8},{24,0},{1,25},{9,17},{17,9},{25,1},{2,26},{10... | collective-permute-start | bytes 1327112 | tf_op jit(solution)/shard_map/ppermute | solution.py:29
  86.0 2.0 %collective-permute-done.4.got = bf16[896,128]{1,0:T(8,128)(2,1)S(1)} collective-permute-done((bf16[896,128]{1,0:T(8,128)(2,1)S(1)}, bf16[896,128]{1,0:T(8,128)(2,1)S(1)}, u32[]{:S(2)}, u32[]{:S(2)}) %collective-permute-start.4) | collective-permute-done | bytes 229408 | tf_op jit(solution)/shard_map/ppermute | solution.py:29
  89.8 3.0 %grad_up.1 = bf16[128,384]{1,0:T(8,128)(2,1)} custom-call(s32[19]{0:T(128)} %stack.126.at, bf16[512,6144]{1,0:T(8,128)(2,1)} %grad.5, bf16[48,6144]{1,0:T(8,128)(2,1)} %copy-done.1, bf16[512,48]{1,0:T(8,128)(2,1)} %get-tuple-element.34.hot, bf16[512,128]{1,0:T(8,128)(2,1)} %copy-done.4), custom_call_target="tpu_custom_call" | custom-call | bytes 589824 | tf_op jit(solution)/shard_map/grad_up/pallas_call | solution.py:336
  95.5 2.1 %collective-permute-done.28 = bf16[128,384]{1,0:T(8,128)(2,1)S(1)} collective-permute-done((bf16[128,384]{1,0:T(8,128)(2,1)}, bf16[128,384]{1,0:T(8,128)(2,1)S(1)}, u32[]{:S(2)}, u32[]{:S(2)}) %collective-permute-start.28) | collective-permute-done | bytes 98336 | tf_op jit(solution)/shard_map/ppermute | solution.py:29
  98.5 2.8 %collective-permute-start.29 = (bf16[128,384]{1,0:T(8,128)(2,1)S(1)}, bf16[128,384]{1,0:T(8,128)(2,1)S(1)}, u32[]{:S(2)}, u32[]{:S(2)}) collective-permute-start(bf16[128,384]{1,0:T(8,128)(2,1)S(1)} %reduce-precision_convert_fusion.13), channel_id=1, source_target_pairs={{0,96},{32,64},{64,32},{96,0},{1,97},{33,65},{65,33},{97,1},{2,98}... | collective-permute-start | bytes 294920 | tf_op jit(solution)/shard_map/ppermute | solution.py:29
  108.3 10.7 %back.1 = (bf16[128,1280]{1,0:T(8,128)(2,1)}, f32[512,896]{1,0:T(8,128)}, bf16[512,6144]{1,0:T(8,128)(2,1)}) custom-call(bf16[512,6144]{1,0:T(8,128)(2,1)} %grad.5, bf16[48,6144]{1,0:T(8,128)(2,1)} %copy-done.1, bf16[512,48]{1,0:T(8,128)(2,1)} %get-tuple-element.34.hot, bf16[128,6144]{1,0:T(8,128)(2,1)} %up.5, bf16[512,128]{1,0:T(8,128)(2,1)} %get-tuple-element.35.slots, ...), custom_call_target="tpu_custom_call" | custom-call | flops 1610612736 | bytes 6291456 | tf_op jit(solution)/shard_map/back/pallas_call | solution.py:393
  123.8 2.1 %collective-permute-start.26 = (bf16[256,1536]{1,0:T(8,128)(2,1)}, bf16[256,1536]{1,0:T(8,128)(2,1)}, u32[]{:S(2)}, u32[]{:S(2)}) collective-permute-start(bf16[256,1536]{1,0:T(8,128)(2,1)} %pad_maximum_fusion.3), channel_id=1, source_target_pairs={{0,24},{8,16},{16,8},{24,0},{1,25},{9,17},{17,9},{25,1},{2,26},{10... | collective-permute-start | bytes 2359304 | tf_op jit(solution)/shard_map/ppermute | solution.py:29
  129.5 2.3 %place.1.refs_5_ = bf16[512,6144]{1,0:T(8,128)(2,1)} custom-call(s32[8]{0:T(128)S(1)} %stack.129.at, bf16[128,1536]{1,0:T(8,128)(2,1)S(1)} %fusion.refs_0_, bf16[128,1536]{1,0:T(8,128)(2,1)S(1)} %collective-permute-done.8.refs_1_, bf16[128,1536]{1,0:T(8,128)(2,1)S(1)} %fusion.1.refs_2_, bf16[128,1536]{1,0:T(8,128)(2,1)S(1)} %collective-permute-done.13.refs_3_, ...), custom_call_target="tpu_custom_call" | custom-call | tf_op jit(solution)/shard_map/place/pallas_call | solution.py:240
  133.1 11.8 %backward.1 = bf16[512,896]{1,0:T(8,128)(2,1)} custom-call(bf16[512,6144]{1,0:T(8,128)(2,1)} %get-tuple-element.57.scaled, bf16[896,6144]{1,0:T(8,128)(2,1)} %frozen.5, f32[512,896]{1,0:T(8,128)} %get-tuple-element.60.start), custom_call_target="tpu_custom_call" | custom-call | flops 5637144576 | bytes 17301504 | tf_op jit(solution)/shard_map/backward/pallas_call | solution.py:436
  146.2 5.6 %all_to_all.9 = bf16[2,640,896]{2,1,0:T(8,128)(2,1)S(1)} all-to-all(bf16[2,640,896]{2,1,0:T(8,128)(2,1)S(1)} %bitcast.40), channel_id=1, replica_groups=mesh['dp'=4,'z'=4,'y'=4,'col'=2] {'col'}, dimensions={0} | all-to-all | bytes 4587520 | tf_op jit(solution)/shard_map/all_to_all | solution.py:545
  156.8 3.9 %place_last.1 = bf16[512,6144]{1,0:T(8,128)(2,1)} custom-call(s32[8]{0:T(128)S(1)} %stack.107.at, bf16[256,1536]{1,0:T(8,128)(2,1)} %collective-permute-done.24.refs_0_, bf16[256,1536]{1,0:T(8,128)(2,1)} %collective-permute-done.25.refs_1_, bf16[256,1536]{1,0:T(8,128)(2,1)} %collective-permute-done.26.refs_2_, ...), custom_call_target="tpu_custom_call", output_to_operand_aliasing={{}: (6, {})} | custom-call | tf_op jit(solution)/shard_map/place_last/pallas_call | solution.py:289
  (150 shorter events, 43.2 us)
Async XLA Ops:
  7.2 147.9 %all-gather.2.cloned.1.call-start = ((), (), s32[]{:S(2)}) async-start(), calls=%async_computation.1 | async-start | bytes 1671168 | tf_op jit(solution)/shard_map/all_gather | solution.py:539
  25.3 20.5 %collective-permute-start = (bf16[272,1536]{1,0:T(8,128)(2,1)}, bf16[272,1536]{1,0:T(8,128)(2,1)S(1)}, u32[]{:S(2)}, u32[]{:S(2)}) collective-permute-start(bf16[272,1536]{1,0:T(8,128)(2,1)} %get-tuple-element.36), channel_id=1, source_target_pairs={{0,2},{2,0},{4,6},{6,4},{1,3},{3,1},{5,7},{7,5},{8,10},{10,8},{12,... | collective-permute-start | bytes 2506760 | tf_op jit(solution)/shard_map/ppermute | solution.py:29
  27.1 23.0 %collective-permute-start.9 = (bf16[272,1536]{1,0:T(8,128)(2,1)}, bf16[272,1536]{1,0:T(8,128)(2,1)S(1)}, u32[]{:S(2)}, u32[]{:S(2)}) collective-permute-start(bf16[272,1536]{1,0:T(8,128)(2,1)} %get-tuple-element.42), channel_id=1, source_target_pairs={{0,6},{2,4},{4,2},{6,0},{1,7},{3,5},{5,3},{7,1},{8,14},{10,12},{12... | collective-permute-start | bytes 2506760 | tf_op jit(solution)/shard_map/ppermute | solution.py:29
  29.2 21.6 %collective-permute-start.14 = (bf16[272,1536]{1,0:T(8,128)(2,1)}, bf16[272,1536]{1,0:T(8,128)(2,1)S(1)}, u32[]{:S(2)}, u32[]{:S(2)}) collective-permute-start(bf16[272,1536]{1,0:T(8,128)(2,1)} %get-tuple-element.45), channel_id=1, source_target_pairs={{0,8},{8,0},{16,24},{24,16},{1,9},{9,1},{17,25},{25,17},{2,10},{10... | collective-permute-start | bytes 2506760 | tf_op jit(solution)/shard_map/ppermute | solution.py:29
  31.2 23.9 %collective-permute-start.19 = (bf16[272,1536]{1,0:T(8,128)(2,1)}, bf16[272,1536]{1,0:T(8,128)(2,1)S(1)}, u32[]{:S(2)}, u32[]{:S(2)}) collective-permute-start(bf16[272,1536]{1,0:T(8,128)(2,1)} %get-tuple-element.48), channel_id=1, source_target_pairs={{0,24},{8,16},{16,8},{24,0},{1,25},{9,17},{17,9},{25,1},{2,26},{10... | collective-permute-start | bytes 2506760 | tf_op jit(solution)/shard_map/ppermute | solution.py:29
  51.0 15.6 %collective-permute-start.15 = (bf16[144,1536]{1,0:T(8,128)(2,1)S(1)}, bf16[144,1536]{1,0:T(8,128)(2,1)S(1)}, u32[]{:S(2)}, u32[]{:S(2)}) collective-permute-start(bf16[144,1536]{1,0:T(8,128)(2,1)S(1)} %reduce-precision_convert_fusion.3), channel_id=1, source_target_pairs={{0,24},{8,16},{16,8},{24,0},{1,25},{9,17},{17,9},{25,1},{2,26},{10... | collective-permute-start | bytes 1327112 | tf_op jit(solution)/shard_map/ppermute | solution.py:29
  55.2 13.2 %collective-permute-start.20 = (bf16[144,1536]{1,0:T(8,128)(2,1)S(1)}, bf16[144,1536]{1,0:T(8,128)(2,1)S(1)}, u32[]{:S(2)}, u32[]{:S(2)}) collective-permute-start(bf16[144,1536]{1,0:T(8,128)(2,1)S(1)} %reduce-precision_convert_fusion.1), channel_id=1, source_target_pairs={{0,8},{8,0},{16,24},{24,16},{1,9},{9,1},{17,25},{25,17},{2,10},{10... | collective-permute-start | bytes 1327112 | tf_op jit(solution)/shard_map/ppermute | solution.py:29
  55.4 17.9 %collective-permute-start.2 = (bf16[896,128]{1,0:T(8,128)(2,1)S(1)}, bf16[896,128]{1,0:T(8,128)(2,1)S(1)}, u32[]{:S(2)}, u32[]{:S(2)}) collective-permute-start(bf16[896,128]{1,0:T(8,128)(2,1)S(1)} %reduce-precision_convert_fusion.11), channel_id=1, source_target_pairs={{0,8},{8,0},{16,24},{24,16},{1,9},{9,1},{17,25},{25,17},{2,10},{10... | collective-permute-start | bytes 688136 | tf_op jit(solution)/shard_map/ppermute | solution.py:29
  60.0 21.4 %collective-permute-start.6 = (bf16[144,1536]{1,0:T(8,128)(2,1)S(1)}, bf16[144,1536]{1,0:T(8,128)(2,1)S(1)}, u32[]{:S(2)}, u32[]{:S(2)}) collective-permute-start(bf16[144,1536]{1,0:T(8,128)(2,1)S(1)} %fusion.5), channel_id=1, source_target_pairs={{0,8},{8,0},{16,24},{24,16},{1,9},{9,1},{17,25},{25,17},{2,10},{10... | collective-permute-start | bytes 1327112 | tf_op jit(solution)/shard_map/ppermute | solution.py:29
  62.2 22.0 %collective-permute-start.11 = (bf16[144,1536]{1,0:T(8,128)(2,1)S(1)}, bf16[144,1536]{1,0:T(8,128)(2,1)S(1)}, u32[]{:S(2)}, u32[]{:S(2)}) collective-permute-start(bf16[144,1536]{1,0:T(8,128)(2,1)S(1)} %fusion.6), channel_id=1, source_target_pairs={{0,24},{8,16},{16,8},{24,0},{1,25},{9,17},{17,9},{25,1},{2,26},{10... | collective-permute-start | bytes 1327112 | tf_op jit(solution)/shard_map/ppermute | solution.py:29
  66.8 17.7 %collective-permute-start.16 = (bf16[144,1536]{1,0:T(8,128)(2,1)S(1)}, bf16[144,1536]{1,0:T(8,128)(2,1)S(1)}, u32[]{:S(2)}, u32[]{:S(2)}) collective-permute-start(bf16[144,1536]{1,0:T(8,128)(2,1)S(1)} %fusion.7), channel_id=1, source_target_pairs={{0,2},{2,0},{4,6},{6,4},{1,3},{3,1},{5,7},{7,5},{8,10},{10,8},{12,... | collective-permute-start | bytes 1327112 | tf_op jit(solution)/shard_map/ppermute | solution.py:29
  74.1 20.1 %collective-permute-start.21 = (bf16[144,1536]{1,0:T(8,128)(2,1)S(1)}, bf16[144,1536]{1,0:T(8,128)(2,1)S(1)}, u32[]{:S(2)}, u32[]{:S(2)}) collective-permute-start(bf16[144,1536]{1,0:T(8,128)(2,1)S(1)} %fusion.8), channel_id=1, source_target_pairs={{0,6},{2,4},{4,2},{6,0},{1,7},{3,5},{5,3},{7,1},{8,14},{10,12},{12... | collective-permute-start | bytes 1327112 | tf_op jit(solution)/shard_map/ppermute | solution.py:29
  81.5 19.9 %collective-permute-start.7 = (bf16[144,1536]{1,0:T(8,128)(2,1)S(1)}, bf16[144,1536]{1,0:T(8,128)(2,1)S(1)}, u32[]{:S(2)}, u32[]{:S(2)}) collective-permute-start(bf16[144,1536]{1,0:T(8,128)(2,1)S(1)} %reduce-precision_convert_fusion.6.rest_0_), channel_id=1, source_target_pairs={{0,24},{8,16},{16,8},{24,0},{1,25},{9,17},{17,9},{25,1},{2,26},{10... | collective-permute-start | bytes 1327112 | tf_op jit(solution)/shard_map/ppermute | solution.py:29
  84.4 19.0 %collective-permute-start.12 = (bf16[144,1536]{1,0:T(8,128)(2,1)S(1)}, bf16[144,1536]{1,0:T(8,128)(2,1)S(1)}, u32[]{:S(2)}, u32[]{:S(2)}) collective-permute-start(bf16[144,1536]{1,0:T(8,128)(2,1)S(1)} %reduce-precision_convert_fusion.4.rest_2_), channel_id=1, source_target_pairs={{0,8},{8,0},{16,24},{24,16},{1,9},{9,1},{17,25},{25,17},{2,10},{10... | collective-permute-start | bytes 1327112 | tf_op jit(solution)/shard_map/ppermute | solution.py:29
  84.6 20.2 %collective-permute-start.17 = (bf16[144,1536]{1,0:T(8,128)(2,1)S(1)}, bf16[144,1536]{1,0:T(8,128)(2,1)S(1)}, u32[]{:S(2)}, u32[]{:S(2)}) collective-permute-start(bf16[144,1536]{1,0:T(8,128)(2,1)S(1)} %reduce-precision_convert_fusion.2.rest_4_), channel_id=1, source_target_pairs={{0,6},{2,4},{4,2},{6,0},{1,7},{3,5},{5,3},{7,1},{8,14},{10,12},{12... | collective-permute-start | bytes 1327112 | tf_op jit(solution)/shard_map/ppermute | solution.py:29
  102.4 16.7 %collective-permute-start.8 = (bf16[128,1536]{1,0:T(8,128)(2,1)S(1)}, bf16[128,1536]{1,0:T(8,128)(2,1)S(1)}, u32[]{:S(2)}, u32[]{:S(2)}) collective-permute-start(bf16[128,1536]{1,0:T(8,128)(2,1)S(1)} %fusion.refs_0_), channel_id=1, source_target_pairs={{0,2},{2,0},{4,6},{6,4},{1,3},{3,1},{5,7},{7,5},{8,10},{10,8},{12,... | collective-permute-start | bytes 1179656 | tf_op jit(solution)/shard_map/ppermute | solution.py:29
  103.7 15.4 %collective-permute-start.13 = (bf16[128,1536]{1,0:T(8,128)(2,1)S(1)}, bf16[128,1536]{1,0:T(8,128)(2,1)S(1)}, u32[]{:S(2)}, u32[]{:S(2)}) collective-permute-start(bf16[128,1536]{1,0:T(8,128)(2,1)S(1)} %fusion.1.refs_2_), channel_id=1, source_target_pairs={{0,6},{2,4},{4,2},{6,0},{1,7},{3,5},{5,3},{7,1},{8,14},{10,12},{12... | collective-permute-start | bytes 1179656 | tf_op jit(solution)/shard_map/ppermute | solution.py:29
  105.8 13.2 %collective-permute-start.18 = (bf16[128,1536]{1,0:T(8,128)(2,1)S(1)}, bf16[128,1536]{1,0:T(8,128)(2,1)S(1)}, u32[]{:S(2)}, u32[]{:S(2)}) collective-permute-start(bf16[128,1536]{1,0:T(8,128)(2,1)S(1)} %fusion.2.refs_4_), channel_id=1, source_target_pairs={{0,8},{8,0},{16,24},{24,16},{1,9},{9,1},{17,25},{25,17},{2,10},{10... | collective-permute-start | bytes 1179656 | tf_op jit(solution)/shard_map/ppermute | solution.py:29
  106.3 12.8 %collective-permute-start.23 = (bf16[128,1536]{1,0:T(8,128)(2,1)S(1)}, bf16[128,1536]{1,0:T(8,128)(2,1)S(1)}, u32[]{:S(2)}, u32[]{:S(2)}) collective-permute-start(bf16[128,1536]{1,0:T(8,128)(2,1)S(1)} %fusion.3.refs_6_), channel_id=1, source_target_pairs={{0,24},{8,16},{16,8},{24,0},{1,25},{9,17},{17,9},{25,1},{2,26},{10... | collective-permute-start | bytes 1179656 | tf_op jit(solution)/shard_map/ppermute | solution.py:29
  122.4 34.4 %collective-permute-start.27 = (bf16[256,1536]{1,0:T(8,128)(2,1)}, bf16[256,1536]{1,0:T(8,128)(2,1)}, u32[]{:S(2)}, u32[]{:S(2)}) collective-permute-start(bf16[256,1536]{1,0:T(8,128)(2,1)} %pad_maximum_fusion.4), channel_id=1, source_target_pairs={{0,8},{8,0},{16,24},{24,16},{1,9},{9,1},{17,25},{25,17},{2,10},{10... | collective-permute-start | bytes 2359304 | tf_op jit(solution)/shard_map/ppermute | solution.py:29
  123.8 33.0 %collective-permute-start.26 = (bf16[256,1536]{1,0:T(8,128)(2,1)}, bf16[256,1536]{1,0:T(8,128)(2,1)}, u32[]{:S(2)}, u32[]{:S(2)}) collective-permute-start(bf16[256,1536]{1,0:T(8,128)(2,1)} %pad_maximum_fusion.3), channel_id=1, source_target_pairs={{0,24},{8,16},{16,8},{24,0},{1,25},{9,17},{17,9},{25,1},{2,26},{10... | collective-permute-start | bytes 2359304 | tf_op jit(solution)/shard_map/ppermute | solution.py:29
  125.9 31.0 %collective-permute-start.25 = (bf16[256,1536]{1,0:T(8,128)(2,1)}, bf16[256,1536]{1,0:T(8,128)(2,1)}, u32[]{:S(2)}, u32[]{:S(2)}) collective-permute-start(bf16[256,1536]{1,0:T(8,128)(2,1)} %pad_maximum_fusion.2), channel_id=1, source_target_pairs={{0,2},{2,0},{4,6},{6,4},{1,3},{3,1},{5,7},{7,5},{8,10},{10,8},{12,... | collective-permute-start | bytes 2359304 | tf_op jit(solution)/shard_map/ppermute | solution.py:29
  127.4 29.4 %collective-permute-start.24 = (bf16[256,1536]{1,0:T(8,128)(2,1)}, bf16[256,1536]{1,0:T(8,128)(2,1)}, u32[]{:S(2)}, u32[]{:S(2)}) collective-permute-start(bf16[256,1536]{1,0:T(8,128)(2,1)} %pad_maximum_fusion.1), channel_id=1, source_target_pairs={{0,6},{2,4},{4,2},{6,0},{1,7},{3,5},{5,3},{7,1},{8,14},{10,12},{12... | collective-permute-start | bytes 2359304 | tf_op jit(solution)/shard_map/ppermute | solution.py:29
  131.8 13.0 %collective-permute-start.31 = (bf16[128,1280]{1,0:T(8,128)(2,1)S(1)}, bf16[128,1280]{1,0:T(8,128)(2,1)S(1)}, u32[]{:S(2)}, u32[]{:S(2)}) collective-permute-start(bf16[128,1280]{1,0:T(8,128)(2,1)S(1)} %reduce-precision_convert_fusion.8), channel_id=1, source_target_pairs={{0,96},{32,64},{64,32},{96,0},{1,97},{33,65},{65,33},{97,1},{2,98}... | collective-permute-start | bytes 983048 | tf_op jit(solution)/shard_map/ppermute | solution.py:29
  (34 other events, 296.8 us)
Sparse Core Ops, SparseCore 0:
  108.5 44.1 all-gather.1
